TPU v7x, 128 devices: a whole 4x4x4 slice. The times are simulated.
128 devices in a mesh: ccd: 64 (over x, z, y), strip: 2 (over core).
Axes of the slice: x: 4, y: 4, z: 4, core: 2. Of those that a mesh axis runs over, the one named last changes fastest.
Arguments:
- template: bfloat16 [16384, 8, 512], P(('ccd', 'strip')), may hold values from -8 to 8
- route_dest: int32 [16384], P(('ccd', 'strip')), may hold values from 0 to 127, as said below
- route_row: int32 [16384], P(('ccd', 'strip')), may hold values from 0 to 1016
- kern_row: bfloat16 [12, 21], replicated, may hold values from -1 to 1
- kern_col: bfloat16 [12, 21], replicated, may hold values from -1 to 1
- science: float32 [131072, 512], P(('ccd', 'strip'))
- noise_sigma: float32 [128], P(('ccd', 'strip')), may hold values from 1 to 4
- stamp_row: int32 [2048], P(('ccd', 'strip')), may hold values from 0 to 992
- stamp_col: int32 [2048], P(('ccd', 'strip')), may hold values from 0 to 480
- band_shift: int32 [128], replicated, may hold values from 0 to 63, as said below
- psf_row: bfloat16 [15], replicated, may hold values from -1.5 to 1.5
- psf_col: bfloat16 [15], replicated, may hold values from -1.5 to 1.5
Outputs:
- difference: bfloat16 [131072, 512], P(('ccd', 'strip'))
- stamp_cut: bfloat16 [2048, 1024], P(('ccd', 'strip'))
- coefficients: float32 [12], replicated
- filtered: float32 [131072, 512], P(('ccd', 'strip'))
Inputs may be any that keep to these rules, and one draw needn't show every extreme that they name: `route_dest`: among the 128 pieces of one device no destination appears more than 2 times, and on every device some destination appears exactly 2 times. `band_shift`: no value appears more than 4 times, and some value appears exactly 4 times.
All inputs are finite; a program needn't handle non-finite values.
Results may differ from a plain program's by a relative error of at most 0.0065.
Values may be sent and summed in bfloat16 or wider, within the bound.
No kernel may reach another device: no remote copies, remote signals or barrier semaphores. Data moves between devices by JAX's collectives and lax.ppermute only.
A program may use at most 128 MiB of HBM per device.

v0:
```python
import jax
import jax.numpy as jnp
from jax import lax
from jax.sharding import PartitionSpec as P

CAP = 2
BASIS = 12
HALF = 10
PSF_HALF = 7
STAMP = 32


def with_halo(array, sides, width):
    for axis, dim in sides:
        devices, length = (lax.axis_size(axis), array.shape[dim])
        up = [(i, (i + 1) % devices) for i in range(devices - 1)]
        down = [(j, i) for i, j in up]
        last = lax.slice_in_dim(array, length - width, length, axis=dim)
        first = lax.slice_in_dim(array, 0, width, axis=dim)
        before = lax.ppermute(last, axis, up)
        after = lax.ppermute(first, axis, down)
        array = jnp.concatenate([before, array, after], axis=dim)
    return array


def lag_table(kernel, block_size):
    tap_count = kernel.shape[1]
    offset = jnp.arange(block_size + tap_count - 1)[:, None] - jnp.arange(block_size)[None, :]
    onehot = (offset[:, :, None] == jnp.arange(tap_count)[None, None, :]).astype(jnp.bfloat16)
    return jnp.einsum("bt,ijt->bij", kernel, onehot, preferred_element_type=jnp.float32).astype(
        jnp.bfloat16
    )


def column_windows(padded, half_width, block_size):
    height, columns = padded.shape
    block_count = columns // block_size
    wide = jnp.pad(padded, ((0, 0), (half_width, half_width + block_size - 2 * half_width)))
    middle = wide[:, :columns].reshape(height, block_count, block_size)
    border = wide[:, block_size : block_size + columns].reshape(height, block_count, block_size)[
        :, :, : 2 * half_width
    ]
    return jnp.concatenate([middle, border], axis=2)


def row_windows(padded, half_width, block_size):
    height = padded.shape[0] - 2 * half_width
    return jnp.stack(
        [
            padded[first_row : first_row + block_size + 2 * half_width]
            for first_row in range(0, height, block_size)
        ],
        axis=0,
    )


def separable(framed, kernel_rows, kernel_cols, rounding):
    half_width = (kernel_rows.shape[1] - 1) // 2
    height = framed.shape[0] - 2 * half_width
    columns = framed.shape[1]
    windows = column_windows(framed, half_width, min(256, columns))
    col_tables = lag_table(kernel_cols, min(256, columns))
    row_tables = lag_table(kernel_rows, min(256, height))

    def one_kernel(tables):
        col_table, row_table = tables
        across = jnp.einsum("rkc,co->rko", windows, col_table, preferred_element_type=jnp.float32)
        across = across.reshape(height + 2 * half_width, columns).astype(jnp.bfloat16)
        stacked = row_windows(across, half_width, min(256, height))
        result = jnp.einsum("ij,kiw->kjw", row_table, stacked, preferred_element_type=jnp.float32)
        return result.reshape(height, columns).astype(rounding)

    return lax.map(one_kernel, (col_tables, row_tables))


def stamp_blocks(picture, corner_rows, corner_cols):

    def single(corner_row, corner_col):
        return lax.dynamic_slice(
            picture,
            (jnp.zeros((), jnp.int32), corner_row, corner_col),
            (picture.shape[0], STAMP, STAMP),
        )

    return jax.vmap(single)(corner_rows, corner_cols)


def shards(
    template,
    route_dest,
    route_row,
    kern_row,
    kern_col,
    science,
    noise_sigma,
    stamp_row,
    stamp_col,
    band_shift,
    psf_row,
    psf_col,
):
    ccd_count = lax.axis_size("ccd")
    strip_count = lax.axis_size("strip")
    devices = ccd_count * strip_count
    pieces, band_rows, columns = template.shape
    height = science.shape[0]
    slot_count = devices * CAP
    piece_order = jnp.arange(pieces)
    same_dest = (route_dest[:, None] == route_dest[None, :]) & (
        piece_order[None, :] < piece_order[:, None]
    )
    position = route_dest * CAP + jnp.sum(same_dest.astype(jnp.int32), axis=1)
    chooser = jnp.arange(slot_count)[:, None] == position[None, :]
    outgoing = jnp.dot(
        chooser.astype(jnp.bfloat16),
        template.reshape(pieces, band_rows * columns),
        preferred_element_type=jnp.float32,
    ).astype(jnp.bfloat16)
    offsets = jnp.sum(jnp.where(chooser, route_row[None, :] + 1, 0), axis=1) - 1
    arrived, arrived_rows = (
        lax.all_to_all(
            outgoing.reshape(devices, CAP * band_rows, columns),
            ("ccd", "strip"),
            split_axis=0,
            concat_axis=0,
            tiled=True,
        ),
        lax.all_to_all(
            offsets.reshape(devices, CAP), ("ccd", "strip"), split_axis=0, concat_axis=0, tiled=True
        ),
    )
    arrived = arrived.reshape(slot_count * band_rows, columns)
    arrived_rows = arrived_rows.reshape(slot_count)
    first_row = jnp.where(arrived_rows >= 0, arrived_rows, -2 * band_rows)
    target = (first_row[:, None] + jnp.arange(band_rows)[None, :]).reshape(
        1, slot_count * band_rows
    )
    placer = (jnp.arange(height)[:, None] == target).astype(jnp.bfloat16)
    coadd_image = jnp.dot(placer, arrived, preferred_element_type=jnp.float32).astype(jnp.bfloat16)
    framed = with_halo(coadd_image, (("strip", 0),), HALF)
    basis_images = separable(framed, kern_row, kern_col, jnp.bfloat16)
    basis_cut = stamp_blocks(basis_images, stamp_row, stamp_col).reshape(
        stamp_row.shape[0], BASIS, STAMP * STAMP
    )
    sky_cut = stamp_blocks(science[None], stamp_row, stamp_col).reshape(
        stamp_row.shape[0], STAMP * STAMP
    )
    inverse = 1.0 / (noise_sigma[0] * noise_sigma[0])
    gram_matrix = (
        jnp.einsum("kbp,kcp->bc", basis_cut, basis_cut, preferred_element_type=jnp.float32)
        * inverse
    )
    target_sum = (
        jnp.einsum(
            "kbp,kp->b", basis_cut.astype(jnp.float32), sky_cut, precision=lax.Precision.HIGHEST
        )
        * inverse
    )
    gram_matrix, target_sum = lax.psum((gram_matrix, target_sum), ("ccd", "strip"))
    factor = jnp.linalg.cholesky(gram_matrix)
    middle = lax.linalg.triangular_solve(factor, target_sum[:, None], left_side=True, lower=True)
    coefficients = lax.linalg.triangular_solve(
        factor, middle, left_side=True, lower=True, transpose_a=True
    )[:, 0]
    model_image = jnp.sum(coefficients[:, None, None] * basis_images.astype(jnp.float32), axis=0)
    difference = ((science - model_image) / noise_sigma[0]).astype(jnp.bfloat16)
    stamp_cut = stamp_blocks(difference[None], stamp_row, stamp_col).reshape(
        stamp_row.shape[0], STAMP * STAMP
    )
    band_count = height // band_rows
    relay_cap = max(2, 2 * band_count // ccd_count)
    own_ccd = lax.axis_index("ccd")
    band_order = jnp.arange(band_count)
    repeats = (band_shift[:, None] == band_shift[None, :]) & (
        band_order[None, :] < band_order[:, None]
    )
    repeat_count = jnp.sum(repeats.astype(jnp.int32), axis=1)
    outward = (own_ccd + band_shift) % ccd_count * relay_cap + repeat_count
    sender = (jnp.arange(ccd_count * relay_cap)[:, None] == outward[None, :]).astype(jnp.bfloat16)
    leaving = jnp.dot(
        sender,
        difference.reshape(band_count, band_rows * columns),
        preferred_element_type=jnp.float32,
    ).astype(jnp.bfloat16)
    landed = lax.all_to_all(
        leaving.reshape(ccd_count, relay_cap * band_rows, columns),
        "ccd",
        split_axis=0,
        concat_axis=0,
        tiled=True,
    )
    inward = (own_ccd - band_shift) % ccd_count * relay_cap + repeat_count
    picker = (inward[:, None] == jnp.arange(ccd_count * relay_cap)[None, :]).astype(jnp.bfloat16)
    patch_image = (
        jnp.dot(
            picker,
            landed.reshape(ccd_count * relay_cap, band_rows * columns),
            preferred_element_type=jnp.float32,
        )
        .astype(jnp.bfloat16)
        .reshape(height, columns)
    )
    framed_patch = with_halo(patch_image, (("strip", 0),), PSF_HALF)
    filtered = separable(framed_patch, psf_row[None, :], psf_col[None, :], jnp.float32)[0]
    return (difference, stamp_cut, coefficients, filtered)


def solution(mesh):
    placed = (
        P(("ccd", "strip"), None, None),
        P(("ccd", "strip")),
        P(("ccd", "strip")),
        P(),
        P(),
        P(("ccd", "strip"), None),
        P(("ccd", "strip")),
        P(("ccd", "strip")),
        P(("ccd", "strip")),
        P(),
        P(),
        P(),
    )
    return jax.shard_map(
        shards,
        mesh=mesh,
        in_specs=placed,
        out_specs=(
            P(("ccd", "strip"), None),
            P(("ccd", "strip"), None),
            P(),
            P(("ccd", "strip"), None),
        ),
        check_vma=False,
    )
```

profile of v0, /device:TPU:1, one launch (start us, length us, event | category | flops | bytes accessed | tf_op | source)
XLA Modules:
  0.0 433.9 jit_solution(4428196305884269868)
XLA Ops:
  3.1 11.5 %all-to-all-start = ((s32[128,1,2]{2,1,0:T(1,128)}), s32[128,1,2]{2,1,0:T(1,128)S(1)}, u32[]{:S(2)}, u32[]{:S(2)}) async-start(s32[128,1,2]{2,1,0:T(1,128)} %bitcast.9), calls=%async_computation | async-start | bytes 131072 | tf_op jit(solution)/shard_map/all_to_all | solution.py:128
  17.1 2.3 reshape.196
  19.4 4.7 %all-to-all-done = s32[128,1,2]{2,1,0:T(1,128)S(1)} async-done(((s32[128,1,2]{2,1,0:T(1,128)}), s32[128,1,2]{2,1,0:T(1,128)S(1)}, u32[]{:S(2)}, u32[]{:S(2)}) %all-to-all-start) | async-done | bytes 1056 | tf_op jit(solution)/shard_map/all_to_all | solution.py:128
  24.1 5.6 %all-to-all-start.1 = ((bf16[128,16,512]{2,1,0:T(8,128)(2,1)}), bf16[128,16,512]{2,1,0:T(8,128)(2,1)}, u32[]{:S(2)}, u32[]{:S(2)}) async-start(bf16[128,16,512]{2,1,0:T(8,128)(2,1)} %reshape.196), calls=%async_computation.1 | async-start | bytes 4194304 | tf_op jit(solution)/shard_map/all_to_all | solution.py:121
  29.7 55.0 %while.19 = (s32[]{:T(128)}, f32[1,1024,512]{2,1,0:T(8,128)}, s32[16,3]{0,1:T(4,128)S(1)}, f32[16,1,32,32]{3,2,1,0:T(8,128)}, s32[]{:T(128)}) while((s32[]{:T(128)}, f32[1,1024,512]{2,1,0:T(8,128)}, s32[16,3]{0,1:T(4,128)S(1)}, f32[16,1,32,32]{3,2,1,0:T(8,128)}, s32[]{:T(128)}) %tuple.98), condition=%wide.while_cond.1, body=%wide.while_body.1.sunk | while | flops 2 | bytes 34409 | solution.py:79
  30.4 2.8 bitcast_dynamic-update-slice_fusion.7
  33.8 2.8 bitcast_dynamic-update-slice_fusion.7
  37.3 2.8 bitcast_dynamic-update-slice_fusion.7
  40.7 2.8 bitcast_dynamic-update-slice_fusion.7
  44.1 2.8 bitcast_dynamic-update-slice_fusion.7
  47.6 2.8 bitcast_dynamic-update-slice_fusion.7
  51.0 2.8 bitcast_dynamic-update-slice_fusion.7
  54.5 2.8 bitcast_dynamic-update-slice_fusion.7
  57.9 2.7 bitcast_dynamic-update-slice_fusion.7
  61.3 2.7 bitcast_dynamic-update-slice_fusion.7
  64.7 2.8 bitcast_dynamic-update-slice_fusion.7
  68.2 2.8 bitcast_dynamic-update-slice_fusion.7
  71.6 2.8 bitcast_dynamic-update-slice_fusion.7
  75.1 2.8 bitcast_dynamic-update-slice_fusion.7
  78.5 2.7 bitcast_dynamic-update-slice_fusion.7
  81.9 2.8 bitcast_dynamic-update-slice_fusion.7
  84.9 2.9 convert_bitcast_fusion.1
  91.1 3.9 fusion.27
  96.3 3.2 collective-permute-start.1
  99.6 3.4 copy.72
  103.0 1.8 copy.73
  112.1 76.0 %while.17 = (s32[]{:T(128)}, bf16[12,1024,512]{2,1,0:T(8,128)(2,1)}, bf16[12,276,256]{2,1,0:T(8,128)(2,1)}, bf16[1044,2,276]{0,2,1:T(8,128)(2,1)S(1)}, bf16[12,276,256]{2,1,0:T(8,128)(2,1)}, /*index=5*/s32[]{:T(128)}) while((s32[]{:T(128)}, bf16[12,1024,512]{2,1,0:T(8,128)(2,1)}, bf16[12,276,256]{2,1,0:T(8,128)(2,1)}, ...), condition=%wide.region_3.4_spmd, body=%wide.region_2.3_spmd.sunk | while | flops 587220992 | bytes 13569157 | solution.py:73
  112.1 1.8 fusion.102
  124.7 1.8 fusion.102
  131.0 1.8 fusion.102
  150.0 1.8 fusion.102
  175.5 1.8 fusion.102
  188.1 59.7 %while.18 = (s32[]{:T(128)}, bf16[12,1024,512]{2,1,0:T(8,128)(2,1)}, s32[16,3]{0,1:T(4,128)S(1)}, bf16[16,12,32,32]{3,2,1,0:T(8,128)(2,1)}, s32[]{:T(128)}) while((s32[]{:T(128)}, bf16[12,1024,512]{2,1,0:T(8,128)(2,1)}, s32[16,3]{0,1:T(4,128)S(1)}, bf16[16,12,32,32]{3,2,1,0:T(8,128)(2,1)}, s32[]{:T(128)}) %tuple.99), condition=%wide.while_cond, body=%wide.while_body.sunk | while | flops 2 | bytes 198249 | solution.py:79
  188.8 3.1 bitcast_dynamic-update-slice_fusion.6
  192.5 3.1 bitcast_dynamic-update-slice_fusion.6
  196.3 3.1 bitcast_dynamic-update-slice_fusion.6
  200.0 3.1 bitcast_dynamic-update-slice_fusion.6
  203.8 3.1 bitcast_dynamic-update-slice_fusion.6
  207.5 3.1 bitcast_dynamic-update-slice_fusion.6
  211.2 3.1 bitcast_dynamic-update-slice_fusion.6
  215.0 3.1 bitcast_dynamic-update-slice_fusion.6
  218.7 3.0 bitcast_dynamic-update-slice_fusion.6
  222.4 3.0 bitcast_dynamic-update-slice_fusion.6
  226.1 3.1 bitcast_dynamic-update-slice_fusion.6
  229.9 3.1 bitcast_dynamic-update-slice_fusion.6
  233.6 3.1 bitcast_dynamic-update-slice_fusion.6
  237.3 3.1 bitcast_dynamic-update-slice_fusion.6
  241.1 3.0 bitcast_dynamic-update-slice_fusion.6
  244.8 3.1 bitcast_dynamic-update-slice_fusion.6
  247.9 3.0 reshape.295
  252.5 67.3 %all-reduce.2 = (f32[12,12]{0,1:T(8,128)S(1)}, f32[12]{0:T(128)S(1)}) all-reduce(f32[12,12]{0,1:T(8,128)S(1)} %fusion.42, f32[12]{0:T(128)S(1)} %fusion.45), channel_id=1, replica_groups=mesh['ccd'=64,'strip'=2] {'ccd','strip'}, use_global_device_ids=true, to_apply=%region_4.5 | all-reduce | flops 156 | bytes 1248 | tf_op jit(solution)/shard_map/psum | solution.py:159
  323.6 7.4 %multiply_reduce_fusion = f32[1024,512]{1,0:T(8,128)S(1)} fusion(bf16[12,1024,512]{2,1,0:T(8,128)(2,1)} %get-tuple-element.344, f32[12]{0:T(128)S(1)} %convolution_bitcast_fusion), kind=kLoop, calls=%fused_computation.24 | loop fusion | flops 18350080 | bytes 14680112 | tf_op jit(solution)/shard_map/reduce_sum | solution.py:165
  331.0 2.2 divide_convert_fusion
  334.4 1.9 convolution_convert_fusion.2
  336.4 2.3 reshape.204
  338.7 5.7 %all-to-all-start.2 = ((bf16[64,32,512]{2,1,0:T(8,128)(2,1)}), bf16[64,32,512]{2,1,0:T(8,128)(2,1)S(1)}, u32[]{:S(2)}, u32[]{:S(2)}) async-start(bf16[64,32,512]{2,1,0:T(8,128)(2,1)} %reshape.204), calls=%async_computation.2 | async-start | bytes 4194304 | tf_op jit(solution)/shard_map/all_to_all | solution.py:185
  348.4 23.4 %all-to-all-done.2 = bf16[64,32,512]{2,1,0:T(8,128)(2,1)S(1)} async-done(((bf16[64,32,512]{2,1,0:T(8,128)(2,1)}), bf16[64,32,512]{2,1,0:T(8,128)(2,1)S(1)}, u32[]{:S(2)}, u32[]{:S(2)}) %all-to-all-start.2) | async-done | bytes 2097184 | tf_op jit(solution)/shard_map/all_to_all | solution.py:185
  371.8 2.3 reshape.205
  374.1 2.1 convolution_convert_fusion.4
  378.1 5.3 %collective-permute-start.3 = (bf16[7,512]{1,0:T(8,128)(2,1)S(1)}, bf16[7,512]{1,0:T(8,128)(2,1)S(1)}, u32[]{:S(2)}, u32[]{:S(2)}) collective-permute-start(bf16[7,512]{1,0:T(8,128)(2,1)S(1)} %get-tuple-element.145), channel_id=1, source_target_pairs={{1,0},{3,2},{5,4},{7,6},{9,8},{11,10},{13,12},{15,14},{17,16},{19,... | collective-permute-start | bytes 21512 | tf_op jit(solution)/shard_map/ppermute | solution.py:21
  383.4 31.8 %while.20 = (s32[]{:T(128)}, bf16[1,1024,512]{2,1,0:T(8,128)(2,1)S(1)}, s32[16,3]{0,1:T(4,128)S(1)}, bf16[16,1,32,32]{3,2,1,0:T(8,128)(2,1)S(1)}, s32[]{:T(128)}) while((s32[]{:T(128)}, bf16[1,1024,512]{2,1,0:T(8,128)(2,1)S(1)}, s32[16,3]{0,1:T(4,128)S(1)}, bf16[16,1,32,32]{3,2,1,0:T(8,128)(2,1)S(1)}, s32[]{:T(128)}) %tuple.100), condition=%wide.while_cond.2, body=%wide.while_body.2.sunk | while | flops 2 | bytes 16501 | solution.py:79
  416.2 7.0 %concatenate.20 = bf16[1038,512]{1,0:T(8,128)(2,1)} concatenate(bf16[7,512]{1,0:T(8,128)(2,1)S(1)} %collective-permute-done.2, bf16[1024,512]{1,0:T(8,128)(2,1)S(1)} %reshape.206, bf16[7,512]{1,0:T(8,128)(2,1)S(1)} %collective-permute-done.3), dimensions={0} | concatenate | bytes 2125824 | tf_op jit(solution)/shard_map/concatenate | solution.py:22
  423.3 3.2 pad_slice_fusion.3
  431.7 2.2 fusion.31
  (348 shorter events, 154.0 us)
Async XLA Ops:
  0.6 84.3 %copy-start = (bf16[12,21]{1,0:T(8,128)(2,1)S(1)}, bf16[12,21]{1,0:T(8,128)(2,1)}, u32[]{:S(2)}) copy-start(bf16[12,21]{1,0:T(8,128)(2,1)} %param.18) | copy-start | bytes 1516
  3.1 21.0 %all-to-all-start = ((s32[128,1,2]{2,1,0:T(1,128)}), s32[128,1,2]{2,1,0:T(1,128)S(1)}, u32[]{:S(2)}, u32[]{:S(2)}) async-start(s32[128,1,2]{2,1,0:T(1,128)} %bitcast.9), calls=%async_computation | async-start | bytes 131072 | tf_op jit(solution)/shard_map/all_to_all | solution.py:128
  16.3 0.7 copy-start.7
  16.3 0.7 copy-start.8
  19.4 65.3 %copy-start.6 = (s32[128]{0:T(128)S(1)}, s32[128]{0:T(128)}, u32[]{:S(2)}) copy-start(s32[128]{0:T(128)} %param.23) | copy-start | bytes 1540
  24.1 67.0 %all-to-all-start.1 = ((bf16[128,16,512]{2,1,0:T(8,128)(2,1)}), bf16[128,16,512]{2,1,0:T(8,128)(2,1)}, u32[]{:S(2)}, u32[]{:S(2)}) async-start(bf16[128,16,512]{2,1,0:T(8,128)(2,1)} %reshape.196), calls=%async_computation.1 | async-start | bytes 4194304 | tf_op jit(solution)/shard_map/all_to_all | solution.py:121
  29.7 58.2 %copy-start.4 = (bf16[12,21]{1,0:T(8,128)(2,1)S(1)}, bf16[12,21]{1,0:T(8,128)(2,1)}, u32[]{:S(2)}) copy-start(bf16[12,21]{1,0:T(8,128)(2,1)} %param.17) | copy-start | bytes 1516
  95.0 11.6 %collective-permute-start = (bf16[10,512]{1,0:T(8,128)(2,1)S(1)}, bf16[10,512]{1,0:T(8,128)(2,1)S(1)}, u32[]{:S(2)}, u32[]{:S(2)}) collective-permute-start(bf16[10,512]{1,0:T(8,128)(2,1)S(1)} %get-tuple-element.148), channel_id=1, source_target_pairs={{0,1},{2,3},{4,5},{6,7},{8,9},{10,11},{12,13},{14,15},{16,17},{18,... | collective-permute-start | bytes 30728 | tf_op jit(solution)/shard_map/ppermute | solution.py:20
  96.3 10.3 %collective-permute-start.1 = (bf16[10,512]{1,0:T(8,128)(2,1)S(1)}, bf16[10,512]{1,0:T(8,128)(2,1)S(1)}, u32[]{:S(2)}, u32[]{:S(2)}) collective-permute-start(bf16[10,512]{1,0:T(8,128)(2,1)S(1)} %get-tuple-element.147), channel_id=1, source_target_pairs={{1,0},{3,2},{5,4},{7,6},{9,8},{11,10},{13,12},{15,14},{17,16},{19,... | collective-permute-start | bytes 30728 | tf_op jit(solution)/shard_map/ppermute | solution.py:21
  247.9 3.0 copy-start.3
  323.6 7.4 %copy-start.5 = (f32[12]{0:T(128)}, f32[12]{0:T(128)S(1)}, u32[]{:S(2)}) copy-start(f32[12]{0:T(128)S(1)} %convolution_bitcast_fusion) | copy-start | bytes 148
  338.7 6.3 %copy-start.9 = (bf16[15]{0:T(256)(128)(2,1)S(1)}, bf16[15]{0:T(256)(128)(2,1)}, u32[]{:S(2)}) copy-start(bf16[15]{0:T(256)(128)(2,1)} %param.25) | copy-start | bytes 94
  338.7 33.1 %all-to-all-start.2 = ((bf16[64,32,512]{2,1,0:T(8,128)(2,1)}), bf16[64,32,512]{2,1,0:T(8,128)(2,1)S(1)}, u32[]{:S(2)}, u32[]{:S(2)}) async-start(bf16[64,32,512]{2,1,0:T(8,128)(2,1)} %reshape.204), calls=%async_computation.2 | async-start | bytes 4194304 | tf_op jit(solution)/shard_map/all_to_all | solution.py:185
  345.0 1.7 copy-start.10
  376.8 39.5 %collective-permute-start.2 = (bf16[7,512]{1,0:T(8,128)(2,1)S(1)}, bf16[7,512]{1,0:T(8,128)(2,1)S(1)}, u32[]{:S(2)}, u32[]{:S(2)}) collective-permute-start(bf16[7,512]{1,0:T(8,128)(2,1)S(1)} %get-tuple-element.146), channel_id=1, source_target_pairs={{0,1},{2,3},{4,5},{6,7},{8,9},{10,11},{12,13},{14,15},{16,17},{18,... | collective-permute-start | bytes 21512 | tf_op jit(solution)/shard_map/ppermute | solution.py:20
  378.1 38.2 %collective-permute-start.3 = (bf16[7,512]{1,0:T(8,128)(2,1)S(1)}, bf16[7,512]{1,0:T(8,128)(2,1)S(1)}, u32[]{:S(2)}, u32[]{:S(2)}) collective-permute-start(bf16[7,512]{1,0:T(8,128)(2,1)S(1)} %get-tuple-element.145), channel_id=1, source_target_pairs={{1,0},{3,2},{5,4},{7,6},{9,8},{11,10},{13,12},{15,14},{17,16},{19,... | collective-permute-start | bytes 21512 | tf_op jit(solution)/shard_map/ppermute | solution.py:21
  415.3 11.3 %copy-start.2 = (bf16[1,1024,512]{2,1,0:T(8,128)(2,1)}, bf16[1,1024,512]{2,1,0:T(8,128)(2,1)S(1)}, u32[]{:S(2)}) copy-start(bf16[1,1024,512]{2,1,0:T(8,128)(2,1)S(1)} %get-tuple-element.348) | copy-start | bytes 3145732
  428.2 1.0 copy-start.12
  430.4 1.2 copy-start.11
  431.5 2.4 copy-start.1
where the time goes:
time: 438 us; the launch traced here: 434 us
  local copies, waits for them, and re-layouts  222 us (51%)
  blocking collectives  67.3 us (15%)
  matrix products  63.2 us (14%)
  starting transfers between devices  34 us (8%)
  waiting for transfers between devices  28 us (6%)
  other arithmetic  16.5 us (4%)
    gather x144, local copies, waits for them, and re-layouts  146 us
    psum x1, blocking collectives, shards(): lax.psum((gram_matrix, target_sum), ('ccd', 'strip'))  67.3 us
    all_to_all x1, waiting for transfers between devices, shards(): lax.all_to_all(leaving.reshape(ccd_count, relay_cap * band_rows, columns)...  23.4 us
    dot_general x13, matrix products, one_kernel(): jnp.einsum('ij,kiw->kjw', row_table, stacked, preferred_element_type=jnp....  22.6 us
    dot_general x13, matrix products, one_kernel(): jnp.einsum('rkc,co->rko', windows, col_table, preferred_element_type=jnp....  22.2 us
    dynamic_update_slice x12, local copies, waits for them, and re-layouts, separable(): return lax.map(one_kernel, (col_tables, row_tables))  12.9 us
    slice x65, local copies, waits for them, and re-layouts, row_windows(): padded[first_row:first_row + block_size + 2 * half_width]  12.5 us
    all_to_all x1, starting transfers between devices, shards(): lax.all_to_all(offsets.reshape(devices, CAP), ('ccd', 'strip'), split_axi...  11.5 us
  transfers between devices with their start and end apart: 7, of which 2 were waited for; matrix products, arithmetic and copies ran while one was open for 25% of the time, Pallas kernels for 0%

commit v1 on v0

v1 whole, which is shorter than its diff:
```python
import jax
import jax.numpy as jnp
from jax import lax
from jax.experimental import pallas as pl
from jax.experimental.pallas import tpu as pltpu
from jax.sharding import PartitionSpec as P

BASIS = 12
KTAPS = 21
PSF_TAPS = 15
STAMPS = 16
ROWS = 1024
COLS = 512
PAD = 16
FRAMED = ROWS + 2 * PAD
STEP = 224
SPAN = 256
WIN = 56
LANES = BASIS * 32
BOTH = ("ccd", "strip")
SWAP = [(0, 1), (1, 0)]
F32 = jnp.float32
BF16 = jnp.bfloat16
I32 = jnp.int32
HIGH = lax.Precision.HIGHEST

BLOCKS = [(j, min(STEP, ROWS - j), min(SPAN, FRAMED - j)) for j in range(0, ROWS, STEP)]


def vmem():
    return pl.BlockSpec(memory_space=pltpu.VMEM)


def smem():
    return pl.BlockSpec(memory_space=pltpu.SMEM)


def params(mib):
    return pltpu.CompilerParams(vmem_limit_bytes=mib * 2**20)


def iota(shape, dim):
    return lax.broadcasted_iota(I32, shape, dim)


def shape(dims, dtype):
    return jax.ShapeDtypeStruct(dims, dtype)


def cost(flops, moved):
    return pl.CostEstimate(flops=flops, bytes_accessed=moved, transcendentals=0)


def pack_body(dest, row, pieces, out, count, rows):
    devices = out.shape[0]

    def clear(d, c):
        count[d] = 0
        rows[2 * d] = 4096
        rows[2 * d + 1] = 4096
        return c

    lax.fori_loop(0, devices, clear, 0, unroll=8)
    out[...] = jnp.zeros(out.shape, out.dtype)

    def place(i, c):
        d = dest[i]
        k = count[d]
        count[d] = k + 1
        rows[2 * d + k] = row[i]
        piece = pieces[i]
        for q in range(4):
            out[d, 4 * k + q] = piece[:, 128 * q : 128 * (q + 1)]
        return c

    lax.fori_loop(0, pieces.shape[0], place, 0, unroll=8)
    sub, lane = iota((8, 128), 0), iota((8, 128), 1)

    def tell(d, c):
        target = jnp.where(lane < 64, rows[2 * d], rows[2 * d + 1]) + sub
        told = jnp.where((lane & 32) == 0, target >> 5, target & 31)
        out[d, 8] = told.astype(F32).astype(BF16)
        return c

    lax.fori_loop(0, devices, tell, 0, unroll=8)


def pack(route_dest, route_row, template, devices):
    return pl.pallas_call(
        pack_body,
        out_shape=shape((devices, 9, 8, 128), BF16),
        in_specs=[smem(), smem(), vmem()],
        out_specs=vmem(),
        scratch_shapes=[pltpu.SMEM((devices,), I32), pltpu.SMEM((2 * devices,), I32)],
        compiler_params=params(32),
        name="pack",
    )(route_dest, route_row, template)


def band_table(taps, count, size, offset):
    lag = iota((128, 128), 0) - iota((128, 128), 1) + offset
    table = jnp.zeros((128, 128), F32)
    for t in range(count):
        if -127 <= t - offset <= 127:
            table = jnp.where(lag == t, taps(t), table)
    return table.astype(BF16)


def window(ref, first_row, rows, first_col):
    tile = jnp.minimum(jnp.maximum(first_col, 0) >> 7, 2) * 128
    top = jnp.minimum((first_row >> 3) * 8, ref.shape[0] - rows - 8)
    block = ref[pl.ds(pl.multiple_of(top, 8), rows + 8), pl.ds(pl.multiple_of(tile, 128), 256)]
    turn = (256 - (first_col - tile)) & 255
    block = pltpu.roll(block, turn, 1)[:, :128]
    return pltpu.roll(block, lax.rem(rows + 8 - (first_row - top), rows + 8), 0)[:rows]


def tables_body(
    kr, kc, pr, pc, kcl, shift, srow, scol, science,
    cols_out, rows_out, pcols_out, prows_out, stamp_out, slot_out, pick_out, sky_out, count,
):
    for b in range(BASIS):
        for k in range(3):
            cols_out[b, k] = band_table(lambda t: kc[b, t], KTAPS, 128, 10 + 128 * (k - 1))
        for k in range(2):
            lag = iota((128, 128), 1) - iota((128, 128), 0) - 6 + 128 * k
            table = jnp.zeros((128, 128), F32)
            for t in range(KTAPS):
                table = jnp.where(lag == t, kr[b, t], table)
            rows_out[b, k] = table.astype(BF16)
    for k in range(3):
        pcols_out[k] = band_table(lambda t: pc[t], PSF_TAPS, 128, 7 + 128 * (k - 1))
    for k in range(2):
        lag = iota((128, 128), 1) - iota((128, 128), 0) - 9 + 128 * k
        table = jnp.zeros((128, 128), F32)
        for t in range(PSF_TAPS):
            table = jnp.where(lag == t, pr[t], table)
        prows_out[k] = table.astype(BF16)
    lag = iota((128, LANES), 0) - (iota((128, LANES), 1) & 31)
    table = jnp.zeros((128, LANES), F32)
    for t in range(KTAPS):
        table = jnp.where(lag == t, kcl[t : t + 1, :], table)
    stamp_out[...] = table.astype(BF16)

    own, ccds = lax.axis_index("ccd"), lax.axis_size("ccd")
    cap = slot_out.shape[0] * 2 // ccds

    def clear(v, c):
        count[v] = 0
        return c

    lax.fori_loop(0, ccds, clear, 0)

    def seat(m, c):
        v = shift[m]
        k = count[v]
        count[v] = k + 1
        slot_out[m] = lax.rem(own + v, ccds) * cap + k
        pick_out[m] = lax.rem(own - v + ccds, ccds) * cap + k
        return c

    lax.fori_loop(0, slot_out.shape[0], seat, 0)
    lane = iota((32, 128), 1)

    def cut(s, c):
        sky = jnp.where(lane < 32, window(science, srow[s], 32, scol[s]), 0.0)
        sky = sky + pltpu.roll(sky, 32, 1)
        sky_out[s] = sky + pltpu.roll(sky, 64, 1)
        return c

    lax.fori_loop(0, STAMPS, cut, 0)


def tables(kern_row, kern_col, psf_row, psf_col, band_shift, stamp_row, stamp_col, science):
    kc = kern_col.astype(F32)
    lanes = jnp.pad(jnp.repeat(kc.T, 32, axis=1), ((0, 3), (0, 0)))
    return pl.pallas_call(
        tables_body,
        out_shape=(
            shape((BASIS, 3, 128, 128), BF16),
            shape((BASIS, 2, 128, 128), BF16),
            shape((3, 128, 128), BF16),
            shape((2, 128, 128), BF16),
            shape((128, LANES), BF16),
            shape(band_shift.shape, I32),
            shape(band_shift.shape, I32),
            shape((STAMPS, 32, 128), F32),
        ),
        in_specs=[smem()] * 4 + [vmem()] + [smem()] * 3 + [vmem()],
        out_specs=(vmem(),) * 5 + (smem(),) * 2 + (vmem(),),
        scratch_shapes=[pltpu.SMEM((64,), I32)],
        compiler_params=params(32),
        cost_estimate=cost(2 * 10**9, 4 * 10**6),
        name="tables",
    )(
        kern_row.astype(F32), kc, psf_row.astype(F32), psf_col.astype(F32), lanes,
        band_shift, stamp_row, stamp_col, science,
    )


def coadd_body(arrived, out, edge, held):
    senders = arrived.shape[0]
    half = senders * 8
    told = arrived[:, 8].astype(F32).reshape(half, 128).T
    target = jnp.concatenate(
        [told[64 * k : 64 * k + 1] * 32.0 + told[64 * k + 32 : 64 * k + 33] for k in range(2)], axis=1
    ).astype(I32)
    for k in range(2):
        for q in range(4):
            part = arrived[:, 4 * k + q].astype(F32).reshape(half, 128)
            held[half * k : half * (k + 1), 128 * q : 128 * (q + 1)] = part.astype(BF16)
    for m in range(0, ROWS, 256):
        hit = (iota((256, 2 * half), 0) + m) == target
        placer = jnp.where(hit, 1.0, 0.0).astype(BF16)
        out[m : m + 256] = jnp.dot(placer, held[...], preferred_element_type=F32).astype(BF16)
    strip = lax.axis_index("strip")

    @pl.when(strip == 0)
    def _():
        edge[...] = out[ROWS - PAD :]

    @pl.when(strip != 0)
    def _():
        edge[...] = out[:PAD]


def coadd(arrived):
    senders = arrived.shape[0]
    return pl.pallas_call(
        coadd_body,
        out_shape=(shape((ROWS, COLS), BF16), shape((PAD, COLS), BF16)),
        in_specs=[vmem()],
        out_specs=(vmem(), vmem()),
        scratch_shapes=[pltpu.VMEM((senders * 16, COLS), BF16)],
        compiler_params=params(40),
        name="coadd",
    )(arrived)


def frame(framed, image, near):
    strip = lax.axis_index("strip")
    rows = near[...].astype(F32)
    framed[PAD : PAD + ROWS] = image[...].astype(framed.dtype)
    framed[:PAD] = jnp.where(strip == 0, 0.0, rows).astype(framed.dtype)
    framed[PAD + ROWS :] = jnp.where(strip == 0, rows, 0.0).astype(framed.dtype)


def stamps_body(image, near, sigma, srow, scol, table, krl, sky, out, framed, wins, across, basis):
    frame(framed, image, near)
    lane = iota((WIN, 128), 1)

    def cut(s, c):
        first = scol[s] - 10
        block = window(framed, srow[s] + 6, WIN, first)
        inside = (lane < 52) & (lane + first >= 0) & (lane + first < COLS)
        wins[s] = jnp.where(inside, block, 0.0)
        return c

    lax.fori_loop(0, STAMPS, cut, 0, unroll=2)
    wide = jnp.dot(
        wins[...].reshape(STAMPS * WIN, 128).astype(BF16), table[...], preferred_element_type=F32
    )
    across[...] = wide.astype(BF16).astype(F32).reshape(STAMPS, WIN, LANES)

    def rows(s, total):
        parts = []
        for q in range(3):
            acc = jnp.zeros((32, 128), F32)
            for t in range(KTAPS):
                acc = acc + krl[t : t + 1, 128 * q : 128 * q + 128] * across[s, t : t + 32, 128 * q : 128 * q + 128]
            done = acc.astype(BF16)
            basis[pl.ds(pl.multiple_of(s * 32, 32), 32), 128 * q : 128 * q + 128] = done
            parts.append(total[q] + jnp.sum(done.astype(F32) * sky[s], axis=0, keepdims=True))
        return tuple(parts)

    total = lax.fori_loop(0, STAMPS, rows, tuple(jnp.zeros((1, 128), F32) for _ in range(3)))
    total = jnp.concatenate(total, axis=1)
    pairs = lax.dot_general(
        basis[...], basis[...], (((0,), (0,)), ((), ())), preferred_element_type=F32
    )
    same = (iota((LANES, LANES), 0) & 31) == (iota((LANES, LANES), 1) & 31)
    pairs = jnp.where(same, pairs, 0.0)
    left = ((iota((16, LANES), 1) >> 5) == iota((16, LANES), 0)).astype(F32)
    right = ((iota((LANES, 128), 0) >> 5) == (iota((LANES, 128), 1) & 15)).astype(F32)
    gram = jnp.dot(jnp.dot(left, pairs, precision=HIGH, preferred_element_type=F32), right,
                   precision=HIGH, preferred_element_type=F32)
    goal = jnp.sum(left * total, axis=1, keepdims=True)
    row, col = iota((16, 128), 0), iota((16, 128), 1)
    both = jnp.where((col & 15) == BASIS, goal, gram)
    both = jnp.where((col >> 4) == (row & 7), both, 0.0) / (sigma[0] * sigma[0])
    packed = jnp.concatenate(
        [jnp.sum(both[:8], axis=0, keepdims=True), jnp.sum(both[8:], axis=0, keepdims=True)], axis=0
    )
    out[...] = jnp.broadcast_to(packed[None], out.shape)


def stamp_sums(image, near, sigma, srow, scol, table, krl, sky, devices):
    return pl.pallas_call(
        stamps_body,
        out_shape=shape((devices, 2, 128), F32),
        in_specs=[vmem(), vmem(), smem(), smem(), smem(), vmem(), vmem(), vmem()],
        out_specs=vmem(),
        scratch_shapes=[
            pltpu.VMEM((FRAMED, COLS), F32),
            pltpu.VMEM((STAMPS, WIN, 128), F32),
            pltpu.VMEM((STAMPS, WIN, LANES), F32),
            pltpu.VMEM((STAMPS * 32, LANES), BF16),
        ],
        compiler_params=params(40),
        name="stamp_sums",
    )(image, near, sigma, srow, scol, table, krl, sky)


def fill_cols(wide, blocks):
    for i in range(4):
        for o in range(4):
            if abs(i - o) <= 1:
                wide[128 * i : 128 * i + 128, 128 * o : 128 * o + 128] = blocks[i - o + 1]
            else:
                wide[128 * i : 128 * i + 128, 128 * o : 128 * o + 128] = jnp.zeros((128, 128), BF16)


def across_body(image, near, blocks, out, framed, wide):
    @pl.when(pl.program_id(0) == 0)
    def _():
        frame(framed, image, near)

    fill_cols(wide, blocks[0])
    for m in range(0, FRAMED, 352):
        out[0, m : m + 352] = jnp.dot(
            framed[m : m + 352], wide[...], preferred_element_type=F32
        ).astype(BF16)


def across_all(image, near, blocks):
    return pl.pallas_call(
        across_body,
        grid=(BASIS,),
        out_shape=shape((BASIS, FRAMED, COLS), BF16),
        in_specs=[
            pl.BlockSpec((ROWS, COLS), lambda b: (0, 0)),
            pl.BlockSpec((PAD, COLS), lambda b: (0, 0)),
            pl.BlockSpec((1, 3, 128, 128), lambda b: (b, 0, 0, 0)),
        ],
        out_specs=pl.BlockSpec((1, FRAMED, COLS), lambda b: (b, 0, 0)),
        scratch_shapes=[pltpu.VMEM((FRAMED, COLS), BF16), pltpu.VMEM((COLS, COLS), BF16)],
        compiler_params=params(32),
        cost_estimate=cost(2 * BASIS * FRAMED * COLS * COLS, 16 * 10**6),
        name="across",
    )(image, near, blocks)


def solve(sums):
    total = jnp.sum(sums[...], axis=0)
    row, col = iota((16, 128), 0), iota((16, 128), 1)
    both = jnp.where(row < 8, total[0:1], total[1:2])
    both = jnp.where((col >> 4) == (row & 7), both, 0.0)
    for turn in (64, 32, 16):
        both = both + pltpu.roll(both, turn, 1)
    for k in range(BASIS):
        pivot = both[k : k + 1] / both[k : k + 1, k : k + 1]
        both = jnp.where(row == k, pivot, both - both[:, k : k + 1] * pivot)
    return both[:, BASIS : BASIS + 1]


def fill_rows(table, blocks):
    table[:128, :128] = blocks[0]
    table[:128, 128:] = blocks[1]
    table[128:, :128] = jnp.zeros((STEP - 128, 128), BF16)
    table[128:, 128:] = blocks[0][: STEP - 128]


def difference_body(
    sums, across, blocks, science, sigma, slot, coef_out, diff_out, leave_out, model, coef, table
):
    b = pl.program_id(0)

    @pl.when(b == 0)
    def _():
        found = solve(sums)
        coef[...] = jnp.broadcast_to(found, coef.shape)
        eye = iota((16, 128), 0) == iota((16, 128), 1)
        coef_out[...] = jnp.sum(jnp.where(eye, found, 0.0), axis=0, keepdims=True)
        model[...] = jnp.zeros(model.shape, F32)

    fill_rows(table, blocks[0])
    weight = coef[pl.ds(b, 1), :]
    for first, rows, span in BLOCKS:
        basis = jnp.dot(
            table[:rows, :span], across[0, first : first + span], preferred_element_type=F32
        )
        model[first : first + rows] += weight * basis.astype(BF16).astype(F32)

    @pl.when(b == BASIS - 1)
    def _():
        scale = 1.0 / sigma[0]

        def finish(m, c):
            rows = pl.ds(pl.multiple_of(m * 16, 16), 16)
            left = (science[rows] - model[rows]) * scale
            diff_out[rows] = left.astype(BF16)
            leave_out[slot[2 * m]] = left[:8].astype(BF16)
            leave_out[slot[2 * m + 1]] = left[8:].astype(BF16)
            return c

        lax.fori_loop(0, ROWS // 16, finish, 0, unroll=4)


def difference_all(sums, across, blocks, science, sigma, slot, slots):
    whole = lambda *dims: pl.BlockSpec(dims, lambda b: (0,) * len(dims))
    return pl.pallas_call(
        difference_body,
        grid=(BASIS,),
        out_shape=(shape((1, 128), F32), shape((ROWS, COLS), BF16), shape((slots, 8, COLS), BF16)),
        in_specs=[
            whole(*sums.shape),
            pl.BlockSpec((1, FRAMED, COLS), lambda b: (b, 0, 0)),
            pl.BlockSpec((1, 2, 128, 128), lambda b: (b, 0, 0, 0)),
            whole(ROWS, COLS),
            smem(),
            smem(),
        ],
        out_specs=(whole(1, 128), whole(ROWS, COLS), whole(slots, 8, COLS)),
        scratch_shapes=[
            pltpu.VMEM((ROWS, COLS), F32),
            pltpu.VMEM((16, COLS), F32),
            pltpu.VMEM((STEP, SPAN), BF16),
        ],
        compiler_params=params(40),
        name="difference",
    )(sums, across, blocks, science, sigma, slot)


def cut_body(diff, srow, scol, out, wide):
    wide[...] = diff[...].astype(F32)
    row, lane = iota((32, 128), 0), iota((32, 128), 1)
    pick = (iota((8, 32), 1) >> 2 == iota((8, 32), 0)).astype(BF16)

    def cut(s, c):
        block = jnp.where(lane < 32, window(wide, srow[s], 32, scol[s]), 0.0)
        block = block + pltpu.roll(block, 32, 1)
        block = block + pltpu.roll(block, 64, 1)
        block = jnp.where((lane >> 5) == (row & 3), block, 0.0).astype(BF16)
        out[s] = jnp.dot(pick, block, preferred_element_type=F32).astype(BF16)
        return c

    lax.fori_loop(0, STAMPS, cut, 0)


def cut_stamps(diff, srow, scol):
    return pl.pallas_call(
        cut_body,
        out_shape=shape((STAMPS, 8, 128), BF16),
        in_specs=[vmem(), smem(), smem()],
        out_specs=vmem(),
        scratch_shapes=[pltpu.VMEM((ROWS, COLS), F32)],
        compiler_params=params(32),
        cost_estimate=cost(10**8, 3 * 10**6),
        name="cut_stamps",
    )(diff, srow, scol)


def smooth_body(landed, pick, blocks, out, patch, wide):
    fill_cols(wide, blocks)
    for first in range(0, ROWS, 256):

        def gather(m, c):
            pair = jnp.concatenate(
                [landed[pick[2 * m]].astype(F32), landed[pick[2 * m + 1]].astype(F32)], axis=0
            )
            patch[pl.ds(pl.multiple_of(m * 16, 16), 16)] = pair.astype(BF16)
            return c

        lax.fori_loop(first // 16, first // 16 + 16, gather, 0, unroll=4)
        out[first : first + 256] = jnp.dot(
            patch[first : first + 256], wide[...], preferred_element_type=F32
        ).astype(BF16)


def smooth(landed, pick, blocks):
    return pl.pallas_call(
        smooth_body,
        out_shape=shape((ROWS, COLS), BF16),
        in_specs=[vmem(), smem(), vmem()],
        out_specs=vmem(),
        scratch_shapes=[pltpu.VMEM((ROWS, COLS), BF16), pltpu.VMEM((COLS, COLS), BF16)],
        compiler_params=params(32),
        cost_estimate=cost(2 * ROWS * COLS * COLS, 3 * 10**6),
        name="smooth",
    )(landed, pick, blocks)


def filter_body(smoothed, near, cblocks, rblocks, out, framed, wide, table, tail):
    fill_cols(wide, cblocks)
    fill_rows(table, rblocks)
    tail[...] = jnp.concatenate(
        [near[...].astype(F32), jnp.zeros((8, COLS), F32)], axis=0
    ).astype(BF16)
    edge = jnp.dot(tail[...], wide[...], preferred_element_type=F32)
    edge = jnp.where(lax.axis_index("strip") == 0, edge, jnp.concatenate([edge[8:], edge[:8]], axis=0))
    frame(framed, smoothed, edge.astype(BF16))
    for first, rows, span in BLOCKS:
        out[first : first + rows] = jnp.dot(
            table[:rows, :span], framed[first : first + span], preferred_element_type=F32
        )


def filter_rows(smoothed, near, cblocks, rblocks):
    return pl.pallas_call(
        filter_body,
        out_shape=shape((ROWS, COLS), F32),
        in_specs=[vmem()] * 4,
        out_specs=vmem(),
        scratch_shapes=[
            pltpu.VMEM((FRAMED, COLS), BF16),
            pltpu.VMEM((COLS, COLS), BF16),
            pltpu.VMEM((STEP, SPAN), BF16),
            pltpu.VMEM((PAD, COLS), BF16),
        ],
        compiler_params=params(32),
        name="filter_rows",
    )(smoothed, near, cblocks, rblocks)


def shards(
    template, route_dest, route_row, kern_row, kern_col, science, noise_sigma,
    stamp_row, stamp_col, band_shift, psf_row, psf_col,
):
    ccds = lax.axis_size("ccd")
    devices = ccds * lax.axis_size("strip")
    bands = band_shift.shape[0]
    cap = 2 * bands // ccds
    outgoing = pack(route_dest, route_row, template, devices)
    arrived = lax.all_to_all(outgoing, BOTH, split_axis=0, concat_axis=0, tiled=True)
    cols, rows, pcols, prows, stamp_table, slot, pick, sky = tables(
        kern_row, kern_col, psf_row, psf_col, band_shift, stamp_row, stamp_col, science
    )
    krl = jnp.pad(jnp.repeat(kern_row.astype(F32).T, 32, axis=1), ((0, 3), (0, 0)))
    image, edge = coadd(arrived)
    near = lax.ppermute(edge, "strip", SWAP)
    sums = stamp_sums(
        image, near, noise_sigma, stamp_row, stamp_col, stamp_table, krl, sky, devices
    )
    sums = lax.all_to_all(sums, BOTH, split_axis=0, concat_axis=0, tiled=True)
    across = across_all(image, near, cols)
    coef, diff, leaving = difference_all(
        sums, across, rows, science, noise_sigma, slot, ccds * cap
    )
    landed = lax.all_to_all(
        leaving.reshape(ccds, cap, 8, COLS), "ccd", split_axis=0, concat_axis=0, tiled=True
    ).reshape(ccds * cap, 8, COLS)
    stamp_cut = cut_stamps(diff, stamp_row, stamp_col).reshape(STAMPS, 1024)
    last = jnp.where(lax.axis_index("strip") == 0, pick[bands - 1], pick[0])
    beside = lax.ppermute(
        lax.dynamic_slice(landed, (last, 0, 0), (1, 8, COLS))[0], "strip", SWAP
    )
    smoothed = smooth(landed, pick, pcols)
    filtered = filter_rows(smoothed, beside, pcols, prows)
    return (diff, stamp_cut, coef[0, :BASIS], filtered)


def solution(mesh):
    placed = (
        P(BOTH, None, None), P(BOTH), P(BOTH), P(), P(), P(BOTH, None),
        P(BOTH), P(BOTH), P(BOTH), P(), P(), P(),
    )
    return jax.shard_map(
        shards,
        mesh=mesh,
        in_specs=placed,
        out_specs=(P(BOTH, None), P(BOTH, None), P(), P(BOTH, None)),
        check_vma=False,
    )
```

time: 438 us -> 160 us (0.37)
  local copies, waits for them, and re-layouts: 222 us -> 19.2 us
  blocking collectives: 67.3 us -> 0 us
  matrix products: 63.2 us -> 0 us
  Pallas kernels: 0 us -> 56.2 us
  waiting for transfers between devices: 28 us -> 49.6 us
  other arithmetic: 16.5 us -> 1.63 us
    gather x144 -> x0, local copies, waits for them, and re-layouts: 146 us -> none
    psum x1 -> x0, blocking collectives: 67.3 us -> none  [shards(): lax.psum((gram_matrix, target_sum), ('ccd', 'strip'))]
    dot_general x36 -> x0, matrix products: 62.9 us -> none  [the longest x13 22.6 us: one_kernel(): jnp.einsum('ij,kiw->kjw', row_table, stacked, preferred_element_type=jnp....]
    pallas_call x0 -> x9, Pallas kernels: none -> 56.2 us  [the longest x1 13.9 us: difference_all(): pl.pallas_call(difference_body, grid=(BASIS,), out_shape=(shape((1, 128),...]
    all_to_all x3, waiting for transfers between devices: 28 us -> 49.6 us  [the longest x1 31.3 us: shards(): lax.all_to_all(outgoing, BOTH, split_axis=0, concat_axis=0, tiled=True)]
    slice x73 -> x1, local copies, waits for them, and re-layouts: 19.8 us -> 0.58 us  [shards(): last = jnp.where(lax.axis_index('strip') == 0, pick[bands - 1], pick[0])]
    reshape x11 -> x2, local copies, waits for them, and re-layouts: 16.1 us -> 0.21 us  [the longest x1 0.11 us: tables(): lanes = jnp.pad(jnp.repeat(kc.T, 32, axis=1), ((0, 3), (0, 0)))]
    unnamed x27 -> x61, local copies, waits for them, and re-layouts: 1.9 us -> 17.5 us
  transfers between devices with their start and end apart: 7 -> 5, of which waited for: 2 -> 2; matrix products, arithmetic and copies ran while one was open for 25% -> 2% of each run, Pallas kernels for 0% -> 18%
where the time goes in v1:
time: 160 us; the launch traced here: 159 us
  Pallas kernels  56.2 us (35%)
  waiting for transfers between devices  49.6 us (31%)
  starting transfers between devices  29.8 us (19%)
  local copies, waits for them, and re-layouts  19.2 us (12%)
  between operations  2.86 us (2%)
  other arithmetic  1.63 us (1%)
    all_to_all x1, waiting for transfers between devices, shards(): lax.all_to_all(outgoing, BOTH, split_axis=0, concat_axis=0, tiled=True)  31.3 us
    all_to_all x1, waiting for transfers between devices, shards(): lax.all_to_all(leaving.reshape(ccds, cap, 8, COLS), 'ccd', split_axis=0,...  18.3 us
    unnamed x61, local copies, waits for them, and re-layouts  17.5 us
    pallas_call x1, Pallas kernels, difference_all(): pl.pallas_call(difference_body, grid=(BASIS,), out_shape=(shape((1, 128),...  13.9 us
    all_to_all x1, starting transfers between devices, shards(): lax.all_to_all(outgoing, BOTH, split_axis=0, concat_axis=0, tiled=True)  11.5 us
    all_to_all x1, starting transfers between devices, shards(): lax.all_to_all(leaving.reshape(ccds, cap, 8, COLS), 'ccd', split_axis=0,...  10.7 us
    pallas_call x1, Pallas kernels, tables(): pl.pallas_call(tables_body, out_shape=(shape((BASIS, 3, 128, 128), BF16),...  10.6 us
    pallas_call x1, Pallas kernels, across_all(): pl.pallas_call(across_body, grid=(BASIS,), out_shape=shape((BASIS, FRAMED...  9.45 us
  transfers between devices with their start and end apart: 5, of which 2 were waited for; matrix products, arithmetic and copies ran while one was open for 2% of the time, Pallas kernels for 18%

profile of v1, /device:TPU:1, one launch (start us, length us, event | category | flops | bytes accessed | tf_op | source)
XLA Modules:
  0.0 159.3 jit_solution(13335363713723299814)
XLA Ops:
  0.6 0.0 copy-start.6
  0.6 1.2 copy-done.6
  1.9 0.7 copy-done.18
  2.5 0.7 copy-done.19
  3.2 2.2 %pack.1 = bf16[128,9,8,128]{3,2,1,0:T(8,128)(2,1)S(1)} custom-call(s32[128]{0:T(128)S(1)} %copy-done.18, s32[128]{0:T(128)S(1)} %copy-done.19, bf16[128,8,512]{2,1,0:T(8,128)(2,1)S(1)} %copy-done.6), custom_call_target="tpu_custom_call" | custom-call | tf_op jit(solution)/shard_map/pack/pallas_call | solution.py:89
  5.3 0.0 copy-start.1
  5.4 1.4 copy-done.1
  6.8 11.5 %all-to-all-start = ((bf16[128,9,8,128]{3,2,1,0:T(8,128)(2,1)}), bf16[128,9,8,128]{3,2,1,0:T(8,128)(2,1)S(1)}, u32[]{:S(2)}, u32[]{:S(2)}) async-start(bf16[128,9,8,128]{3,2,1,0:T(8,128)(2,1)} %copy-done.1), calls=%async_computation | async-start | bytes 4718592 | tf_op jit(solution)/shard_map/all_to_all | solution.py:534
  18.3 0.0 copy-done.26
  18.3 0.0 copy-done.27
  18.3 0.6 convert_bitcast_fusion
  18.9 0.1 copy.18
  19.0 0.1 broadcast_in_dim.6
  19.1 0.1 reshape.23
  19.2 0.0 copy-done.28
  19.2 0.5 convert_element_type.18.pr
  19.8 0.0 copy-done.29
  19.8 0.5 convert_element_type.19.pc
  20.3 31.3 %all-to-all-done.arrived = bf16[128,9,8,128]{3,2,1,0:T(8,128)(2,1)S(1)} async-done(((bf16[128,9,8,128]{3,2,1,0:T(8,128)(2,1)}), bf16[128,9,8,128]{3,2,1,0:T(8,128)(2,1)S(1)}, u32[]{:S(2)}, u32[]{:S(2)}) %all-to-all-start) | async-done | bytes 2359328 | tf_op jit(solution)/shard_map/all_to_all | solution.py:534
  51.6 3.2 %coadd.1 = (bf16[1024,512]{1,0:T(8,128)(2,1)S(1)}, bf16[16,512]{1,0:T(8,128)(2,1)}) custom-call(bf16[128,9,8,128]{3,2,1,0:T(8,128)(2,1)S(1)} %all-to-all-done.arrived), custom_call_target="tpu_custom_call" | custom-call | tf_op jit(solution)/shard_map/coadd/pallas_call | solution.py:229
  54.8 1.0 collective-permute-start
  55.8 0.0 copy-done.2
  55.8 0.0 copy-done.11
  55.8 0.0 copy-done.21
  55.8 0.0 copy-done.22
  55.8 0.0 copy-start.12
  55.8 0.6 copy-done.12
  56.5 0.7 copy-done.15
  57.1 0.7 copy-done.20
  57.8 10.6 %tables.1 = (bf16[12,3,128,128]{3,2,1,0:T(8,128)(2,1)S(1)}, bf16[12,2,128,128]{3,2,1,0:T(8,128)(2,1)S(1)}, bf16[3,128,128]{2,1,0:T(8,128)(2,1)S(1)}, bf16[2,128,...) custom-call(f32[12,21]{1,0:T(8,128)S(1)} %copy-done.11, ...), custom_call_target="tpu_custom_call" | custom-call | flops 2000000000 | bytes 4000000 | tf_op jit(solution)/shard_map/tables/pallas_call | solution.py:177
  68.4 0.0 copy-start.7
  68.4 0.9 copy-done.7
  69.3 0.6 copy-done.9
  69.9 1.0 copy-done.23
  70.9 0.0 copy-done.25
  70.9 0.1 copy.19
  71.0 0.1 broadcast_in_dim.7
  71.1 0.1 reshape.24
  71.9 0.0 collective-permute-done.near
  71.9 0.0 copy-done.13
  71.9 0.0 copy-done.16
  71.9 6.8 %stamp_sums.1 = f32[128,2,128]{2,1,0:T(2,128)} custom-call(bf16[1024,512]{1,0:T(8,128)(2,1)S(1)} %get-tuple-element.17.image, bf16[16,512]{1,0:T(8,128)(2,1)S(1)} %collective-permute-done.near, f32[1]{0:T(128)S(6)} %copy.23.sigma, s32[16]{0:T(128)S(1)} %copy-done.13, s32[16]{0:T(128)S(1)} %copy-done.16, bf16[128,384]{1,0:T(8,128)(2,1)S(1)} %get-tuple-element.19.table, ...), custom_call_target="tpu_custom_call" | custom-call | tf_op jit(solution)/shard_map/stamp_sums/pallas_call | solution.py:298
  78.7 3.5 %all-to-all-start.1 = ((f32[128,2,128]{2,1,0:T(2,128)}), f32[128,2,128]{2,1,0:T(2,128)S(1)}, u32[]{:S(2)}, u32[]{:S(2)}) async-start(f32[128,2,128]{2,1,0:T(2,128)} %stamp_sums.1), calls=%async_computation.1 | async-start | bytes 262144 | tf_op jit(solution)/shard_map/all_to_all | solution.py:544
  82.2 0.0 copy-start.24
  82.2 1.3 copy-done.24
  83.5 9.5 %across.1 = bf16[12,1056,512]{2,1,0:T(8,128)(2,1)S(1)} custom-call(bf16[1024,512]{1,0:T(8,128)(2,1)S(1)} %get-tuple-element.17.image, bf16[16,512]{1,0:T(8,128)(2,1)S(1)} %collective-permute-done.near, bf16[12,3,128,128]{3,2,1,0:T(8,128)(2,1)S(1)} %copy-done.24), custom_call_target="tpu_custom_call" | custom-call | flops 6643777536 | bytes 16000000 | tf_op jit(solution)/shard_map/across/pallas_call | solution.py:336
  92.9 0.0 copy-start
  92.9 4.7 %copy-done = bf16[12,1056,512]{2,1,0:T(8,128)(2,1)} copy-done((bf16[12,1056,512]{2,1,0:T(8,128)(2,1)}, bf16[12,1056,512]{2,1,0:T(8,128)(2,1)S(1)}, u32[]{:S(2)}) %copy-start) | copy-done | bytes 12976152
  97.6 0.0 all-to-all-done.1.sums
  97.6 0.0 copy-done.3
  97.6 1.1 copy-done.8
  98.7 13.9 %difference.1 = (f32[1,128]{1,0:T(1,128)S(1)}, bf16[1024,512]{1,0:T(8,128)(2,1)}, bf16[256,8,512]{2,1,0:T(8,128)(2,1)S(1)}) custom-call(f32[128,2,128]{2,1,0:T(2,128)S(1)} %all-to-all-done.1.sums, bf16[12,1056,512]{2,1,0:T(8,128)(2,1)} %copy-done, bf16[12,2,128,128]{3,2,1,0:T(8,128)(2,1)S(1)} %copy-done.8, f32[1024,512]{1,0:T(8,128)S(1)} %copy-done.3, ...), custom_call_target="tpu_custom_call" | custom-call | tf_op jit(solution)/shard_map/difference/pallas_call | solution.py:411
  112.6 1.3 copy-done.4
  114.0 10.7 %all-to-all-start.2 = ((bf16[64,4,8,512]{3,2,1,0:T(8,128)(2,1)}), bf16[64,4,8,512]{3,2,1,0:T(8,128)(2,1)S(1)}, u32[]{:S(2)}, u32[]{:S(2)}) async-start(bf16[64,4,8,512]{3,2,1,0:T(8,128)(2,1)} %bitcast.18), calls=%async_computation.2 | async-start | bytes 4194304 | tf_op jit(solution)/shard_map/all_to_all | solution.py:549
  124.7 0.6 fusion
  126.5 0.0 copy-done.5
  126.6 6.1 %cut_stamps.1 = bf16[16,8,128]{2,1,0:T(8,128)(2,1)S(1)} custom-call(bf16[1024,512]{1,0:T(8,128)(2,1)S(1)} %copy-done.5, s32[16]{0:T(128)S(1)} %copy-done.14, s32[16]{0:T(128)S(1)} %copy-done.17), custom_call_target="tpu_custom_call" | custom-call | flops 100000000 | bytes 3000000 | tf_op jit(solution)/shard_map/cut_stamps/pallas_call | solution.py:451
  132.7 0.6 copy.22
  133.3 0.5 slice_bitcast_fusion
  133.8 18.3 %all-to-all-done.2 = bf16[64,4,8,512]{3,2,1,0:T(8,128)(2,1)S(1)} async-done(((bf16[64,4,8,512]{3,2,1,0:T(8,128)(2,1)}), bf16[64,4,8,512]{3,2,1,0:T(8,128)(2,1)S(1)}, u32[]{:S(2)}, u32[]{:S(2)}) %all-to-all-start.2) | async-done | bytes 2097184 | tf_op jit(solution)/shard_map/all_to_all | solution.py:549
  152.1 3.1 %collective-permute-start.1 = (bf16[8,512]{1,0:T(8,128)(2,1)S(1)}, bf16[8,512]{1,0:T(8,128)(2,1)S(1)}, u32[]{:S(2)}, u32[]{:S(2)}) collective-permute-start(bf16[8,512]{1,0:T(8,128)(2,1)S(1)} %dynamic-slice_bitcast_fusion), channel_id=1, source_target_pairs={{0,1},{1,0},{2,3},{3,2},{4,5},{5,4},{6,7},{7,6},{8,9},{9,8},{10,11... | collective-permute-start | bytes 24584 | tf_op jit(solution)/shard_map/ppermute | solution.py:554
  155.2 2.1 %smooth.1.smoothed = bf16[1024,512]{1,0:T(8,128)(2,1)S(1)} custom-call(bf16[256,8,512]{2,1,0:T(8,128)(2,1)S(1)} %bitcast.17, s32[128]{0:T(128)S(1)} %get-tuple-element.27.pick, bf16[3,128,128]{2,1,0:T(8,128)(2,1)S(1)} %get-tuple-element.28.blocks.cblocks), custom_call_target="tpu_custom_call" | custom-call | flops 536870912 | bytes 3000000 | tf_op jit(solution)/shard_map/smooth/pallas_call | solution.py:481
  157.3 0.0 collective-permute-done.1.near
  157.3 2.0 %filter_rows.1 = f32[1024,512]{1,0:T(8,128)} custom-call(bf16[1024,512]{1,0:T(8,128)(2,1)S(1)} %smooth.1.smoothed, bf16[8,512]{1,0:T(8,128)(2,1)S(1)} %collective-permute-done.1.near, bf16[3,128,128]{2,1,0:T(8,128)(2,1)S(1)} %get-tuple-element.28.blocks.cblocks, bf16[2,128,128]{2,1,0:T(8,128)(2,1)S(1)} %copy-done.10), custom_call_target="tpu_custom_call" | custom-call | tf_op jit(solution)/shard_map/filter_rows/pallas_call | solution.py:509
  (30 shorter events, 0.1 us)
Async XLA Ops:
  0.6 1.2 copy-start.6
  1.9 0.7 copy-start.18
  2.5 0.7 copy-start.19
  5.3 1.4 copy-start.1
  6.8 11.5 %copy-start.26 = (bf16[12,21]{1,0:T(8,128)(2,1)S(1)}, bf16[12,21]{1,0:T(8,128)(2,1)}, u32[]{:S(2)}) copy-start(bf16[12,21]{1,0:T(8,128)(2,1)} %param.16) | copy-start | bytes 1516
  6.8 11.5 %copy-start.27 = (bf16[12,21]{1,0:T(8,128)(2,1)S(1)}, bf16[12,21]{1,0:T(8,128)(2,1)}, u32[]{:S(2)}) copy-start(bf16[12,21]{1,0:T(8,128)(2,1)} %param.15) | copy-start | bytes 1516
  6.8 12.5 %copy-start.28 = (bf16[15]{0:T(256)(128)(2,1)S(1)}, bf16[15]{0:T(256)(128)(2,1)}, u32[]{:S(2)}) copy-start(bf16[15]{0:T(256)(128)(2,1)} %param.22) | copy-start | bytes 94
  6.8 13.0 %copy-start.29 = (bf16[15]{0:T(256)(128)(2,1)S(1)}, bf16[15]{0:T(256)(128)(2,1)}, u32[]{:S(2)}) copy-start(bf16[15]{0:T(256)(128)(2,1)} %param.23) | copy-start | bytes 94
  6.8 44.8 %all-to-all-start = ((bf16[128,9,8,128]{3,2,1,0:T(8,128)(2,1)}), bf16[128,9,8,128]{3,2,1,0:T(8,128)(2,1)S(1)}, u32[]{:S(2)}, u32[]{:S(2)}) async-start(bf16[128,9,8,128]{3,2,1,0:T(8,128)(2,1)} %copy-done.1), calls=%async_computation | async-start | bytes 4718592 | tf_op jit(solution)/shard_map/all_to_all | solution.py:534
  51.6 4.2 %copy-start.2 = (f32[1024,512]{1,0:T(8,128)S(1)}, f32[1024,512]{1,0:T(8,128)}, u32[]{:S(2)}) copy-start(f32[1024,512]{1,0:T(8,128)} %science.3) | copy-start | bytes 6291460
  51.6 4.2 %copy-start.11 = (f32[12,21]{1,0:T(8,128)S(1)}, f32[12,21]{1,0:T(8,128)}, u32[]{:S(2)}) copy-start(f32[12,21]{1,0:T(8,128)} %get-tuple-element.36.kr) | copy-start | bytes 3028
  51.6 4.2 %copy-start.21 = (f32[15]{0:T(128)S(1)}, f32[15]{0:T(128)}, u32[]{:S(2)}) copy-start(f32[15]{0:T(128)} %convert_element_type.18.pr) | copy-start | bytes 184
  51.6 4.2 %copy-start.22 = (f32[15]{0:T(128)S(1)}, f32[15]{0:T(128)}, u32[]{:S(2)}) copy-start(f32[15]{0:T(128)} %convert_element_type.19.pc) | copy-start | bytes 184
  54.8 17.1 %collective-permute-start = (bf16[16,512]{1,0:T(8,128)(2,1)}, bf16[16,512]{1,0:T(8,128)(2,1)S(1)}, u32[]{:S(2)}, u32[]{:S(2)}) collective-permute-start(bf16[16,512]{1,0:T(8,128)(2,1)} %get-tuple-element.18), channel_id=1, source_target_pairs={{0,1},{1,0},{2,3},{3,2},{4,5},{5,4},{6,7},{7,6},{8,9},{9,8},{10,11... | collective-permute-start | bytes 49160 | tf_op jit(solution)/shard_map/ppermute | solution.py:540
  55.8 0.7 copy-start.12
  56.5 0.7 copy-start.15
  57.1 0.7 copy-start.20
  57.8 13.1 %copy-start.25 = (f32[21,12]{0,1:T(8,128)S(1)}, f32[21,12]{0,1:T(8,128)}, u32[]{:S(2)}) copy-start(f32[21,12]{0,1:T(8,128)} %get-tuple-element.37) | copy-start | bytes 3028
  57.8 14.1 %copy-start.13 = (s32[16]{0:T(128)S(1)}, s32[16]{0:T(128)}, u32[]{:S(2)}) copy-start(s32[16]{0:T(128)} %srow.5) | copy-start | bytes 196
  57.8 14.1 %copy-start.16 = (s32[16]{0:T(128)S(1)}, s32[16]{0:T(128)}, u32[]{:S(2)}) copy-start(s32[16]{0:T(128)} %scol.5) | copy-start | bytes 196
  68.4 0.9 copy-start.7
  69.3 0.6 copy-start.9
  69.9 1.0 copy-start.23
  78.7 18.9 %all-to-all-start.1 = ((f32[128,2,128]{2,1,0:T(2,128)}), f32[128,2,128]{2,1,0:T(2,128)S(1)}, u32[]{:S(2)}, u32[]{:S(2)}) async-start(f32[128,2,128]{2,1,0:T(2,128)} %stamp_sums.1), calls=%async_computation.1 | async-start | bytes 262144 | tf_op jit(solution)/shard_map/all_to_all | solution.py:544
  82.2 1.3 copy-start.24
  83.5 14.1 %copy-start.3 = (f32[1024,512]{1,0:T(8,128)S(1)}, f32[1024,512]{1,0:T(8,128)}, u32[]{:S(2)}) copy-start(f32[1024,512]{1,0:T(8,128)} %science.3) | copy-start | bytes 6291460
  92.9 4.7 %copy-start = (bf16[12,1056,512]{2,1,0:T(8,128)(2,1)}, bf16[12,1056,512]{2,1,0:T(8,128)(2,1)S(1)}, u32[]{:S(2)}) copy-start(bf16[12,1056,512]{2,1,0:T(8,128)(2,1)S(1)} %across.1) | copy-start | bytes 38928388
  97.6 1.1 copy-start.8
  112.6 1.3 copy-start.4
  114.0 12.6 %copy-start.5 = (bf16[1024,512]{1,0:T(8,128)(2,1)S(1)}, bf16[1024,512]{1,0:T(8,128)(2,1)}, u32[]{:S(2)}) copy-start(bf16[1024,512]{1,0:T(8,128)(2,1)} %get-tuple-element.13.diff) | copy-start | bytes 3145732
  114.0 12.6 %copy-start.14 = (s32[16]{0:T(128)S(1)}, s32[16]{0:T(128)}, u32[]{:S(2)}) copy-start(s32[16]{0:T(128)} %srow.5) | copy-start | bytes 196
  114.0 12.6 %copy-start.17 = (s32[16]{0:T(128)S(1)}, s32[16]{0:T(128)}, u32[]{:S(2)}) copy-start(s32[16]{0:T(128)} %scol.5) | copy-start | bytes 196
  114.0 38.1 %all-to-all-start.2 = ((bf16[64,4,8,512]{3,2,1,0:T(8,128)(2,1)}), bf16[64,4,8,512]{3,2,1,0:T(8,128)(2,1)S(1)}, u32[]{:S(2)}, u32[]{:S(2)}) async-start(bf16[64,4,8,512]{3,2,1,0:T(8,128)(2,1)} %bitcast.18), calls=%async_computation.2 | async-start | bytes 4194304 | tf_op jit(solution)/shard_map/all_to_all | solution.py:549
  126.6 30.7 %copy-start.10 = (bf16[2,128,128]{2,1,0:T(8,128)(2,1)S(1)}, bf16[2,128,128]{2,1,0:T(8,128)(2,1)}, u32[]{:S(2)}) copy-start(bf16[2,128,128]{2,1,0:T(8,128)(2,1)} %copy-done.9) | copy-start | bytes 196612
  152.1 5.2 %collective-permute-start.1 = (bf16[8,512]{1,0:T(8,128)(2,1)S(1)}, bf16[8,512]{1,0:T(8,128)(2,1)S(1)}, u32[]{:S(2)}, u32[]{:S(2)}) collective-permute-start(bf16[8,512]{1,0:T(8,128)(2,1)S(1)} %dynamic-slice_bitcast_fusion), channel_id=1, source_target_pairs={{0,1},{1,0},{2,3},{3,2},{4,5},{5,4},{6,7},{7,6},{8,9},{9,8},{10,11... | collective-permute-start | bytes 24584 | tf_op jit(solution)/shard_map/ppermute | solution.py:554

commit v2 on v1

--- a/solution.py
+++ b/solution.py
@@ -17,6 +17,7 @@
 SPAN = 256
 WIN = 56
 LANES = BASIS * 32
+LARGE = 58
 BOTH = ("ccd", "strip")
 SWAP = [(0, 1), (1, 0)]
 F32 = jnp.float32
@@ -31,6 +32,10 @@
     return pl.BlockSpec(memory_space=pltpu.VMEM)
 
 
+def hbm():
+    return pl.BlockSpec(memory_space=pltpu.HBM)
+
+
 def smem():
     return pl.BlockSpec(memory_space=pltpu.SMEM)
 
@@ -51,8 +56,18 @@
     return pl.CostEstimate(flops=flops, bytes_accessed=moved, transcendentals=0)
 
 
-def pack_body(dest, row, pieces, out, count, rows):
+CHUNKS = 8
+
+
+def pack_body(dest_in, row_in, pieces_in, sent, dest, row, pieces, out, count, rows, sems):
     devices = out.shape[0]
+    loads = [
+        pltpu.make_async_copy(src, dst, sems.at[CHUNKS + i])
+        for i, (src, dst) in enumerate([(dest_in, dest), (row_in, row), (pieces_in, pieces)])
+    ]
+    for load in loads:
+        load.start()
+    out[...] = jnp.zeros(out.shape, out.dtype)
 
     def clear(d, c):
         count[d] = 0
@@ -61,7 +76,8 @@
         return c
 
     lax.fori_loop(0, devices, clear, 0, unroll=8)
-    out[...] = jnp.zeros(out.shape, out.dtype)
+    for load in loads:
+        load.wait()
 
     def place(i, c):
         d = dest[i]
@@ -82,17 +98,34 @@
         out[d, 8] = told.astype(F32).astype(BF16)
         return c
 
-    lax.fori_loop(0, devices, tell, 0, unroll=8)
+    part = devices // CHUNKS
+    sends = []
+    for i in range(CHUNKS):
+        lax.fori_loop(i * part, (i + 1) * part, tell, 0, unroll=8)
+        some = pl.ds(i * part, part)
+        sends.append(pltpu.make_async_copy(out.at[some], sent.at[some], sems.at[i]))
+        sends[-1].start()
+    for send in sends:
+        send.wait()
 
 
 def pack(route_dest, route_row, template, devices):
+    pieces = template.shape[0]
     return pl.pallas_call(
         pack_body,
         out_shape=shape((devices, 9, 8, 128), BF16),
-        in_specs=[smem(), smem(), vmem()],
-        out_specs=vmem(),
-        scratch_shapes=[pltpu.SMEM((devices,), I32), pltpu.SMEM((2 * devices,), I32)],
-        compiler_params=params(32),
+        in_specs=[hbm()] * 3,
+        out_specs=hbm(),
+        scratch_shapes=[
+            pltpu.SMEM((pieces,), I32),
+            pltpu.SMEM((pieces,), I32),
+            pltpu.VMEM(template.shape, BF16),
+            pltpu.VMEM((devices, 9, 8, 128), BF16),
+            pltpu.SMEM((devices,), I32),
+            pltpu.SMEM((2 * devices,), I32),
+            pltpu.SemaphoreType.DMA((CHUNKS + 3,)),
+        ],
+        compiler_params=params(LARGE),
         name="pack",
     )(route_dest, route_row, template)
 
@@ -116,8 +149,9 @@
 
 
 def tables_body(
-    kr, kc, pr, pc, kcl, shift, srow, scol, science,
-    cols_out, rows_out, pcols_out, prows_out, stamp_out, slot_out, pick_out, sky_out, count,
+    kr, kc, pr, pc, kcl, krl, shift, srow, scol, science,
+    cols_out, rows_out, pcols_out, prows_out, stamp_out, krl_out, seam_out,
+    slot_out, pick_out, sky_out, count,
 ):
     for b in range(BASIS):
         for k in range(3):
@@ -127,7 +161,11 @@
             table = jnp.zeros((128, 128), F32)
             for t in range(KTAPS):
                 table = jnp.where(lag == t, kr[b, t], table)
-            rows_out[b, k] = table.astype(BF16)
+            table = table.astype(BF16)
+            rows_out[b, :128, 128 * k : 128 * k + 128] = table
+            if k == 0:
+                rows_out[b, 128:, 128:] = table[: STEP - 128]
+                rows_out[b, 128:, :128] = jnp.zeros((STEP - 128, 128), BF16)
     for k in range(3):
         pcols_out[k] = band_table(lambda t: pc[t], PSF_TAPS, 128, 7 + 128 * (k - 1))
     for k in range(2):
@@ -141,6 +179,18 @@
     for t in range(KTAPS):
         table = jnp.where(lag == t, kcl[t : t + 1, :], table)
     stamp_out[...] = table.astype(BF16)
+    krl_out[...] = krl[...]
+    seam_out[...] = jnp.zeros(seam_out.shape, BF16)
+    place = ((iota((32, 128), 1) + 16) & 31) - 16
+    source = iota((32, 128), 0) - 16
+    crosses = (place >= -10) & (place < 10) & ((place < 0) != (source < 0))
+    lag = jnp.where(crosses, source - place + 10, -1)
+    for v in range(3):
+        taps = pltpu.roll(kcl[:, 128 * v : 128 * v + 128], 112, 1)
+        table = jnp.zeros((32, 128), F32)
+        for t in range(KTAPS):
+            table = jnp.where(lag == t, taps[t : t + 1, :], table)
+        seam_out[112:144, 128 * v : 128 * v + 128] = table.astype(BF16)
 
     own, ccds = lax.axis_index("ccd"), lax.axis_size("ccd")
     cap = slot_out.shape[0] * 2 // ccds
@@ -173,32 +223,35 @@
 
 def tables(kern_row, kern_col, psf_row, psf_col, band_shift, stamp_row, stamp_col, science):
     kc = kern_col.astype(F32)
-    lanes = jnp.pad(jnp.repeat(kc.T, 32, axis=1), ((0, 3), (0, 0)))
+    expand = lambda taps: jnp.pad(jnp.repeat(taps.T, 32, axis=1), ((0, 3), (0, 0)))
     return pl.pallas_call(
         tables_body,
         out_shape=(
             shape((BASIS, 3, 128, 128), BF16),
-            shape((BASIS, 2, 128, 128), BF16),
+            shape((BASIS, STEP, SPAN), BF16),
             shape((3, 128, 128), BF16),
             shape((2, 128, 128), BF16),
             shape((128, LANES), BF16),
+            shape((24, LANES), F32),
+            shape((256, LANES), BF16),
             shape(band_shift.shape, I32),
             shape(band_shift.shape, I32),
             shape((STAMPS, 32, 128), F32),
         ),
-        in_specs=[smem()] * 4 + [vmem()] + [smem()] * 3 + [vmem()],
-        out_specs=(vmem(),) * 5 + (smem(),) * 2 + (vmem(),),
+        in_specs=[smem()] * 4 + [vmem()] * 2 + [smem()] * 3 + [vmem()],
+        out_specs=(vmem(),) * 7 + (smem(),) * 2 + (vmem(),),
         scratch_shapes=[pltpu.SMEM((64,), I32)],
-        compiler_params=params(32),
+        compiler_params=params(16),
         cost_estimate=cost(2 * 10**9, 4 * 10**6),
         name="tables",
     )(
-        kern_row.astype(F32), kc, psf_row.astype(F32), psf_col.astype(F32), lanes,
+        kern_row.astype(F32), kc, psf_row.astype(F32), psf_col.astype(F32),
+        expand(kc), expand(kern_row.astype(F32)),
         band_shift, stamp_row, stamp_col, science,
     )
 
 
-def coadd_body(arrived, out, edge, held):
+def coadd_body(arrived, ready, out, edge, held):
     senders = arrived.shape[0]
     half = senders * 8
     told = arrived[:, 8].astype(F32).reshape(half, 128).T
@@ -224,17 +277,17 @@
         edge[...] = out[:PAD]
 
 
-def coadd(arrived):
+def coadd(arrived, ready):
     senders = arrived.shape[0]
     return pl.pallas_call(
         coadd_body,
         out_shape=(shape((ROWS, COLS), BF16), shape((PAD, COLS), BF16)),
-        in_specs=[vmem()],
+        in_specs=[vmem(), pl.BlockSpec(memory_space=pl.ANY)],
         out_specs=(vmem(), vmem()),
         scratch_shapes=[pltpu.VMEM((senders * 16, COLS), BF16)],
-        compiler_params=params(40),
+        compiler_params=params(16),
         name="coadd",
-    )(arrived)
+    )(arrived, ready)
 
 
 def frame(framed, image, near):
@@ -280,14 +333,24 @@
     )
     same = (iota((LANES, LANES), 0) & 31) == (iota((LANES, LANES), 1) & 31)
     pairs = jnp.where(same, pairs, 0.0)
-    left = ((iota((16, LANES), 1) >> 5) == iota((16, LANES), 0)).astype(F32)
-    right = ((iota((LANES, 128), 0) >> 5) == (iota((LANES, 128), 1) & 15)).astype(F32)
-    gram = jnp.dot(jnp.dot(left, pairs, precision=HIGH, preferred_element_type=F32), right,
-                   precision=HIGH, preferred_element_type=F32)
-    goal = jnp.sum(left * total, axis=1, keepdims=True)
+    gram = [jnp.sum(pairs[32 * b : 32 * b + 32], axis=0, keepdims=True) for b in range(BASIS)]
+    gram = jnp.concatenate(gram + [total, jnp.zeros((3, LANES), F32)], axis=0)
+    parts = []
+    for q in range(3):
+        part = gram[:, 128 * q : 128 * q + 128]
+        for turn in (1, 2, 4, 8, 16):
+            part = part + pltpu.roll(part, 128 - turn, 1)
+        parts.append(part)
     row, col = iota((16, 128), 0), iota((16, 128), 1)
-    both = jnp.where((col & 15) == BASIS, goal, gram)
-    both = jnp.where((col >> 4) == (row & 7), both, 0.0) / (sigma[0] * sigma[0])
+    both = jnp.zeros((16, 128), F32)
+    goal = jnp.zeros((16, 1), F32)
+    for b in range(BASIS):
+        entry = parts[b // 4][:, 32 * (b & 3) : 32 * (b & 3) + 1]
+        both = jnp.where((col & 15) == b, entry, both)
+        goal = jnp.where(row[:, :1] == b, entry[BASIS : BASIS + 1], goal)
+    both = jnp.where((col & 15) == BASIS, goal, both)
+    both = jnp.where(((col >> 4) == (row & 7)) & (row < BASIS), both, 0.0)
+    both = both / (sigma[0] * sigma[0])
     packed = jnp.concatenate(
         [jnp.sum(both[:8], axis=0, keepdims=True), jnp.sum(both[8:], axis=0, keepdims=True)], axis=0
     )
@@ -306,7 +369,7 @@
             pltpu.VMEM((STAMPS, WIN, LANES), F32),
             pltpu.VMEM((STAMPS * 32, LANES), BF16),
         ],
-        compiler_params=params(40),
+        compiler_params=params(16),
         name="stamp_sums",
     )(image, near, sigma, srow, scol, table, krl, sky)
 
@@ -320,34 +383,71 @@
                 wide[128 * i : 128 * i + 128, 128 * o : 128 * o + 128] = jnp.zeros((128, 128), BF16)
 
 
-def across_body(image, near, blocks, out, framed, wide):
-    @pl.when(pl.program_id(0) == 0)
-    def _():
-        frame(framed, image, near)
-
-    fill_cols(wide, blocks[0])
+def across_body(image, near, blocks, seam, out, framed, wide, border, held, sems):
+    frame(framed, image, near)
     for m in range(0, FRAMED, 352):
-        out[0, m : m + 352] = jnp.dot(
-            framed[m : m + 352], wide[...], preferred_element_type=F32
-        ).astype(BF16)
-
-
-def across_all(image, near, blocks):
+        for v in range(3):
+            border[v, m : m + 352] = jnp.dot(
+                framed[m : m + 352, 128:384],
+                seam[:, 128 * v : 128 * v + 128],
+                preferred_element_type=F32,
+            )
+    lane = iota((352, 128), 1)
+
+    def save(b, g):
+        return pltpu.make_async_copy(held.at[g], out.at[b], sems.at[g])
+
+    def four(v, c):
+        for g in range(4):
+            b = 4 * v + g
+            for i in range(2):
+                for o in range(2):
+                    wide[128 * i : 128 * i + 128, 128 * o : 128 * o + 128] = blocks[b, i - o + 1]
+
+            @pl.when(v > 0)
+            def _():
+                save(b - 4, g).wait()
+
+            for m in range(0, FRAMED, 352):
+                rows = slice(m, m + 352)
+                left = jnp.dot(framed[rows, :256], wide[...], preferred_element_type=F32)
+                right = jnp.dot(framed[rows, 256:], wide[...], preferred_element_type=F32)
+                extra = border[v, rows]
+                if g:
+                    extra = pltpu.roll(extra, 128 - 32 * g, 1)
+                held[g, rows, :128] = left[:, :128].astype(BF16)
+                held[g, rows, 128:256] = (
+                    left[:, 128:] + jnp.where(lane >= 118, extra, 0.0)
+                ).astype(BF16)
+                held[g, rows, 256:384] = (
+                    right[:, :128] + jnp.where(lane < 10, extra, 0.0)
+                ).astype(BF16)
+                held[g, rows, 384:] = right[:, 128:].astype(BF16)
+            save(b, g).start()
+        return c
+
+    lax.fori_loop(0, BASIS // 4, four, 0)
+    for g in range(4):
+        save(BASIS - 4 + g, g).wait()
+
+
+def across_all(image, near, blocks, seam):
     return pl.pallas_call(
         across_body,
-        grid=(BASIS,),
         out_shape=shape((BASIS, FRAMED, COLS), BF16),
-        in_specs=[
-            pl.BlockSpec((ROWS, COLS), lambda b: (0, 0)),
-            pl.BlockSpec((PAD, COLS), lambda b: (0, 0)),
-            pl.BlockSpec((1, 3, 128, 128), lambda b: (b, 0, 0, 0)),
+        in_specs=[vmem()] * 4,
+        out_specs=hbm(),
+        scratch_shapes=[
+            pltpu.VMEM((FRAMED, COLS), BF16),
+            pltpu.VMEM((256, 256), BF16),
+            pltpu.VMEM((3, FRAMED, 128), F32),
+            pltpu.VMEM((4, FRAMED, COLS), BF16),
+            pltpu.SemaphoreType.DMA((4,)),
         ],
-        out_specs=pl.BlockSpec((1, FRAMED, COLS), lambda b: (b, 0, 0)),
-        scratch_shapes=[pltpu.VMEM((FRAMED, COLS), BF16), pltpu.VMEM((COLS, COLS), BF16)],
-        compiler_params=params(32),
-        cost_estimate=cost(2 * BASIS * FRAMED * COLS * COLS, 16 * 10**6),
+        compiler_params=params(54),
+        cost_estimate=cost(BASIS * FRAMED * COLS * COLS, 16 * 10**6),
         name="across",
-    )(image, near, blocks)
+    )(image, near, blocks, seam)
 
 
 def solve(sums):
@@ -363,76 +463,92 @@
     return both[:, BASIS : BASIS + 1]
 
 
-def fill_rows(table, blocks):
-    table[:128, :128] = blocks[0]
-    table[:128, 128:] = blocks[1]
-    table[128:, :128] = jnp.zeros((STEP - 128, 128), BF16)
-    table[128:, 128:] = blocks[0][: STEP - 128]
-
-
 def difference_body(
-    sums, across, blocks, science, sigma, slot, coef_out, diff_out, leave_out, model, coef, table
+    sums, across_in, table_in, science_in, sigma, slot, coef_out, diff_out, leave_out,
+    across, table, science, coef, bands, sems, save_sems,
 ):
-    b = pl.program_id(0)
-
-    @pl.when(b == 0)
-    def _():
-        found = solve(sums)
-        coef[...] = jnp.broadcast_to(found, coef.shape)
-        eye = iota((16, 128), 0) == iota((16, 128), 1)
-        coef_out[...] = jnp.sum(jnp.where(eye, found, 0.0), axis=0, keepdims=True)
-        model[...] = jnp.zeros(model.shape, F32)
-
-    fill_rows(table, blocks[0])
-    weight = coef[pl.ds(b, 1), :]
-    for first, rows, span in BLOCKS:
-        basis = jnp.dot(
-            table[:rows, :span], across[0, first : first + span], preferred_element_type=F32
+    def load(i):
+        first, _, span = BLOCKS[i]
+        return pltpu.make_async_copy(
+            across_in.at[:, pl.ds(first, span), :],
+            across.at[i & 1, :, pl.ds(0, span), :],
+            sems.at[i & 1],
         )
-        model[first : first + rows] += weight * basis.astype(BF16).astype(F32)
-
-    @pl.when(b == BASIS - 1)
-    def _():
-        scale = 1.0 / sigma[0]
-
-        def finish(m, c):
-            rows = pl.ds(pl.multiple_of(m * 16, 16), 16)
-            left = (science[rows] - model[rows]) * scale
-            diff_out[rows] = left.astype(BF16)
-            leave_out[slot[2 * m]] = left[:8].astype(BF16)
-            leave_out[slot[2 * m + 1]] = left[8:].astype(BF16)
+
+    load(0).start()
+    table_load = pltpu.make_async_copy(table_in, table, sems.at[2])
+    table_load.start()
+    science_load = pltpu.make_async_copy(science_in, science, sems.at[3])
+    science_load.start()
+    found = solve(sums)
+    coef[...] = jnp.broadcast_to(found, coef.shape)
+    eye = iota((16, 128), 0) == iota((16, 128), 1)
+    coef_out[...] = jnp.sum(jnp.where(eye, found, 0.0), axis=0, keepdims=True)
+    scale = 1.0 / sigma[0]
+    saves = []
+    table_load.wait()
+    for i, (first, rows, span) in enumerate(BLOCKS):
+        load(i).wait()
+        if i + 1 < len(BLOCKS):
+            load(i + 1).start()
+        for h in range(0, COLS, 256):
+            model = None
+            for b in range(BASIS):
+                basis = jnp.dot(
+                    table[b, :rows, :span],
+                    across[i & 1, b, :span, h : h + 256],
+                    preferred_element_type=F32,
+                )
+                term = coef[b : b + 1, :] * basis.astype(BF16).astype(F32)
+                model = term if model is None else model + term
+            if i == 0 and h == 0:
+                science_load.wait()
+            left = (science[first : first + rows, h : h + 256] - model) * scale
+            bands[first // 8 : (first + rows) // 8, :, h : h + 256] = left.reshape(
+                rows // 8, 8, 256
+            ).astype(BF16)
+
+        def send(band, c):
+            pltpu.make_async_copy(
+                bands.at[band], leave_out.at[slot[band]], save_sems.at[0]
+            ).start()
             return c
 
-        lax.fori_loop(0, ROWS // 16, finish, 0, unroll=4)
-
-
-def difference_all(sums, across, blocks, science, sigma, slot, slots):
-    whole = lambda *dims: pl.BlockSpec(dims, lambda b: (0,) * len(dims))
+        lax.fori_loop(first // 8, (first + rows) // 8, send, 0, unroll=4)
+        some = pl.ds(first // 8, rows // 8)
+        saves.append(pltpu.make_async_copy(bands.at[some], diff_out.at[some], save_sems.at[1 + i]))
+        saves[-1].start()
+    for save in saves:
+        save.wait()
+    pltpu.make_async_copy(bands, leave_out.at[pl.ds(0, ROWS // 8)], save_sems.at[0]).wait()
+
+
+def difference_all(sums, across, table, science, sigma, slot, slots):
     return pl.pallas_call(
         difference_body,
-        grid=(BASIS,),
-        out_shape=(shape((1, 128), F32), shape((ROWS, COLS), BF16), shape((slots, 8, COLS), BF16)),
-        in_specs=[
-            whole(*sums.shape),
-            pl.BlockSpec((1, FRAMED, COLS), lambda b: (b, 0, 0)),
-            pl.BlockSpec((1, 2, 128, 128), lambda b: (b, 0, 0, 0)),
-            whole(ROWS, COLS),
-            smem(),
-            smem(),
+        out_shape=(
+            shape((1, 128), F32),
+            shape((ROWS // 8, 8, COLS), BF16),
+            shape((slots, 8, COLS), BF16),
+        ),
+        in_specs=[vmem()] + [hbm()] * 3 + [smem()] * 2,
+        out_specs=(vmem(), hbm(), hbm()),
+        scratch_shapes=[
+            pltpu.VMEM((2, BASIS, SPAN, COLS), BF16),
+            pltpu.VMEM((BASIS, STEP, SPAN), BF16),
+            pltpu.VMEM((ROWS, COLS), F32),
+            pltpu.VMEM((16, 256), F32),
+            pltpu.VMEM((ROWS // 8, 8, COLS), BF16),
+            pltpu.SemaphoreType.DMA((4,)),
+            pltpu.SemaphoreType.DMA((1 + len(BLOCKS),)),
         ],
-        out_specs=(whole(1, 128), whole(ROWS, COLS), whole(slots, 8, COLS)),
-        scratch_shapes=[
-            pltpu.VMEM((ROWS, COLS), F32),
-            pltpu.VMEM((16, COLS), F32),
-            pltpu.VMEM((STEP, SPAN), BF16),
-        ],
-        compiler_params=params(40),
+        compiler_params=params(54),
         name="difference",
-    )(sums, across, blocks, science, sigma, slot)
+    )(sums, across, table, science, sigma, slot)
 
 
 def cut_body(diff, srow, scol, out, wide):
-    wide[...] = diff[...].astype(F32)
+    wide[...] = diff[...].astype(F32).reshape(ROWS, COLS)
     row, lane = iota((32, 128), 0), iota((32, 128), 1)
     pick = (iota((8, 32), 1) >> 2 == iota((8, 32), 0)).astype(BF16)
 
@@ -454,7 +570,7 @@
         in_specs=[vmem(), smem(), smem()],
         out_specs=vmem(),
         scratch_shapes=[pltpu.VMEM((ROWS, COLS), F32)],
-        compiler_params=params(32),
+        compiler_params=params(16),
         cost_estimate=cost(10**8, 3 * 10**6),
         name="cut_stamps",
     )(diff, srow, scol)
@@ -484,10 +600,17 @@
         in_specs=[vmem(), smem(), vmem()],
         out_specs=vmem(),
         scratch_shapes=[pltpu.VMEM((ROWS, COLS), BF16), pltpu.VMEM((COLS, COLS), BF16)],
-        compiler_params=params(32),
+        compiler_params=params(16),
         cost_estimate=cost(2 * ROWS * COLS * COLS, 3 * 10**6),
         name="smooth",
     )(landed, pick, blocks)
+
+
+def fill_rows(table, blocks):
+    table[:128, :128] = blocks[0]
+    table[:128, 128:] = blocks[1]
+    table[128:, :128] = jnp.zeros((STEP - 128, 128), BF16)
+    table[128:, 128:] = blocks[0][: STEP - 128]
 
 
 def filter_body(smoothed, near, cblocks, rblocks, out, framed, wide, table, tail):
@@ -517,7 +640,7 @@
             pltpu.VMEM((STEP, SPAN), BF16),
             pltpu.VMEM((PAD, COLS), BF16),
         ],
-        compiler_params=params(32),
+        compiler_params=params(16),
         name="filter_rows",
     )(smoothed, near, cblocks, rblocks)
 
@@ -532,17 +655,16 @@
     cap = 2 * bands // ccds
     outgoing = pack(route_dest, route_row, template, devices)
     arrived = lax.all_to_all(outgoing, BOTH, split_axis=0, concat_axis=0, tiled=True)
-    cols, rows, pcols, prows, stamp_table, slot, pick, sky = tables(
+    cols, rows, pcols, prows, stamp_table, krl, seam, slot, pick, sky = tables(
         kern_row, kern_col, psf_row, psf_col, band_shift, stamp_row, stamp_col, science
     )
-    krl = jnp.pad(jnp.repeat(kern_row.astype(F32).T, 32, axis=1), ((0, 3), (0, 0)))
-    image, edge = coadd(arrived)
+    image, edge = coadd(arrived, stamp_table)
     near = lax.ppermute(edge, "strip", SWAP)
     sums = stamp_sums(
         image, near, noise_sigma, stamp_row, stamp_col, stamp_table, krl, sky, devices
     )
     sums = lax.all_to_all(sums, BOTH, split_axis=0, concat_axis=0, tiled=True)
-    across = across_all(image, near, cols)
+    across = across_all(image, near, cols, seam)
     coef, diff, leaving = difference_all(
         sums, across, rows, science, noise_sigma, slot, ccds * cap
     )
@@ -556,7 +678,7 @@
     )
     smoothed = smooth(landed, pick, pcols)
     filtered = filter_rows(smoothed, beside, pcols, prows)
-    return (diff, stamp_cut, coef[0, :BASIS], filtered)
+    return (diff.reshape(ROWS, COLS), stamp_cut, coef[0, :BASIS], filtered)
 
 
 def solution(mesh):

time: 160 us -> 135 us (0.84)
  waiting for transfers between devices: 49.6 us -> 34.4 us
  local copies, waits for them, and re-layouts: 19.2 us -> 10.8 us
  other arithmetic: 1.63 us -> 0.01 us
    all_to_all x1, waiting for transfers between devices: 31.3 us -> 14.8 us  [shards(): lax.all_to_all(outgoing, BOTH, split_axis=0, concat_axis=0, tiled=True)]
    unnamed x61 -> x49, local copies, waits for them, and re-layouts: 17.5 us -> 9.11 us
  transfers between devices with their start and end apart: 5 -> 5, of which waited for: 2 -> 4; matrix products, arithmetic and copies ran while one was open for 2% -> 2% of each run, Pallas kernels for 18% -> 21%
where the time goes in v2:
time: 135 us; the launch traced here: 134 us
  Pallas kernels  56.6 us (42%)
  waiting for transfers between devices  34.4 us (25%)
  starting transfers between devices  29.2 us (22%)
  local copies, waits for them, and re-layouts  10.8 us (8%)
  between operations  2.95 us (2%)
    all_to_all x1, waiting for transfers between devices, shards(): lax.all_to_all(leaving.reshape(ccds, cap, 8, COLS), 'ccd', split_axis=0,...  18.3 us
    all_to_all x1, waiting for transfers between devices, shards(): lax.all_to_all(outgoing, BOTH, split_axis=0, concat_axis=0, tiled=True)  14.8 us
    pallas_call x1, Pallas kernels, difference_all(): pl.pallas_call(difference_body, out_shape=(shape((1, 128), F32), shape((R...  13.3 us
    all_to_all x1, starting transfers between devices, shards(): lax.all_to_all(outgoing, BOTH, split_axis=0, concat_axis=0, tiled=True)  11.5 us
    pallas_call x1, Pallas kernels, tables(): pl.pallas_call(tables_body, out_shape=(shape((BASIS, 3, 128, 128), BF16),...  10.9 us
    all_to_all x1, starting transfers between devices, shards(): lax.all_to_all(leaving.reshape(ccds, cap, 8, COLS), 'ccd', split_axis=0,...  9.73 us
    unnamed x49, local copies, waits for them, and re-layouts  9.11 us
    pallas_call x1, Pallas kernels, across_all(): pl.pallas_call(across_body, out_shape=shape((BASIS, FRAMED, COLS), BF16),...  8.92 us
  transfers between devices with their start and end apart: 5, of which 4 were waited for; matrix products, arithmetic and copies ran while one was open for 2% of the time, Pallas kernels for 21%

profile of v2, /device:TPU:1, one launch (start us, length us, event | category | flops | bytes accessed | tf_op | source)
XLA Modules:
  0.0 134.0 jit_solution(15468347495562464875)
XLA Ops:
  0.6 3.5 %pack.1 = bf16[128,9,8,128]{3,2,1,0:T(8,128)(2,1)} custom-call(s32[128]{0:T(128)} %dest_in.1, s32[128]{0:T(128)} %row_in.1, bf16[128,8,512]{2,1,0:T(8,128)(2,1)} %pieces_in.1), custom_call_target="tpu_custom_call" | custom-call | tf_op jit(solution)/shard_map/pack/pallas_call | solution.py:114
  4.1 0.0 copy-start.21
  4.1 0.0 copy-start.22
  4.1 0.0 copy-start.19
  4.2 0.0 copy-start.20
  4.2 0.0 copy-start.14
  4.2 0.0 copy-start.15
  4.2 0.0 copy-start.17
  4.2 11.5 %all-to-all-start = ((bf16[128,9,8,128]{3,2,1,0:T(8,128)(2,1)}), bf16[128,9,8,128]{3,2,1,0:T(8,128)(2,1)S(1)}, u32[]{:S(2)}, u32[]{:S(2)}) async-start(bf16[128,9,8,128]{3,2,1,0:T(8,128)(2,1)} %pack.1), calls=%async_computation | async-start | bytes 4718592 | tf_op jit(solution)/shard_map/all_to_all | solution.py:657
  15.7 0.0 copy-done.21
  15.7 0.0 copy-done.22
  15.8 0.0 copy-done.19
  15.8 0.0 copy-done.20
  15.8 0.1 copy.18
  15.9 0.1 broadcast_in_dim.6
  16.0 0.1 reshape.26
  16.1 0.1 copy.19
  16.2 0.1 broadcast_in_dim.7
  16.3 0.1 reshape.27
  16.4 0.0 copy-done.14
  16.5 0.0 copy-done.15
  16.5 0.0 copy-done.17
  16.5 0.0 copy-start.1
  16.5 1.6 %copy-done.1 = f32[1024,512]{1,0:T(8,128)S(1)} copy-done((f32[1024,512]{1,0:T(8,128)S(1)}, f32[1024,512]{1,0:T(8,128)}, u32[]{:S(2)}) %copy-start.1) | copy-done | bytes 2097176
  18.1 10.9 %tables.1 = (bf16[12,3,128,128]{3,2,1,0:T(8,128)(2,1)S(1)}, bf16[12,224,256]{2,1,0:T(8,128)(2,1)S(1)}, bf16[3,128,128]{2,1,0:T(8,128)(2,1)S(1)}, bf16[2,128,128]...) custom-call(f32[12,21]{1,0:T(8,128)S(1)} %get-tuple-element.40.kr, ...), custom_call_target="tpu_custom_call" | custom-call | flops 2000000000 | bytes 4000000 | tf_op jit(solution)/shard_map/tables/pallas_call | solution.py:227
  28.9 0.0 copy-start.2
  28.9 1.1 copy-done.2
  30.0 1.0 copy-done.3
  31.0 0.6 copy-done.5
  31.7 0.7 copy-done.8
  32.4 0.7 copy-done.10
  33.1 0.6 copy-done.12
  33.7 0.5 copy-done.16
  34.2 14.8 %all-to-all-done.arrived = bf16[128,9,8,128]{3,2,1,0:T(8,128)(2,1)S(1)} async-done(((bf16[128,9,8,128]{3,2,1,0:T(8,128)(2,1)}), bf16[128,9,8,128]{3,2,1,0:T(8,128)(2,1)S(1)}, u32[]{:S(2)}, u32[]{:S(2)}) %all-to-all-start) | async-done | bytes 2359328 | tf_op jit(solution)/shard_map/all_to_all | solution.py:657
  49.0 0.9 copy-done.6
  49.9 2.6 %coadd.1 = (bf16[1024,512]{1,0:T(8,128)(2,1)S(1)}, bf16[16,512]{1,0:T(8,128)(2,1)S(1)}) custom-call(bf16[128,9,8,128]{3,2,1,0:T(8,128)(2,1)S(1)} %all-to-all-done.arrived, bf16[128,384]{1,0:T(8,128)(2,1)S(1)} %copy-done.6), custom_call_target="tpu_custom_call" | custom-call | tf_op jit(solution)/shard_map/coadd/pallas_call | solution.py:282
  52.5 0.0 copy-start
  52.5 1.1 collective-permute-start
  54.3 0.2 collective-permute-done.near
  54.5 0.0 copy-done.7
  54.5 0.0 copy-done.9
  54.5 7.2 %stamp_sums.1 = f32[128,2,128]{2,1,0:T(2,128)} custom-call(bf16[1024,512]{1,0:T(8,128)(2,1)S(1)} %get-tuple-element.20.image, bf16[16,512]{1,0:T(8,128)(2,1)S(1)} %collective-permute-done.near, f32[1]{0:T(128)S(6)} %copy.23.sigma, s32[16]{0:T(128)S(1)} %copy-done.14, s32[16]{0:T(128)S(1)} %copy-done.15, bf16[128,384]{1,0:T(8,128)(2,1)S(1)} %copy-done.7, ...), custom_call_target="tpu_custom_call" | custom-call | tf_op jit(solution)/shard_map/stamp_sums/pallas_call | solution.py:361
  61.7 3.7 %all-to-all-start.1 = ((f32[128,2,128]{2,1,0:T(2,128)}), f32[128,2,128]{2,1,0:T(2,128)S(1)}, u32[]{:S(2)}, u32[]{:S(2)}) async-start(f32[128,2,128]{2,1,0:T(2,128)} %stamp_sums.1), calls=%async_computation.1 | async-start | bytes 262144 | tf_op jit(solution)/shard_map/all_to_all | solution.py:666
  65.5 0.0 copy-done
  65.5 0.0 copy-done.11
  65.5 8.9 %across.1.across_in = bf16[12,1056,512]{2,1,0:T(8,128)(2,1)} custom-call(bf16[1024,512]{1,0:T(8,128)(2,1)} %copy-done, bf16[16,512]{1,0:T(8,128)(2,1)} %copy-done.11, bf16[12,3,128,128]{3,2,1,0:T(8,128)(2,1)} %copy-done.3, bf16[256,384]{1,0:T(8,128)(2,1)} %copy-done.10), custom_call_target="tpu_custom_call" | custom-call | flops 3321888768 | bytes 16000000 | tf_op jit(solution)/shard_map/across/pallas_call | solution.py:435
  74.4 1.1 all-to-all-done.1.sums
  75.6 0.7 copy-done.18
  76.2 13.3 %difference.1 = (f32[1,128]{1,0:T(1,128)}, bf16[128,8,512]{2,1,0:T(8,128)(2,1)}, bf16[256,8,512]{2,1,0:T(8,128)(2,1)}) custom-call(f32[128,2,128]{2,1,0:T(2,128)} %copy-done.18, bf16[12,1056,512]{2,1,0:T(8,128)(2,1)} %across.1.across_in, bf16[12,224,256]{2,1,0:T(8,128)(2,1)} %copy-done.2, f32[1024,512]{1,0:T(8,128)} %science_in.1, f32[1]{0:T(128)S(6)} %copy.23.sigma, ...), custom_call_target="tpu_custom_call" | custom-call | tf_op jit(solution)/shard_map/difference/pallas_call | solution.py:527
  89.5 0.0 copy-start.4
  89.5 0.0 copy-start.23
  89.6 9.7 %all-to-all-start.2 = ((bf16[64,4,8,512]{3,2,1,0:T(8,128)(2,1)}), bf16[64,4,8,512]{3,2,1,0:T(8,128)(2,1)S(1)}, u32[]{:S(2)}, u32[]{:S(2)}) async-start(bf16[64,4,8,512]{3,2,1,0:T(8,128)(2,1)} %bitcast.21), calls=%async_computation.2 | async-start | bytes 4194304 | tf_op jit(solution)/shard_map/all_to_all | solution.py:671
  99.3 0.6 fusion
  101.2 0.0 copy-done.4
  101.2 0.0 copy-start.13
  101.2 6.1 %cut_stamps.1 = bf16[16,8,128]{2,1,0:T(8,128)(2,1)S(1)} custom-call(bf16[128,8,512]{2,1,0:T(8,128)(2,1)S(1)} %copy-done.4, s32[16]{0:T(128)S(1)} %copy-done.14, s32[16]{0:T(128)S(1)} %copy-done.15), custom_call_target="tpu_custom_call" | custom-call | flops 100000000 | bytes 3000000 | tf_op jit(solution)/shard_map/cut_stamps/pallas_call | solution.py:567
  107.3 0.6 copy.22
  107.9 0.5 slice_bitcast_fusion
  108.4 18.3 %all-to-all-done.2 = bf16[64,4,8,512]{3,2,1,0:T(8,128)(2,1)S(1)} async-done(((bf16[64,4,8,512]{3,2,1,0:T(8,128)(2,1)}), bf16[64,4,8,512]{3,2,1,0:T(8,128)(2,1)S(1)}, u32[]{:S(2)}, u32[]{:S(2)}) %all-to-all-start.2) | async-done | bytes 2097184 | tf_op jit(solution)/shard_map/all_to_all | solution.py:671
  126.8 3.1 %collective-permute-start.1 = (bf16[8,512]{1,0:T(8,128)(2,1)S(1)}, bf16[8,512]{1,0:T(8,128)(2,1)S(1)}, u32[]{:S(2)}, u32[]{:S(2)}) collective-permute-start(bf16[8,512]{1,0:T(8,128)(2,1)S(1)} %dynamic-slice_bitcast_fusion), channel_id=1, source_target_pairs={{0,1},{1,0},{2,3},{3,2},{4,5},{5,4},{6,7},{7,6},{8,9},{9,8},{10,11... | collective-permute-start | bytes 24584 | tf_op jit(solution)/shard_map/ppermute | solution.py:676
  129.9 2.1 %smooth.1.smoothed = bf16[1024,512]{1,0:T(8,128)(2,1)S(1)} custom-call(bf16[256,8,512]{2,1,0:T(8,128)(2,1)S(1)} %bitcast.18, s32[128]{0:T(128)S(1)} %get-tuple-element.31.pick, bf16[3,128,128]{2,1,0:T(8,128)(2,1)S(1)} %get-tuple-element.32.blocks.cblocks), custom_call_target="tpu_custom_call" | custom-call | flops 536870912 | bytes 3000000 | tf_op jit(solution)/shard_map/smooth/pallas_call | solution.py:597
  131.9 0.0 collective-permute-done.1.near
  132.0 0.0 copy-done.13
  132.0 2.0 %filter_rows.1 = f32[1024,512]{1,0:T(8,128)} custom-call(bf16[1024,512]{1,0:T(8,128)(2,1)S(1)} %smooth.1.smoothed, bf16[8,512]{1,0:T(8,128)(2,1)S(1)} %collective-permute-done.1.near, bf16[3,128,128]{2,1,0:T(8,128)(2,1)S(1)} %get-tuple-element.32.blocks.cblocks, bf16[2,128,128]{2,1,0:T(8,128)(2,1)S(1)} %copy-done.13), custom_call_target="tpu_custom_call" | custom-call | tf_op jit(solution)/shard_map/filter_rows/pallas_call | solution.py:632
  (18 shorter events, 0.0 us)
Async XLA Ops:
  4.1 11.6 %copy-start.21 = (bf16[15]{0:T(256)(128)(2,1)S(1)}, bf16[15]{0:T(256)(128)(2,1)}, u32[]{:S(2)}) copy-start(bf16[15]{0:T(256)(128)(2,1)} %param.22) | copy-start | bytes 94
  4.1 11.6 %copy-start.22 = (bf16[15]{0:T(256)(128)(2,1)S(1)}, bf16[15]{0:T(256)(128)(2,1)}, u32[]{:S(2)}) copy-start(bf16[15]{0:T(256)(128)(2,1)} %param.23) | copy-start | bytes 94
  4.1 11.6 %copy-start.19 = (bf16[12,21]{1,0:T(8,128)(2,1)S(1)}, bf16[12,21]{1,0:T(8,128)(2,1)}, u32[]{:S(2)}) copy-start(bf16[12,21]{1,0:T(8,128)(2,1)} %param.16) | copy-start | bytes 1516
  4.2 11.6 %copy-start.20 = (bf16[12,21]{1,0:T(8,128)(2,1)S(1)}, bf16[12,21]{1,0:T(8,128)(2,1)}, u32[]{:S(2)}) copy-start(bf16[12,21]{1,0:T(8,128)(2,1)} %param.15) | copy-start | bytes 1516
  4.2 12.3 %copy-start.14 = (s32[16]{0:T(128)S(1)}, s32[16]{0:T(128)}, u32[]{:S(2)}) copy-start(s32[16]{0:T(128)} %srow.5) | copy-start | bytes 196
  4.2 12.3 %copy-start.15 = (s32[16]{0:T(128)S(1)}, s32[16]{0:T(128)}, u32[]{:S(2)}) copy-start(s32[16]{0:T(128)} %scol.5) | copy-start | bytes 196
  4.2 12.3 %copy-start.17 = (s32[128]{0:T(128)S(1)}, s32[128]{0:T(128)}, u32[]{:S(2)}) copy-start(s32[128]{0:T(128)} %shift.1) | copy-start | bytes 1540
  4.2 44.8 %all-to-all-start = ((bf16[128,9,8,128]{3,2,1,0:T(8,128)(2,1)}), bf16[128,9,8,128]{3,2,1,0:T(8,128)(2,1)S(1)}, u32[]{:S(2)}, u32[]{:S(2)}) async-start(bf16[128,9,8,128]{3,2,1,0:T(8,128)(2,1)} %pack.1), calls=%async_computation | async-start | bytes 4718592 | tf_op jit(solution)/shard_map/all_to_all | solution.py:657
  16.5 1.6 %copy-start.1 = (f32[1024,512]{1,0:T(8,128)S(1)}, f32[1024,512]{1,0:T(8,128)}, u32[]{:S(2)}) copy-start(f32[1024,512]{1,0:T(8,128)} %science_in.1) | copy-start | bytes 6291460
  28.9 1.1 copy-start.2
  30.0 1.0 copy-start.3
  31.0 0.6 copy-start.5
  31.7 0.7 copy-start.8
  32.4 0.7 copy-start.10
  33.1 0.6 copy-start.12
  33.7 0.5 copy-start.16
  49.0 0.9 copy-start.6
  49.9 4.6 %copy-start.7 = (bf16[128,384]{1,0:T(8,128)(2,1)S(1)}, bf16[128,384]{1,0:T(8,128)(2,1)}, u32[]{:S(2)}) copy-start(bf16[128,384]{1,0:T(8,128)(2,1)} %copy-done.5) | copy-start | bytes 294916
  49.9 4.6 %copy-start.9 = (f32[16,32,128]{2,1,0:T(8,128)S(1)}, f32[16,32,128]{2,1,0:T(8,128)}, u32[]{:S(2)}) copy-start(f32[16,32,128]{2,1,0:T(8,128)} %copy-done.8) | copy-start | bytes 786436
  52.5 13.0 %copy-start = (bf16[1024,512]{1,0:T(8,128)(2,1)}, bf16[1024,512]{1,0:T(8,128)(2,1)S(1)}, u32[]{:S(2)}) copy-start(bf16[1024,512]{1,0:T(8,128)(2,1)S(1)} %get-tuple-element.20.image) | copy-start | bytes 3145732
  52.5 2.0 %collective-permute-start = (bf16[16,512]{1,0:T(8,128)(2,1)S(1)}, bf16[16,512]{1,0:T(8,128)(2,1)S(1)}, u32[]{:S(2)}, u32[]{:S(2)}) collective-permute-start(bf16[16,512]{1,0:T(8,128)(2,1)S(1)} %get-tuple-element.21), channel_id=1, source_target_pairs={{0,1},{1,0},{2,3},{3,2},{4,5},{5,4},{6,7},{7,6},{8,9},{9,8},{10,11... | collective-permute-start | bytes 49160 | tf_op jit(solution)/shard_map/ppermute | solution.py:662
  54.5 11.0 %copy-start.11 = (bf16[16,512]{1,0:T(8,128)(2,1)}, bf16[16,512]{1,0:T(8,128)(2,1)S(1)}, u32[]{:S(2)}) copy-start(bf16[16,512]{1,0:T(8,128)(2,1)S(1)} %collective-permute-done.near) | copy-start | bytes 49156
  61.7 13.8 %all-to-all-start.1 = ((f32[128,2,128]{2,1,0:T(2,128)}), f32[128,2,128]{2,1,0:T(2,128)S(1)}, u32[]{:S(2)}, u32[]{:S(2)}) async-start(f32[128,2,128]{2,1,0:T(2,128)} %stamp_sums.1), calls=%async_computation.1 | async-start | bytes 262144 | tf_op jit(solution)/shard_map/all_to_all | solution.py:666
  75.5 0.7 copy-start.18
  89.5 11.7 %copy-start.4 = (bf16[128,8,512]{2,1,0:T(8,128)(2,1)S(1)}, bf16[128,8,512]{2,1,0:T(8,128)(2,1)}, u32[]{:S(2)}) copy-start(bf16[128,8,512]{2,1,0:T(8,128)(2,1)} %get-tuple-element.28.diff) | copy-start | bytes 3145732
  89.5 18.4 %copy-start.23 = (f32[1,128]{1,0:T(1,128)S(1)}, f32[1,128]{1,0:T(1,128)}, u32[]{:S(2)}) copy-start(f32[1,128]{1,0:T(1,128)} %get-tuple-element.29) | copy-start | bytes 1540
  89.6 37.2 %all-to-all-start.2 = ((bf16[64,4,8,512]{3,2,1,0:T(8,128)(2,1)}), bf16[64,4,8,512]{3,2,1,0:T(8,128)(2,1)S(1)}, u32[]{:S(2)}, u32[]{:S(2)}) async-start(bf16[64,4,8,512]{3,2,1,0:T(8,128)(2,1)} %bitcast.21), calls=%async_computation.2 | async-start | bytes 4194304 | tf_op jit(solution)/shard_map/all_to_all | solution.py:671
  101.2 30.8 %copy-start.13 = (bf16[2,128,128]{2,1,0:T(8,128)(2,1)S(1)}, bf16[2,128,128]{2,1,0:T(8,128)(2,1)}, u32[]{:S(2)}) copy-start(bf16[2,128,128]{2,1,0:T(8,128)(2,1)} %copy-done.12) | copy-start | bytes 196612
  126.8 5.2 %collective-permute-start.1 = (bf16[8,512]{1,0:T(8,128)(2,1)S(1)}, bf16[8,512]{1,0:T(8,128)(2,1)S(1)}, u32[]{:S(2)}, u32[]{:S(2)}) collective-permute-start(bf16[8,512]{1,0:T(8,128)(2,1)S(1)} %dynamic-slice_bitcast_fusion), channel_id=1, source_target_pairs={{0,1},{1,0},{2,3},{3,2},{4,5},{5,4},{6,7},{7,6},{8,9},{9,8},{10,11... | collective-permute-start | bytes 24584 | tf_op jit(solution)/shard_map/ppermute | solution.py:676

commit v3 on v2

--- a/solution.py
+++ b/solution.py
@@ -15,7 +15,7 @@
 FRAMED = ROWS + 2 * PAD
 STEP = 224
 SPAN = 256
-WIN = 56
+WIN = 64
 LANES = BASIS * 32
 LARGE = 58
 BOTH = ("ccd", "strip")
@@ -149,8 +149,8 @@
 
 
 def tables_body(
-    kr, kc, pr, pc, kcl, krl, shift, srow, scol, science,
-    cols_out, rows_out, pcols_out, prows_out, stamp_out, krl_out, seam_out,
+    kr, kc, pr, pc, kcl, shift, srow, scol, science,
+    cols_out, rows_out, pcols_out, prows_out, stamp_out, ready_out, down_out, seam_out,
     slot_out, pick_out, sky_out, count,
 ):
     for b in range(BASIS):
@@ -179,7 +179,14 @@
     for t in range(KTAPS):
         table = jnp.where(lag == t, kcl[t : t + 1, :], table)
     stamp_out[...] = table.astype(BF16)
-    krl_out[...] = krl[...]
+    ready_out[...] = jnp.zeros(ready_out.shape, F32)
+    for q in range(3):
+        for g in range(4):
+            lag = iota((32, 64), 1) - iota((32, 64), 0)
+            table = jnp.zeros((32, 64), F32)
+            for t in range(KTAPS):
+                table = jnp.where(lag == t, kr[4 * q + g, t], table)
+            down_out[q, 32 * g : 32 * g + 32] = table.astype(BF16)
     seam_out[...] = jnp.zeros(seam_out.shape, BF16)
     place = ((iota((32, 128), 1) + 16) & 31) - 16
     source = iota((32, 128), 0) - 16
@@ -232,21 +239,22 @@
             shape((3, 128, 128), BF16),
             shape((2, 128, 128), BF16),
             shape((128, LANES), BF16),
-            shape((24, LANES), F32),
+            shape((8, 128), F32),
+            shape((3, 128, WIN), BF16),
             shape((256, LANES), BF16),
             shape(band_shift.shape, I32),
             shape(band_shift.shape, I32),
             shape((STAMPS, 32, 128), F32),
         ),
-        in_specs=[smem()] * 4 + [vmem()] * 2 + [smem()] * 3 + [vmem()],
-        out_specs=(vmem(),) * 7 + (smem(),) * 2 + (vmem(),),
+        in_specs=[smem()] * 4 + [vmem()] + [smem()] * 3 + [vmem()],
+        out_specs=(vmem(),) * 8 + (smem(),) * 2 + (vmem(),),
         scratch_shapes=[pltpu.SMEM((64,), I32)],
         compiler_params=params(16),
         cost_estimate=cost(2 * 10**9, 4 * 10**6),
         name="tables",
     )(
         kern_row.astype(F32), kc, psf_row.astype(F32), psf_col.astype(F32),
-        expand(kc), expand(kern_row.astype(F32)),
+        expand(kc),
         band_shift, stamp_row, stamp_col, science,
     )
 
@@ -282,7 +290,7 @@
     return pl.pallas_call(
         coadd_body,
         out_shape=(shape((ROWS, COLS), BF16), shape((PAD, COLS), BF16)),
-        in_specs=[vmem(), pl.BlockSpec(memory_space=pl.ANY)],
+        in_specs=[vmem(), vmem()],
         out_specs=(vmem(), vmem()),
         scratch_shapes=[pltpu.VMEM((senders * 16, COLS), BF16)],
         compiler_params=params(16),
@@ -298,7 +306,7 @@
     framed[PAD + ROWS :] = jnp.where(strip == 0, rows, 0.0).astype(framed.dtype)
 
 
-def stamps_body(image, near, sigma, srow, scol, table, krl, sky, out, framed, wins, across, basis):
+def stamps_body(image, near, sigma, srow, scol, table, down, sky, out, framed, wins, across, basis):
     frame(framed, image, near)
     lane = iota((WIN, 128), 1)
 
@@ -306,27 +314,33 @@
         first = scol[s] - 10
         block = window(framed, srow[s] + 6, WIN, first)
         inside = (lane < 52) & (lane + first >= 0) & (lane + first < COLS)
-        wins[s] = jnp.where(inside, block, 0.0)
+        wins[s] = jnp.where(inside, block, 0.0).astype(BF16)
         return c
 
     lax.fori_loop(0, STAMPS, cut, 0, unroll=2)
     wide = jnp.dot(
-        wins[...].reshape(STAMPS * WIN, 128).astype(BF16), table[...], preferred_element_type=F32
-    )
-    across[...] = wide.astype(BF16).astype(F32).reshape(STAMPS, WIN, LANES)
+        wins[...].reshape(STAMPS * WIN, 128), table[...], preferred_element_type=F32
+    )
+    across[...] = wide.astype(BF16).reshape(STAMPS, WIN, LANES)
+    group = iota((32, 128), 1) >> 5
 
     def rows(s, total):
         parts = []
         for q in range(3):
-            acc = jnp.zeros((32, 128), F32)
-            for t in range(KTAPS):
-                acc = acc + krl[t : t + 1, 128 * q : 128 * q + 128] * across[s, t : t + 32, 128 * q : 128 * q + 128]
+            every = jnp.dot(
+                down[q], across[s, :, 128 * q : 128 * q + 128], preferred_element_type=F32
+            )
+            acc = every[:32]
+            for g in range(1, 4):
+                acc = jnp.where(group == g, every[32 * g : 32 * g + 32], acc)
             done = acc.astype(BF16)
             basis[pl.ds(pl.multiple_of(s * 32, 32), 32), 128 * q : 128 * q + 128] = done
             parts.append(total[q] + jnp.sum(done.astype(F32) * sky[s], axis=0, keepdims=True))
         return tuple(parts)
 
-    total = lax.fori_loop(0, STAMPS, rows, tuple(jnp.zeros((1, 128), F32) for _ in range(3)))
+    total = lax.fori_loop(
+        0, STAMPS, rows, tuple(jnp.zeros((1, 128), F32) for _ in range(3)), unroll=4
+    )
     total = jnp.concatenate(total, axis=1)
     pairs = lax.dot_general(
         basis[...], basis[...], (((0,), (0,)), ((), ())), preferred_element_type=F32
@@ -357,7 +371,7 @@
     out[...] = jnp.broadcast_to(packed[None], out.shape)
 
 
-def stamp_sums(image, near, sigma, srow, scol, table, krl, sky, devices):
+def stamp_sums(image, near, sigma, srow, scol, table, down, sky, devices):
     return pl.pallas_call(
         stamps_body,
         out_shape=shape((devices, 2, 128), F32),
@@ -365,13 +379,13 @@
         out_specs=vmem(),
         scratch_shapes=[
             pltpu.VMEM((FRAMED, COLS), F32),
-            pltpu.VMEM((STAMPS, WIN, 128), F32),
-            pltpu.VMEM((STAMPS, WIN, LANES), F32),
+            pltpu.VMEM((STAMPS, WIN, 128), BF16),
+            pltpu.VMEM((STAMPS, WIN, LANES), BF16),
             pltpu.VMEM((STAMPS * 32, LANES), BF16),
         ],
         compiler_params=params(16),
         name="stamp_sums",
-    )(image, near, sigma, srow, scol, table, krl, sky)
+    )(image, near, sigma, srow, scol, table, down, sky)
 
 
 def fill_cols(wide, blocks):
@@ -464,8 +478,8 @@
 
 
 def difference_body(
-    sums, across_in, table_in, science_in, sigma, slot, coef_out, diff_out, leave_out,
-    across, table, science, coef, bands, sems, save_sems,
+    across_in, sums_in, sigma_in, slot_in, table, science, coef_out, diff_out, leave_out,
+    across, sums, sigma, slot, coef, bands, sems, save_sems,
 ):
     def load(i):
         first, _, span = BLOCKS[i]
@@ -475,22 +489,25 @@
             sems.at[i & 1],
         )
 
+    small = [
+        pltpu.make_async_copy(src, dst, sems.at[2 + i])
+        for i, (src, dst) in enumerate([(sums_in, sums), (sigma_in, sigma), (slot_in, slot)])
+    ]
+    for one in small:
+        one.start()
     load(0).start()
-    table_load = pltpu.make_async_copy(table_in, table, sems.at[2])
-    table_load.start()
-    science_load = pltpu.make_async_copy(science_in, science, sems.at[3])
-    science_load.start()
+    for one in small:
+        one.wait()
     found = solve(sums)
     coef[...] = jnp.broadcast_to(found, coef.shape)
     eye = iota((16, 128), 0) == iota((16, 128), 1)
     coef_out[...] = jnp.sum(jnp.where(eye, found, 0.0), axis=0, keepdims=True)
     scale = 1.0 / sigma[0]
     saves = []
-    table_load.wait()
     for i, (first, rows, span) in enumerate(BLOCKS):
-        load(i).wait()
         if i + 1 < len(BLOCKS):
             load(i + 1).start()
+        load(i).wait()
         for h in range(0, COLS, 256):
             model = None
             for b in range(BASIS):
@@ -501,8 +518,6 @@
                 )
                 term = coef[b : b + 1, :] * basis.astype(BF16).astype(F32)
                 model = term if model is None else model + term
-            if i == 0 and h == 0:
-                science_load.wait()
             left = (science[first : first + rows, h : h + 256] - model) * scale
             bands[first // 8 : (first + rows) // 8, :, h : h + 256] = left.reshape(
                 rows // 8, 8, 256
@@ -531,20 +546,21 @@
             shape((ROWS // 8, 8, COLS), BF16),
             shape((slots, 8, COLS), BF16),
         ),
-        in_specs=[vmem()] + [hbm()] * 3 + [smem()] * 2,
+        in_specs=[hbm()] * 4 + [vmem()] * 2,
         out_specs=(vmem(), hbm(), hbm()),
         scratch_shapes=[
             pltpu.VMEM((2, BASIS, SPAN, COLS), BF16),
-            pltpu.VMEM((BASIS, STEP, SPAN), BF16),
-            pltpu.VMEM((ROWS, COLS), F32),
+            pltpu.VMEM(sums.shape, F32),
+            pltpu.SMEM((1,), F32),
+            pltpu.SMEM(slot.shape, I32),
             pltpu.VMEM((16, 256), F32),
             pltpu.VMEM((ROWS // 8, 8, COLS), BF16),
-            pltpu.SemaphoreType.DMA((4,)),
+            pltpu.SemaphoreType.DMA((5,)),
             pltpu.SemaphoreType.DMA((1 + len(BLOCKS),)),
         ],
-        compiler_params=params(54),
+        compiler_params=params(48),
         name="difference",
-    )(sums, across, table, science, sigma, slot)
+    )(across, sums, sigma, slot, table, science)
 
 
 def cut_body(diff, srow, scol, out, wide):
@@ -655,13 +671,13 @@
     cap = 2 * bands // ccds
     outgoing = pack(route_dest, route_row, template, devices)
     arrived = lax.all_to_all(outgoing, BOTH, split_axis=0, concat_axis=0, tiled=True)
-    cols, rows, pcols, prows, stamp_table, krl, seam, slot, pick, sky = tables(
+    cols, rows, pcols, prows, stamp_table, ready, down, seam, slot, pick, sky = tables(
         kern_row, kern_col, psf_row, psf_col, band_shift, stamp_row, stamp_col, science
     )
-    image, edge = coadd(arrived, stamp_table)
+    image, edge = coadd(arrived, ready)
     near = lax.ppermute(edge, "strip", SWAP)
     sums = stamp_sums(
-        image, near, noise_sigma, stamp_row, stamp_col, stamp_table, krl, sky, devices
+        image, near, noise_sigma, stamp_row, stamp_col, stamp_table, down, sky, devices
     )
     sums = lax.all_to_all(sums, BOTH, split_axis=0, concat_axis=0, tiled=True)
     across = across_all(image, near, cols, seam)

time: 135 us -> 130 us (0.963)
  Pallas kernels: 56.6 us -> 51.6 us
    pallas_call x1, Pallas kernels: 13.3 us -> 10 us  [difference_all(): pl.pallas_call(difference_body, out_shape=(shape((1, 128), F32), shape((R...]
    pallas_call x1, Pallas kernels: 7.25 us -> 5.24 us  [stamp_sums(): pl.pallas_call(stamps_body, out_shape=shape((devices, 2, 128), F32), in_s...]
    unnamed x49 -> x51, local copies, waits for them, and re-layouts: 9.11 us -> 10.3 us
  transfers between devices with their start and end apart: 5 -> 5, of which waited for: 4 -> 4; matrix products, arithmetic and copies ran while one was open for 2% -> 2% of each run, Pallas kernels for 21% -> 22%
where the time goes in v3:
time: 130 us
  Pallas kernels  51.6 us (40%)
  waiting for transfers between devices  34.3 us (26%)
  starting transfers between devices  29.2 us (22%)
  local copies, waits for them, and re-layouts  11.7 us (9%)
  between operations  2.93 us (2%)
    all_to_all x1, waiting for transfers between devices, shards(): lax.all_to_all(leaving.reshape(ccds, cap, 8, COLS), 'ccd', split_axis=0,...  18.3 us
    all_to_all x1, waiting for transfers between devices, shards(): lax.all_to_all(outgoing, BOTH, split_axis=0, concat_axis=0, tiled=True)  14.7 us
    all_to_all x1, starting transfers between devices, shards(): lax.all_to_all(outgoing, BOTH, split_axis=0, concat_axis=0, tiled=True)  11.5 us
    pallas_call x1, Pallas kernels, tables(): pl.pallas_call(tables_body, out_shape=(shape((BASIS, 3, 128, 128), BF16),...  11.2 us
    unnamed x51, local copies, waits for them, and re-layouts  10.3 us
    pallas_call x1, Pallas kernels, difference_all(): pl.pallas_call(difference_body, out_shape=(shape((1, 128), F32), shape((R...  10 us
    all_to_all x1, starting transfers between devices, shards(): lax.all_to_all(leaving.reshape(ccds, cap, 8, COLS), 'ccd', split_axis=0,...  9.77 us
    pallas_call x1, Pallas kernels, across_all(): pl.pallas_call(across_body, out_shape=shape((BASIS, FRAMED, COLS), BF16),...  8.98 us
  transfers between devices with their start and end apart: 5, of which 4 were waited for; matrix products, arithmetic and copies ran while one was open for 2% of the time, Pallas kernels for 22%

profile of v3, /device:TPU:1, one launch (start us, length us, event | category | flops | bytes accessed | tf_op | source)
XLA Modules:
  0.0 129.7 jit_solution(15619985483455920118)
XLA Ops:
  0.6 3.5 %pack.1 = bf16[128,9,8,128]{3,2,1,0:T(8,128)(2,1)} custom-call(s32[128]{0:T(128)} %dest_in.1, s32[128]{0:T(128)} %row_in.1, bf16[128,8,512]{2,1,0:T(8,128)(2,1)} %pieces_in.1), custom_call_target="tpu_custom_call" | custom-call | tf_op jit(solution)/shard_map/pack/pallas_call | solution.py:114
  4.1 0.0 copy-start.21
  4.1 0.0 copy-start.22
  4.1 0.0 copy-start.23
  4.1 0.0 copy-start.24
  4.2 0.0 copy-start.18
  4.2 0.0 copy-start.19
  4.2 0.0 copy-start.20
  4.2 11.5 %all-to-all-start = ((bf16[128,9,8,128]{3,2,1,0:T(8,128)(2,1)}), bf16[128,9,8,128]{3,2,1,0:T(8,128)(2,1)S(1)}, u32[]{:S(2)}, u32[]{:S(2)}) async-start(bf16[128,9,8,128]{3,2,1,0:T(8,128)(2,1)} %pack.1), calls=%async_computation | async-start | bytes 4718592 | tf_op jit(solution)/shard_map/all_to_all | solution.py:673
  15.7 0.0 copy-done.21
  15.7 0.1 copy.17
  15.8 0.1 broadcast_in_dim.3
  15.9 0.1 reshape.23
  16.0 0.0 copy-done.22
  16.1 0.0 copy-done.23
  16.1 0.0 copy-done.24
  16.1 0.0 copy-done.18
  16.1 0.0 copy-done.19
  16.1 0.0 copy-done.20
  16.1 0.0 copy-start.2
  16.2 1.6 %copy-done.2 = f32[1024,512]{1,0:T(8,128)S(1)} copy-done((f32[1024,512]{1,0:T(8,128)S(1)}, f32[1024,512]{1,0:T(8,128)}, u32[]{:S(2)}) %copy-start.2) | copy-done | bytes 2097176
  17.7 11.2 %tables.1 = (bf16[12,3,128,128]{3,2,1,0:T(8,128)(2,1)S(1)}, bf16[12,224,256]{2,1,0:T(8,128)(2,1)S(1)}, bf16[3,128,128]{2,1,0:T(8,128)(2,1)S(1)}, bf16[2,128,128]...) custom-call(f32[12,21]{1,0:T(8,128)S(1)} %convert_element_type.14.kr, ...), custom_call_target="tpu_custom_call" | custom-call | flops 2000000000 | bytes 4000000 | tf_op jit(solution)/shard_map/tables/pallas_call | solution.py:234
  28.9 0.0 copy-start.4
  28.9 1.1 copy-done.4
  30.0 0.0 copy-start.6
  30.0 1.0 copy-done.6
  31.0 0.7 copy-done.8
  31.7 0.7 copy-done.10
  32.4 0.6 copy-done.11
  33.0 0.6 copy-done.13
  33.7 0.6 copy-done.16
  34.3 14.7 %all-to-all-done.arrived = bf16[128,9,8,128]{3,2,1,0:T(8,128)(2,1)S(1)} async-done(((bf16[128,9,8,128]{3,2,1,0:T(8,128)(2,1)}), bf16[128,9,8,128]{3,2,1,0:T(8,128)(2,1)S(1)}, u32[]{:S(2)}, u32[]{:S(2)}) %all-to-all-start) | async-done | bytes 2359328 | tf_op jit(solution)/shard_map/all_to_all | solution.py:673
  49.0 2.6 %coadd.1 = (bf16[1024,512]{1,0:T(8,128)(2,1)S(1)}, bf16[16,512]{1,0:T(8,128)(2,1)S(1)}) custom-call(bf16[128,9,8,128]{3,2,1,0:T(8,128)(2,1)S(1)} %all-to-all-done.arrived, f32[8,128]{1,0:T(8,128)S(1)} %get-tuple-element.20.ready), custom_call_target="tpu_custom_call" | custom-call | tf_op jit(solution)/shard_map/coadd/pallas_call | solution.py:290
  51.6 0.0 copy-start
  51.6 1.1 collective-permute-start
  53.4 0.2 collective-permute-done.near
  53.5 0.0 copy-done.9
  53.5 0.0 copy-done.12
  53.5 0.0 copy-done.14
  53.6 5.2 %stamp_sums.1 = f32[128,2,128]{2,1,0:T(2,128)} custom-call(bf16[1024,512]{1,0:T(8,128)(2,1)S(1)} %get-tuple-element.21.image, bf16[16,512]{1,0:T(8,128)(2,1)S(1)} %collective-permute-done.near, f32[1]{0:T(128)S(6)} %copy.21.sigma.sigma_in, s32[16]{0:T(128)S(1)} %copy-done.18, s32[16]{0:T(128)S(1)} %copy-done.19, bf16[128,384]{1,0:T(8,128)(2,1)S(1)} %copy-done.12, ...), custom_call_target="tpu_custom_call" | custom-call | tf_op jit(solution)/shard_map/stamp_sums/pallas_call | solution.py:375
  58.8 3.7 %all-to-all-start.1 = ((f32[128,2,128]{2,1,0:T(2,128)}), f32[128,2,128]{2,1,0:T(2,128)S(1)}, u32[]{:S(2)}, u32[]{:S(2)}) async-start(f32[128,2,128]{2,1,0:T(2,128)} %stamp_sums.1), calls=%async_computation.1 | async-start | bytes 262144 | tf_op jit(solution)/shard_map/all_to_all | solution.py:682
  62.5 0.0 copy-done
  62.5 0.0 copy-done.15
  62.6 0.0 copy-start.3
  62.6 9.0 %across.1.across_in = bf16[12,1056,512]{2,1,0:T(8,128)(2,1)} custom-call(bf16[1024,512]{1,0:T(8,128)(2,1)} %copy-done, bf16[16,512]{1,0:T(8,128)(2,1)} %copy-done.15, bf16[12,3,128,128]{3,2,1,0:T(8,128)(2,1)} %copy-done.6, bf16[256,384]{1,0:T(8,128)(2,1)} %copy-done.10), custom_call_target="tpu_custom_call" | custom-call | flops 3321888768 | bytes 16000000 | tf_op jit(solution)/shard_map/across/pallas_call | solution.py:449
  71.6 1.1 all-to-all-done.1.sums_in
  72.6 0.0 copy-done.3
  72.6 1.3 %copy-done.5 = bf16[12,224,256]{2,1,0:T(8,128)(2,1)S(1)} copy-done((bf16[12,224,256]{2,1,0:T(8,128)(2,1)S(1)}, bf16[12,224,256]{2,1,0:T(8,128)(2,1)}, u32[]{:S(2)}) %copy-start.5) | copy-done | bytes 1376280
  74.0 10.0 %difference.1 = (f32[1,128]{1,0:T(1,128)S(1)}, bf16[128,8,512]{2,1,0:T(8,128)(2,1)}, bf16[256,8,512]{2,1,0:T(8,128)(2,1)S(1)}) custom-call(bf16[12,1056,512]{2,1,0:T(8,128)(2,1)} %across.1.across_in, f32[128,2,128]{2,1,0:T(2,128)S(1)} %all-to-all-done.1.sums_in, f32[1]{0:T(128)S(6)} %copy.21.sigma.sigma_in, s32[128]{0:T(128)S(1)} %get-tuple-element.28.slot_in, ...), custom_call_target="tpu_custom_call" | custom-call | tf_op jit(solution)/shard_map/difference/pallas_call | solution.py:542
  84.0 0.0 copy-start.1
  84.0 1.3 %copy-done.1 = bf16[256,8,512]{2,1,0:T(8,128)(2,1)} copy-done((bf16[256,8,512]{2,1,0:T(8,128)(2,1)}, bf16[256,8,512]{2,1,0:T(8,128)(2,1)S(1)}, u32[]{:S(2)}) %copy-start.1) | copy-done | bytes 2097176
  85.3 9.8 %all-to-all-start.2 = ((bf16[64,4,8,512]{3,2,1,0:T(8,128)(2,1)}), bf16[64,4,8,512]{3,2,1,0:T(8,128)(2,1)S(1)}, u32[]{:S(2)}, u32[]{:S(2)}) async-start(bf16[64,4,8,512]{3,2,1,0:T(8,128)(2,1)} %bitcast.17), calls=%async_computation.2 | async-start | bytes 4194304 | tf_op jit(solution)/shard_map/all_to_all | solution.py:687
  95.1 0.6 fusion
  97.0 0.0 copy-done.7
  97.0 0.0 copy-start.17
  97.0 6.1 %cut_stamps.1 = bf16[16,8,128]{2,1,0:T(8,128)(2,1)S(1)} custom-call(bf16[128,8,512]{2,1,0:T(8,128)(2,1)S(1)} %copy-done.7, s32[16]{0:T(128)S(1)} %copy-done.18, s32[16]{0:T(128)S(1)} %copy-done.19), custom_call_target="tpu_custom_call" | custom-call | flops 100000000 | bytes 3000000 | tf_op jit(solution)/shard_map/cut_stamps/pallas_call | solution.py:583
  103.1 0.6 copy.20
  103.7 0.5 slice_bitcast_fusion
  104.2 18.3 %all-to-all-done.2 = bf16[64,4,8,512]{3,2,1,0:T(8,128)(2,1)S(1)} async-done(((bf16[64,4,8,512]{3,2,1,0:T(8,128)(2,1)}), bf16[64,4,8,512]{3,2,1,0:T(8,128)(2,1)S(1)}, u32[]{:S(2)}, u32[]{:S(2)}) %all-to-all-start.2) | async-done | bytes 2097184 | tf_op jit(solution)/shard_map/all_to_all | solution.py:687
  122.5 3.1 %collective-permute-start.1 = (bf16[8,512]{1,0:T(8,128)(2,1)S(1)}, bf16[8,512]{1,0:T(8,128)(2,1)S(1)}, u32[]{:S(2)}, u32[]{:S(2)}) collective-permute-start(bf16[8,512]{1,0:T(8,128)(2,1)S(1)} %dynamic-slice_bitcast_fusion), channel_id=1, source_target_pairs={{0,1},{1,0},{2,3},{3,2},{4,5},{5,4},{6,7},{7,6},{8,9},{9,8},{10,11... | collective-permute-start | bytes 24584 | tf_op jit(solution)/shard_map/ppermute | solution.py:692
  125.6 2.1 %smooth.1.smoothed = bf16[1024,512]{1,0:T(8,128)(2,1)S(1)} custom-call(bf16[256,8,512]{2,1,0:T(8,128)(2,1)S(1)} %bitcast.16, s32[128]{0:T(128)S(1)} %get-tuple-element.33.pick, bf16[3,128,128]{2,1,0:T(8,128)(2,1)S(1)} %get-tuple-element.34.blocks.cblocks), custom_call_target="tpu_custom_call" | custom-call | flops 536870912 | bytes 3000000 | tf_op jit(solution)/shard_map/smooth/pallas_call | solution.py:613
  127.7 0.0 collective-permute-done.1.near
  127.7 0.0 copy-done.17
  127.7 2.0 %filter_rows.1 = f32[1024,512]{1,0:T(8,128)} custom-call(bf16[1024,512]{1,0:T(8,128)(2,1)S(1)} %smooth.1.smoothed, bf16[8,512]{1,0:T(8,128)(2,1)S(1)} %collective-permute-done.1.near, bf16[3,128,128]{2,1,0:T(8,128)(2,1)S(1)} %get-tuple-element.34.blocks.cblocks, bf16[2,128,128]{2,1,0:T(8,128)(2,1)S(1)} %copy-done.17), custom_call_target="tpu_custom_call" | custom-call | tf_op jit(solution)/shard_map/filter_rows/pallas_call | solution.py:648
  (17 shorter events, 0.0 us)
Async XLA Ops:
  4.1 11.6 %copy-start.21 = (bf16[12,21]{1,0:T(8,128)(2,1)S(1)}, bf16[12,21]{1,0:T(8,128)(2,1)}, u32[]{:S(2)}) copy-start(bf16[12,21]{1,0:T(8,128)(2,1)} %param.16) | copy-start | bytes 1516
  4.1 11.9 %copy-start.22 = (bf16[12,21]{1,0:T(8,128)(2,1)S(1)}, bf16[12,21]{1,0:T(8,128)(2,1)}, u32[]{:S(2)}) copy-start(bf16[12,21]{1,0:T(8,128)(2,1)} %param.15) | copy-start | bytes 1516
  4.1 11.9 %copy-start.23 = (bf16[15]{0:T(256)(128)(2,1)S(1)}, bf16[15]{0:T(256)(128)(2,1)}, u32[]{:S(2)}) copy-start(bf16[15]{0:T(256)(128)(2,1)} %param.22) | copy-start | bytes 94
  4.1 11.9 %copy-start.24 = (bf16[15]{0:T(256)(128)(2,1)S(1)}, bf16[15]{0:T(256)(128)(2,1)}, u32[]{:S(2)}) copy-start(bf16[15]{0:T(256)(128)(2,1)} %param.23) | copy-start | bytes 94
  4.2 12.0 %copy-start.18 = (s32[16]{0:T(128)S(1)}, s32[16]{0:T(128)}, u32[]{:S(2)}) copy-start(s32[16]{0:T(128)} %srow.5) | copy-start | bytes 196
  4.2 12.0 %copy-start.19 = (s32[16]{0:T(128)S(1)}, s32[16]{0:T(128)}, u32[]{:S(2)}) copy-start(s32[16]{0:T(128)} %scol.5) | copy-start | bytes 196
  4.2 12.0 %copy-start.20 = (s32[128]{0:T(128)S(1)}, s32[128]{0:T(128)}, u32[]{:S(2)}) copy-start(s32[128]{0:T(128)} %shift.1) | copy-start | bytes 1540
  4.2 44.8 %all-to-all-start = ((bf16[128,9,8,128]{3,2,1,0:T(8,128)(2,1)}), bf16[128,9,8,128]{3,2,1,0:T(8,128)(2,1)S(1)}, u32[]{:S(2)}, u32[]{:S(2)}) async-start(bf16[128,9,8,128]{3,2,1,0:T(8,128)(2,1)} %pack.1), calls=%async_computation | async-start | bytes 4718592 | tf_op jit(solution)/shard_map/all_to_all | solution.py:673
  16.1 1.6 %copy-start.2 = (f32[1024,512]{1,0:T(8,128)S(1)}, f32[1024,512]{1,0:T(8,128)}, u32[]{:S(2)}) copy-start(f32[1024,512]{1,0:T(8,128)} %science.3) | copy-start | bytes 6291460
  28.9 1.1 copy-start.4
  30.0 1.0 copy-start.6
  31.0 0.7 copy-start.8
  31.7 0.7 copy-start.10
  32.4 0.6 copy-start.11
  33.0 0.6 copy-start.13
  33.7 0.6 copy-start.16
  49.0 4.6 %copy-start.9 = (f32[16,32,128]{2,1,0:T(8,128)S(1)}, f32[16,32,128]{2,1,0:T(8,128)}, u32[]{:S(2)}) copy-start(f32[16,32,128]{2,1,0:T(8,128)} %copy-done.8) | copy-start | bytes 786436
  49.0 4.6 %copy-start.12 = (bf16[128,384]{1,0:T(8,128)(2,1)S(1)}, bf16[128,384]{1,0:T(8,128)(2,1)}, u32[]{:S(2)}) copy-start(bf16[128,384]{1,0:T(8,128)(2,1)} %copy-done.11) | copy-start | bytes 294916
  49.0 4.6 %copy-start.14 = (bf16[3,128,64]{2,1,0:T(8,128)(2,1)S(1)}, bf16[3,128,64]{2,1,0:T(8,128)(2,1)}, u32[]{:S(2)}) copy-start(bf16[3,128,64]{2,1,0:T(8,128)(2,1)} %copy-done.13) | copy-start | bytes 147460
  51.6 11.0 %copy-start = (bf16[1024,512]{1,0:T(8,128)(2,1)}, bf16[1024,512]{1,0:T(8,128)(2,1)S(1)}, u32[]{:S(2)}) copy-start(bf16[1024,512]{1,0:T(8,128)(2,1)S(1)} %get-tuple-element.21.image) | copy-start | bytes 3145732
  51.6 2.0 %collective-permute-start = (bf16[16,512]{1,0:T(8,128)(2,1)S(1)}, bf16[16,512]{1,0:T(8,128)(2,1)S(1)}, u32[]{:S(2)}, u32[]{:S(2)}) collective-permute-start(bf16[16,512]{1,0:T(8,128)(2,1)S(1)} %get-tuple-element.22), channel_id=1, source_target_pairs={{0,1},{1,0},{2,3},{3,2},{4,5},{5,4},{6,7},{7,6},{8,9},{9,8},{10,11... | collective-permute-start | bytes 49160 | tf_op jit(solution)/shard_map/ppermute | solution.py:678
  53.5 9.0 %copy-start.15 = (bf16[16,512]{1,0:T(8,128)(2,1)}, bf16[16,512]{1,0:T(8,128)(2,1)S(1)}, u32[]{:S(2)}) copy-start(bf16[16,512]{1,0:T(8,128)(2,1)S(1)} %collective-permute-done.near) | copy-start | bytes 49156
  58.8 13.8 %all-to-all-start.1 = ((f32[128,2,128]{2,1,0:T(2,128)}), f32[128,2,128]{2,1,0:T(2,128)S(1)}, u32[]{:S(2)}, u32[]{:S(2)}) async-start(f32[128,2,128]{2,1,0:T(2,128)} %stamp_sums.1), calls=%async_computation.1 | async-start | bytes 262144 | tf_op jit(solution)/shard_map/all_to_all | solution.py:682
  62.6 10.1 %copy-start.3 = (f32[1024,512]{1,0:T(8,128)S(1)}, f32[1024,512]{1,0:T(8,128)}, u32[]{:S(2)}) copy-start(f32[1024,512]{1,0:T(8,128)} %science.3) | copy-start | bytes 6291460
  72.6 1.3 %copy-start.5 = (bf16[12,224,256]{2,1,0:T(8,128)(2,1)S(1)}, bf16[12,224,256]{2,1,0:T(8,128)(2,1)}, u32[]{:S(2)}) copy-start(bf16[12,224,256]{2,1,0:T(8,128)(2,1)} %copy-done.4) | copy-start | bytes 4128772
  84.0 1.3 %copy-start.1 = (bf16[256,8,512]{2,1,0:T(8,128)(2,1)}, bf16[256,8,512]{2,1,0:T(8,128)(2,1)S(1)}, u32[]{:S(2)}) copy-start(bf16[256,8,512]{2,1,0:T(8,128)(2,1)S(1)} %get-tuple-element.32) | copy-start | bytes 6291460
  85.3 11.7 %copy-start.7 = (bf16[128,8,512]{2,1,0:T(8,128)(2,1)S(1)}, bf16[128,8,512]{2,1,0:T(8,128)(2,1)}, u32[]{:S(2)}) copy-start(bf16[128,8,512]{2,1,0:T(8,128)(2,1)} %get-tuple-element.30.diff) | copy-start | bytes 3145732
  85.3 37.2 %all-to-all-start.2 = ((bf16[64,4,8,512]{3,2,1,0:T(8,128)(2,1)}), bf16[64,4,8,512]{3,2,1,0:T(8,128)(2,1)S(1)}, u32[]{:S(2)}, u32[]{:S(2)}) async-start(bf16[64,4,8,512]{3,2,1,0:T(8,128)(2,1)} %bitcast.17), calls=%async_computation.2 | async-start | bytes 4194304 | tf_op jit(solution)/shard_map/all_to_all | solution.py:687
  97.0 30.8 %copy-start.17 = (bf16[2,128,128]{2,1,0:T(8,128)(2,1)S(1)}, bf16[2,128,128]{2,1,0:T(8,128)(2,1)}, u32[]{:S(2)}) copy-start(bf16[2,128,128]{2,1,0:T(8,128)(2,1)} %copy-done.16) | copy-start | bytes 196612
  122.5 5.2 %collective-permute-start.1 = (bf16[8,512]{1,0:T(8,128)(2,1)S(1)}, bf16[8,512]{1,0:T(8,128)(2,1)S(1)}, u32[]{:S(2)}, u32[]{:S(2)}) collective-permute-start(bf16[8,512]{1,0:T(8,128)(2,1)S(1)} %dynamic-slice_bitcast_fusion), channel_id=1, source_target_pairs={{0,1},{1,0},{2,3},{3,2},{4,5},{5,4},{6,7},{7,6},{8,9},{9,8},{10,11... | collective-permute-start | bytes 24584 | tf_op jit(solution)/shard_map/ppermute | solution.py:692

commit v4 on v3

--- a/solution.py
+++ b/solution.py
@@ -317,7 +317,7 @@
         wins[s] = jnp.where(inside, block, 0.0).astype(BF16)
         return c
 
-    lax.fori_loop(0, STAMPS, cut, 0, unroll=2)
+    lax.fori_loop(0, STAMPS, cut, 0, unroll=4)
     wide = jnp.dot(
         wins[...].reshape(STAMPS * WIN, 128), table[...], preferred_element_type=F32
     )
@@ -478,46 +478,54 @@
 
 
 def difference_body(
-    across_in, sums_in, sigma_in, slot_in, table, science, coef_out, diff_out, leave_out,
-    across, sums, sigma, slot, coef, bands, sems, save_sems,
+    across_in, sums_in, sigma_in, slot_in, table_in, science_in, coef_out, diff_out, leave_out,
+    across, table, science, sums, sigma, slot, coef, bands, sems, load_sems, save_sems,
 ):
+    ends = [0] + [first + span for first, _, span in BLOCKS]
+
     def load(i):
-        first, _, span = BLOCKS[i]
+        some = pl.ds(ends[i], ends[i + 1] - ends[i])
         return pltpu.make_async_copy(
-            across_in.at[:, pl.ds(first, span), :],
-            across.at[i & 1, :, pl.ds(0, span), :],
-            sems.at[i & 1],
+            across_in.at[:, some, :], across.at[:, some, :], load_sems.at[i]
         )
 
     small = [
-        pltpu.make_async_copy(src, dst, sems.at[2 + i])
+        pltpu.make_async_copy(src, dst, sems.at[i])
         for i, (src, dst) in enumerate([(sums_in, sums), (sigma_in, sigma), (slot_in, slot)])
     ]
+    table_load = pltpu.make_async_copy(table_in, table, sems.at[3])
+    science_load = pltpu.make_async_copy(science_in, science, sems.at[4])
     for one in small:
         one.start()
     load(0).start()
+    table_load.start()
     for one in small:
         one.wait()
     found = solve(sums)
     coef[...] = jnp.broadcast_to(found, coef.shape)
     eye = iota((16, 128), 0) == iota((16, 128), 1)
     coef_out[...] = jnp.sum(jnp.where(eye, found, 0.0), axis=0, keepdims=True)
+    science_load.start()
+    for i in range(1, len(BLOCKS)):
+        load(i).start()
     scale = 1.0 / sigma[0]
     saves = []
     for i, (first, rows, span) in enumerate(BLOCKS):
-        if i + 1 < len(BLOCKS):
-            load(i + 1).start()
         load(i).wait()
+        if i == 0:
+            table_load.wait()
         for h in range(0, COLS, 256):
             model = None
             for b in range(BASIS):
                 basis = jnp.dot(
                     table[b, :rows, :span],
-                    across[i & 1, b, :span, h : h + 256],
+                    across[b, first : first + span, h : h + 256],
                     preferred_element_type=F32,
                 )
                 term = coef[b : b + 1, :] * basis.astype(BF16).astype(F32)
                 model = term if model is None else model + term
+            if i == 0 and h == 0:
+                science_load.wait()
             left = (science[first : first + rows, h : h + 256] - model) * scale
             bands[first // 8 : (first + rows) // 8, :, h : h + 256] = left.reshape(
                 rows // 8, 8, 256
@@ -546,19 +554,22 @@
             shape((ROWS // 8, 8, COLS), BF16),
             shape((slots, 8, COLS), BF16),
         ),
-        in_specs=[hbm()] * 4 + [vmem()] * 2,
+        in_specs=[hbm()] * 6,
         out_specs=(vmem(), hbm(), hbm()),
         scratch_shapes=[
-            pltpu.VMEM((2, BASIS, SPAN, COLS), BF16),
+            pltpu.VMEM((BASIS, FRAMED, COLS), BF16),
+            pltpu.VMEM(table.shape, BF16),
+            pltpu.VMEM(science.shape, F32),
             pltpu.VMEM(sums.shape, F32),
             pltpu.SMEM((1,), F32),
             pltpu.SMEM(slot.shape, I32),
             pltpu.VMEM((16, 256), F32),
             pltpu.VMEM((ROWS // 8, 8, COLS), BF16),
             pltpu.SemaphoreType.DMA((5,)),
+            pltpu.SemaphoreType.DMA((len(BLOCKS),)),
             pltpu.SemaphoreType.DMA((1 + len(BLOCKS),)),
         ],
-        compiler_params=params(48),
+        compiler_params=params(53),
         name="difference",
     )(across, sums, sigma, slot, table, science)
 
@@ -629,7 +640,7 @@
     table[128:, 128:] = blocks[0][: STEP - 128]
 
 
-def filter_body(smoothed, near, cblocks, rblocks, out, framed, wide, table, tail):
+def filter_body(smoothed, near, cblocks, rblocks, out, framed, wide, table, tail, held, sems):
     fill_cols(wide, cblocks)
     fill_rows(table, rblocks)
     tail[...] = jnp.concatenate(
@@ -638,10 +649,16 @@
     edge = jnp.dot(tail[...], wide[...], preferred_element_type=F32)
     edge = jnp.where(lax.axis_index("strip") == 0, edge, jnp.concatenate([edge[8:], edge[:8]], axis=0))
     frame(framed, smoothed, edge.astype(BF16))
+    saves = []
     for first, rows, span in BLOCKS:
-        out[first : first + rows] = jnp.dot(
+        held[first : first + rows] = jnp.dot(
             table[:rows, :span], framed[first : first + span], preferred_element_type=F32
         )
+        some = pl.ds(first, rows)
+        saves.append(pltpu.make_async_copy(held.at[some], out.at[some], sems.at[len(saves)]))
+        saves[-1].start()
+    for save in saves:
+        save.wait()
 
 
 def filter_rows(smoothed, near, cblocks, rblocks):
@@ -649,12 +666,14 @@
         filter_body,
         out_shape=shape((ROWS, COLS), F32),
         in_specs=[vmem()] * 4,
-        out_specs=vmem(),
+        out_specs=hbm(),
         scratch_shapes=[
             pltpu.VMEM((FRAMED, COLS), BF16),
             pltpu.VMEM((COLS, COLS), BF16),
             pltpu.VMEM((STEP, SPAN), BF16),
             pltpu.VMEM((PAD, COLS), BF16),
+            pltpu.VMEM((ROWS, COLS), F32),
+            pltpu.SemaphoreType.DMA((len(BLOCKS),)),
         ],
         compiler_params=params(16),
         name="filter_rows",

time: 130 us -> 128 us (0.985)
  local copies, waits for them, and re-layouts: 11.7 us -> 9.11 us
    unnamed x51 -> x45, local copies, waits for them, and re-layouts: 10.3 us -> 7.71 us
where the time goes in v4:
time: 128 us; the launch traced here: 127 us
  Pallas kernels  51.7 us (40%)
  waiting for transfers between devices  34.3 us (27%)
  starting transfers between devices  29.2 us (23%)
  local copies, waits for them, and re-layouts  9.11 us (7%)
  between operations  3.08 us (2%)
    all_to_all x1, waiting for transfers between devices, shards(): lax.all_to_all(leaving.reshape(ccds, cap, 8, COLS), 'ccd', split_axis=0,...  18.3 us
    all_to_all x1, waiting for transfers between devices, shards(): lax.all_to_all(outgoing, BOTH, split_axis=0, concat_axis=0, tiled=True)  14.6 us
    all_to_all x1, starting transfers between devices, shards(): lax.all_to_all(outgoing, BOTH, split_axis=0, concat_axis=0, tiled=True)  11.5 us
    pallas_call x1, Pallas kernels, tables(): pl.pallas_call(tables_body, out_shape=(shape((BASIS, 3, 128, 128), BF16),...  11.2 us
    pallas_call x1, Pallas kernels, difference_all(): pl.pallas_call(difference_body, out_shape=(shape((1, 128), F32), shape((R...  10.7 us
    all_to_all x1, starting transfers between devices, shards(): lax.all_to_all(leaving.reshape(ccds, cap, 8, COLS), 'ccd', split_axis=0,...  9.72 us
    pallas_call x1, Pallas kernels, across_all(): pl.pallas_call(across_body, out_shape=shape((BASIS, FRAMED, COLS), BF16),...  8.91 us
    unnamed x45, local copies, waits for them, and re-layouts  7.71 us
  transfers between devices with their start and end apart: 5, of which 4 were waited for; matrix products, arithmetic and copies ran while one was open for 2% of the time, Pallas kernels for 22%

profile of v4, /device:TPU:1, one launch (start us, length us, event | category | flops | bytes accessed | tf_op | source)
XLA Modules:
  0.0 127.3 jit_solution(10061665752134770114)
XLA Ops:
  0.6 3.5 %pack.1 = bf16[128,9,8,128]{3,2,1,0:T(8,128)(2,1)} custom-call(s32[128]{0:T(128)} %dest_in.1, s32[128]{0:T(128)} %row_in.1, bf16[128,8,512]{2,1,0:T(8,128)(2,1)} %pieces_in.1), custom_call_target="tpu_custom_call" | custom-call | tf_op jit(solution)/shard_map/pack/pallas_call | solution.py:114
  4.1 0.0 copy-start.18
  4.1 0.0 copy-start.19
  4.1 0.0 copy-start.20
  4.2 0.0 copy-start.21
  4.2 0.0 copy-start.15
  4.2 0.0 copy-start.16
  4.2 0.0 copy-start.17
  4.2 11.5 %all-to-all-start = ((bf16[128,9,8,128]{3,2,1,0:T(8,128)(2,1)}), bf16[128,9,8,128]{3,2,1,0:T(8,128)(2,1)S(1)}, u32[]{:S(2)}, u32[]{:S(2)}) async-start(bf16[128,9,8,128]{3,2,1,0:T(8,128)(2,1)} %pack.1), calls=%async_computation | async-start | bytes 4718592 | tf_op jit(solution)/shard_map/all_to_all | solution.py:692
  15.7 0.0 copy-done.18
  15.7 0.1 copy.17
  15.8 0.1 broadcast_in_dim.3
  15.9 0.1 reshape.23
  16.1 0.0 copy-done.19
  16.1 0.0 copy-done.20
  16.1 0.0 copy-done.21
  16.1 0.0 copy-done.15
  16.1 0.0 copy-done.16
  16.2 0.0 copy-done.17
  16.2 0.0 copy-start.1
  16.2 1.6 %copy-done.1 = f32[1024,512]{1,0:T(8,128)S(1)} copy-done((f32[1024,512]{1,0:T(8,128)S(1)}, f32[1024,512]{1,0:T(8,128)}, u32[]{:S(2)}) %copy-start.1) | copy-done | bytes 2097176
  17.8 11.2 %tables.1 = (bf16[12,3,128,128]{3,2,1,0:T(8,128)(2,1)S(1)}, bf16[12,224,256]{2,1,0:T(8,128)(2,1)S(1)}, bf16[3,128,128]{2,1,0:T(8,128)(2,1)S(1)}, bf16[2,128,128]...) custom-call(f32[12,21]{1,0:T(8,128)S(1)} %convert_element_type.14.kr, ...), custom_call_target="tpu_custom_call" | custom-call | flops 2000000000 | bytes 4000000 | tf_op jit(solution)/shard_map/tables/pallas_call | solution.py:234
  28.9 0.0 copy-start.2
  28.9 1.1 copy-done.2
  30.0 0.0 copy-start.3
  30.0 1.0 copy-done.3
  31.0 0.0 copy-start.5
  31.0 0.7 copy-done.5
  31.7 0.0 copy-start.7
  31.7 0.7 copy-done.7
  32.4 0.0 copy-start.8
  32.4 0.6 copy-done.8
  33.1 0.0 copy-start.10
  33.1 0.6 copy-done.10
  33.7 0.6 copy-done.13
  34.3 14.6 %all-to-all-done.arrived = bf16[128,9,8,128]{3,2,1,0:T(8,128)(2,1)S(1)} async-done(((bf16[128,9,8,128]{3,2,1,0:T(8,128)(2,1)}), bf16[128,9,8,128]{3,2,1,0:T(8,128)(2,1)S(1)}, u32[]{:S(2)}, u32[]{:S(2)}) %all-to-all-start) | async-done | bytes 2359328 | tf_op jit(solution)/shard_map/all_to_all | solution.py:692
  49.0 2.6 %coadd.1 = (bf16[1024,512]{1,0:T(8,128)(2,1)S(1)}, bf16[16,512]{1,0:T(8,128)(2,1)S(1)}) custom-call(bf16[128,9,8,128]{3,2,1,0:T(8,128)(2,1)S(1)} %all-to-all-done.arrived, f32[8,128]{1,0:T(8,128)S(1)} %get-tuple-element.20.ready), custom_call_target="tpu_custom_call" | custom-call | tf_op jit(solution)/shard_map/coadd/pallas_call | solution.py:290
  51.6 0.0 copy-start
  51.6 1.1 collective-permute-start
  53.4 0.2 collective-permute-done.near
  53.5 0.0 copy-done.6
  53.6 0.0 copy-done.9
  53.6 0.0 copy-done.11
  53.6 4.9 %stamp_sums.1 = f32[128,2,128]{2,1,0:T(2,128)} custom-call(bf16[1024,512]{1,0:T(8,128)(2,1)S(1)} %get-tuple-element.21.image, bf16[16,512]{1,0:T(8,128)(2,1)S(1)} %collective-permute-done.near, f32[1]{0:T(128)S(6)} %copy.21.sigma.sigma_in, s32[16]{0:T(128)S(1)} %copy-done.15, s32[16]{0:T(128)S(1)} %copy-done.16, bf16[128,384]{1,0:T(8,128)(2,1)S(1)} %copy-done.9, ...), custom_call_target="tpu_custom_call" | custom-call | tf_op jit(solution)/shard_map/stamp_sums/pallas_call | solution.py:375
  58.4 3.7 %all-to-all-start.1 = ((f32[128,2,128]{2,1,0:T(2,128)}), f32[128,2,128]{2,1,0:T(2,128)S(1)}, u32[]{:S(2)}, u32[]{:S(2)}) async-start(f32[128,2,128]{2,1,0:T(2,128)} %stamp_sums.1), calls=%async_computation.1 | async-start | bytes 262144 | tf_op jit(solution)/shard_map/all_to_all | solution.py:701
  62.1 0.0 copy-done
  62.2 0.0 copy-done.12
  62.2 8.9 %across.1.across_in = bf16[12,1056,512]{2,1,0:T(8,128)(2,1)} custom-call(bf16[1024,512]{1,0:T(8,128)(2,1)} %copy-done, bf16[16,512]{1,0:T(8,128)(2,1)} %copy-done.12, bf16[12,3,128,128]{3,2,1,0:T(8,128)(2,1)} %copy-done.3, bf16[256,384]{1,0:T(8,128)(2,1)} %copy-done.7), custom_call_target="tpu_custom_call" | custom-call | flops 3321888768 | bytes 16000000 | tf_op jit(solution)/shard_map/across/pallas_call | solution.py:449
  71.1 1.1 all-to-all-done.1.sums_in
  72.2 10.7 %difference.1 = (f32[1,128]{1,0:T(1,128)S(1)}, bf16[128,8,512]{2,1,0:T(8,128)(2,1)}, bf16[256,8,512]{2,1,0:T(8,128)(2,1)}) custom-call(bf16[12,1056,512]{2,1,0:T(8,128)(2,1)} %across.1.across_in, f32[128,2,128]{2,1,0:T(2,128)S(1)} %all-to-all-done.1.sums_in, f32[1]{0:T(128)S(6)} %copy.21.sigma.sigma_in, s32[128]{0:T(128)S(1)} %get-tuple-element.28.slot_in, ...), custom_call_target="tpu_custom_call" | custom-call | tf_op jit(solution)/shard_map/difference/pallas_call | solution.py:550
  82.9 0.0 copy-start.4
  82.9 9.7 %all-to-all-start.2 = ((bf16[64,4,8,512]{3,2,1,0:T(8,128)(2,1)}), bf16[64,4,8,512]{3,2,1,0:T(8,128)(2,1)S(1)}, u32[]{:S(2)}, u32[]{:S(2)}) async-start(bf16[64,4,8,512]{3,2,1,0:T(8,128)(2,1)} %bitcast.19), calls=%async_computation.2 | async-start | bytes 4194304 | tf_op jit(solution)/shard_map/all_to_all | solution.py:706
  92.7 0.6 fusion
  94.6 0.0 copy-done.4
  94.6 0.0 copy-start.14
  94.6 6.1 %cut_stamps.1 = bf16[16,8,128]{2,1,0:T(8,128)(2,1)S(1)} custom-call(bf16[128,8,512]{2,1,0:T(8,128)(2,1)S(1)} %copy-done.4, s32[16]{0:T(128)S(1)} %copy-done.15, s32[16]{0:T(128)S(1)} %copy-done.16), custom_call_target="tpu_custom_call" | custom-call | flops 100000000 | bytes 3000000 | tf_op jit(solution)/shard_map/cut_stamps/pallas_call | solution.py:594
  100.7 0.6 copy.20
  101.3 0.5 slice_bitcast_fusion
  101.8 18.3 %all-to-all-done.2 = bf16[64,4,8,512]{3,2,1,0:T(8,128)(2,1)S(1)} async-done(((bf16[64,4,8,512]{3,2,1,0:T(8,128)(2,1)}), bf16[64,4,8,512]{3,2,1,0:T(8,128)(2,1)S(1)}, u32[]{:S(2)}, u32[]{:S(2)}) %all-to-all-start.2) | async-done | bytes 2097184 | tf_op jit(solution)/shard_map/all_to_all | solution.py:706
  120.1 3.1 %collective-permute-start.1 = (bf16[8,512]{1,0:T(8,128)(2,1)S(1)}, bf16[8,512]{1,0:T(8,128)(2,1)S(1)}, u32[]{:S(2)}, u32[]{:S(2)}) collective-permute-start(bf16[8,512]{1,0:T(8,128)(2,1)S(1)} %dynamic-slice_bitcast_fusion), channel_id=1, source_target_pairs={{0,1},{1,0},{2,3},{3,2},{4,5},{5,4},{6,7},{7,6},{8,9},{9,8},{10,11... | collective-permute-start | bytes 24584 | tf_op jit(solution)/shard_map/ppermute | solution.py:711
  123.2 2.1 %smooth.1.smoothed = bf16[1024,512]{1,0:T(8,128)(2,1)S(1)} custom-call(bf16[256,8,512]{2,1,0:T(8,128)(2,1)S(1)} %bitcast.16, s32[128]{0:T(128)S(1)} %get-tuple-element.33.pick, bf16[3,128,128]{2,1,0:T(8,128)(2,1)S(1)} %get-tuple-element.34.blocks.cblocks), custom_call_target="tpu_custom_call" | custom-call | flops 536870912 | bytes 3000000 | tf_op jit(solution)/shard_map/smooth/pallas_call | solution.py:624
  125.3 0.0 collective-permute-done.1.near
  125.3 0.0 copy-done.14
  125.3 1.8 %filter_rows.1 = f32[1024,512]{1,0:T(8,128)} custom-call(bf16[1024,512]{1,0:T(8,128)(2,1)S(1)} %smooth.1.smoothed, bf16[8,512]{1,0:T(8,128)(2,1)S(1)} %collective-permute-done.1.near, bf16[3,128,128]{2,1,0:T(8,128)(2,1)S(1)} %get-tuple-element.34.blocks.cblocks, bf16[2,128,128]{2,1,0:T(8,128)(2,1)S(1)} %copy-done.14), custom_call_target="tpu_custom_call" | custom-call | tf_op jit(solution)/shard_map/filter_rows/pallas_call | solution.py:665
  (11 shorter events, 0.0 us)
Async XLA Ops:
  4.1 11.6 %copy-start.18 = (bf16[12,21]{1,0:T(8,128)(2,1)S(1)}, bf16[12,21]{1,0:T(8,128)(2,1)}, u32[]{:S(2)}) copy-start(bf16[12,21]{1,0:T(8,128)(2,1)} %param.16) | copy-start | bytes 1516
  4.1 11.9 %copy-start.19 = (bf16[12,21]{1,0:T(8,128)(2,1)S(1)}, bf16[12,21]{1,0:T(8,128)(2,1)}, u32[]{:S(2)}) copy-start(bf16[12,21]{1,0:T(8,128)(2,1)} %param.15) | copy-start | bytes 1516
  4.1 11.9 %copy-start.20 = (bf16[15]{0:T(256)(128)(2,1)S(1)}, bf16[15]{0:T(256)(128)(2,1)}, u32[]{:S(2)}) copy-start(bf16[15]{0:T(256)(128)(2,1)} %param.22) | copy-start | bytes 94
  4.2 11.9 %copy-start.21 = (bf16[15]{0:T(256)(128)(2,1)S(1)}, bf16[15]{0:T(256)(128)(2,1)}, u32[]{:S(2)}) copy-start(bf16[15]{0:T(256)(128)(2,1)} %param.23) | copy-start | bytes 94
  4.2 12.0 %copy-start.15 = (s32[16]{0:T(128)S(1)}, s32[16]{0:T(128)}, u32[]{:S(2)}) copy-start(s32[16]{0:T(128)} %srow.5) | copy-start | bytes 196
  4.2 12.0 %copy-start.16 = (s32[16]{0:T(128)S(1)}, s32[16]{0:T(128)}, u32[]{:S(2)}) copy-start(s32[16]{0:T(128)} %scol.5) | copy-start | bytes 196
  4.2 12.0 %copy-start.17 = (s32[128]{0:T(128)S(1)}, s32[128]{0:T(128)}, u32[]{:S(2)}) copy-start(s32[128]{0:T(128)} %shift.1) | copy-start | bytes 1540
  4.2 44.8 %all-to-all-start = ((bf16[128,9,8,128]{3,2,1,0:T(8,128)(2,1)}), bf16[128,9,8,128]{3,2,1,0:T(8,128)(2,1)S(1)}, u32[]{:S(2)}, u32[]{:S(2)}) async-start(bf16[128,9,8,128]{3,2,1,0:T(8,128)(2,1)} %pack.1), calls=%async_computation | async-start | bytes 4718592 | tf_op jit(solution)/shard_map/all_to_all | solution.py:692
  16.2 1.6 %copy-start.1 = (f32[1024,512]{1,0:T(8,128)S(1)}, f32[1024,512]{1,0:T(8,128)}, u32[]{:S(2)}) copy-start(f32[1024,512]{1,0:T(8,128)} %science_in.1) | copy-start | bytes 6291460
  28.9 1.1 copy-start.2
  30.0 1.0 copy-start.3
  31.0 0.7 copy-start.5
  31.7 0.7 copy-start.7
  32.4 0.6 copy-start.8
  33.1 0.6 copy-start.10
  33.7 0.6 copy-start.13
  49.0 4.6 %copy-start.6 = (f32[16,32,128]{2,1,0:T(8,128)S(1)}, f32[16,32,128]{2,1,0:T(8,128)}, u32[]{:S(2)}) copy-start(f32[16,32,128]{2,1,0:T(8,128)} %copy-done.5) | copy-start | bytes 786436
  49.0 4.6 %copy-start.9 = (bf16[128,384]{1,0:T(8,128)(2,1)S(1)}, bf16[128,384]{1,0:T(8,128)(2,1)}, u32[]{:S(2)}) copy-start(bf16[128,384]{1,0:T(8,128)(2,1)} %copy-done.8) | copy-start | bytes 294916
  49.0 4.6 %copy-start.11 = (bf16[3,128,64]{2,1,0:T(8,128)(2,1)S(1)}, bf16[3,128,64]{2,1,0:T(8,128)(2,1)}, u32[]{:S(2)}) copy-start(bf16[3,128,64]{2,1,0:T(8,128)(2,1)} %copy-done.10) | copy-start | bytes 147460
  51.6 10.6 %copy-start = (bf16[1024,512]{1,0:T(8,128)(2,1)}, bf16[1024,512]{1,0:T(8,128)(2,1)S(1)}, u32[]{:S(2)}) copy-start(bf16[1024,512]{1,0:T(8,128)(2,1)S(1)} %get-tuple-element.21.image) | copy-start | bytes 3145732
  51.6 2.0 %collective-permute-start = (bf16[16,512]{1,0:T(8,128)(2,1)S(1)}, bf16[16,512]{1,0:T(8,128)(2,1)S(1)}, u32[]{:S(2)}, u32[]{:S(2)}) collective-permute-start(bf16[16,512]{1,0:T(8,128)(2,1)S(1)} %get-tuple-element.22), channel_id=1, source_target_pairs={{0,1},{1,0},{2,3},{3,2},{4,5},{5,4},{6,7},{7,6},{8,9},{9,8},{10,11... | collective-permute-start | bytes 49160 | tf_op jit(solution)/shard_map/ppermute | solution.py:697
  53.5 8.6 %copy-start.12 = (bf16[16,512]{1,0:T(8,128)(2,1)}, bf16[16,512]{1,0:T(8,128)(2,1)S(1)}, u32[]{:S(2)}) copy-start(bf16[16,512]{1,0:T(8,128)(2,1)S(1)} %collective-permute-done.near) | copy-start | bytes 49156
  58.4 13.8 %all-to-all-start.1 = ((f32[128,2,128]{2,1,0:T(2,128)}), f32[128,2,128]{2,1,0:T(2,128)S(1)}, u32[]{:S(2)}, u32[]{:S(2)}) async-start(f32[128,2,128]{2,1,0:T(2,128)} %stamp_sums.1), calls=%async_computation.1 | async-start | bytes 262144 | tf_op jit(solution)/shard_map/all_to_all | solution.py:701
  82.9 11.6 %copy-start.4 = (bf16[128,8,512]{2,1,0:T(8,128)(2,1)S(1)}, bf16[128,8,512]{2,1,0:T(8,128)(2,1)}, u32[]{:S(2)}) copy-start(bf16[128,8,512]{2,1,0:T(8,128)(2,1)} %get-tuple-element.30.diff) | copy-start | bytes 3145732
  82.9 37.2 %all-to-all-start.2 = ((bf16[64,4,8,512]{3,2,1,0:T(8,128)(2,1)}), bf16[64,4,8,512]{3,2,1,0:T(8,128)(2,1)S(1)}, u32[]{:S(2)}, u32[]{:S(2)}) async-start(bf16[64,4,8,512]{3,2,1,0:T(8,128)(2,1)} %bitcast.19), calls=%async_computation.2 | async-start | bytes 4194304 | tf_op jit(solution)/shard_map/all_to_all | solution.py:706
  94.6 30.8 %copy-start.14 = (bf16[2,128,128]{2,1,0:T(8,128)(2,1)S(1)}, bf16[2,128,128]{2,1,0:T(8,128)(2,1)}, u32[]{:S(2)}) copy-start(bf16[2,128,128]{2,1,0:T(8,128)(2,1)} %copy-done.13) | copy-start | bytes 196612
  120.1 5.2 %collective-permute-start.1 = (bf16[8,512]{1,0:T(8,128)(2,1)S(1)}, bf16[8,512]{1,0:T(8,128)(2,1)S(1)}, u32[]{:S(2)}, u32[]{:S(2)}) collective-permute-start(bf16[8,512]{1,0:T(8,128)(2,1)S(1)} %dynamic-slice_bitcast_fusion), channel_id=1, source_target_pairs={{0,1},{1,0},{2,3},{3,2},{4,5},{5,4},{6,7},{7,6},{8,9},{9,8},{10,11... | collective-permute-start | bytes 24584 | tf_op jit(solution)/shard_map/ppermute | solution.py:711

commit v5 on v4

--- a/solution.py
+++ b/solution.py
@@ -458,7 +458,7 @@
             pltpu.VMEM((4, FRAMED, COLS), BF16),
             pltpu.SemaphoreType.DMA((4,)),
         ],
-        compiler_params=params(54),
+        compiler_params=params(50),
         cost_estimate=cost(BASIS * FRAMED * COLS * COLS, 16 * 10**6),
         name="across",
     )(image, near, blocks, seam)
@@ -479,7 +479,7 @@
 
 def difference_body(
     across_in, sums_in, sigma_in, slot_in, table_in, science_in, coef_out, diff_out, leave_out,
-    across, table, science, sums, sigma, slot, coef, bands, sems, load_sems, save_sems,
+    across, table, science, sums, sigma, slot, coef, bands, sems, load_sems, sky_sems, save_sems,
 ):
     ends = [0] + [first + span for first, _, span in BLOCKS]
 
@@ -494,7 +494,16 @@
         for i, (src, dst) in enumerate([(sums_in, sums), (sigma_in, sigma), (slot_in, slot)])
     ]
     table_load = pltpu.make_async_copy(table_in, table, sems.at[3])
-    science_load = pltpu.make_async_copy(science_in, science, sems.at[4])
+
+    def sky_load(i):
+        some = pl.ds(BLOCKS[i][0], BLOCKS[i][1])
+        return pltpu.make_async_copy(science_in.at[some], science.at[some], sky_sems.at[i])
+
+    def ahead(i):
+        if i < len(BLOCKS):
+            load(i).start()
+            sky_load(i).start()
+
     for one in small:
         one.start()
     load(0).start()
@@ -505,13 +514,14 @@
     coef[...] = jnp.broadcast_to(found, coef.shape)
     eye = iota((16, 128), 0) == iota((16, 128), 1)
     coef_out[...] = jnp.sum(jnp.where(eye, found, 0.0), axis=0, keepdims=True)
-    science_load.start()
-    for i in range(1, len(BLOCKS)):
-        load(i).start()
+    sky_load(0).start()
+    for i in range(1, 2):
+        ahead(i)
     scale = 1.0 / sigma[0]
     saves = []
     for i, (first, rows, span) in enumerate(BLOCKS):
         load(i).wait()
+        ahead(i + 2)
         if i == 0:
             table_load.wait()
         for h in range(0, COLS, 256):
@@ -524,8 +534,8 @@
                 )
                 term = coef[b : b + 1, :] * basis.astype(BF16).astype(F32)
                 model = term if model is None else model + term
-            if i == 0 and h == 0:
-                science_load.wait()
+            if h == 0:
+                sky_load(i).wait()
             left = (science[first : first + rows, h : h + 256] - model) * scale
             bands[first // 8 : (first + rows) // 8, :, h : h + 256] = left.reshape(
                 rows // 8, 8, 256
@@ -565,7 +575,8 @@
             pltpu.SMEM(slot.shape, I32),
             pltpu.VMEM((16, 256), F32),
             pltpu.VMEM((ROWS // 8, 8, COLS), BF16),
-            pltpu.SemaphoreType.DMA((5,)),
+            pltpu.SemaphoreType.DMA((4,)),
+            pltpu.SemaphoreType.DMA((len(BLOCKS),)),
             pltpu.SemaphoreType.DMA((len(BLOCKS),)),
             pltpu.SemaphoreType.DMA((1 + len(BLOCKS),)),
         ],

time: 128 us -> 125 us (0.977)
  Pallas kernels: 51.7 us -> 48.2 us
    pallas_call x1, Pallas kernels: 10.7 us -> 8.84 us  [difference_all(): pl.pallas_call(difference_body, out_shape=(shape((1, 128), F32), shape((R...]
    pallas_call x1, Pallas kernels: 8.91 us -> 7.29 us  [across_all(): pl.pallas_call(across_body, out_shape=shape((BASIS, FRAMED, COLS), BF16),...]
  transfers between devices with their start and end apart: 5 -> 5, of which waited for: 4 -> 4; matrix products, arithmetic and copies ran while one was open for 2% -> 2% of each run, Pallas kernels for 22% -> 21%
where the time goes in v5:
time: 125 us
  Pallas kernels  48.2 us (39%)
  waiting for transfers between devices  35 us (28%)
  starting transfers between devices  28.5 us (23%)
  local copies, waits for them, and re-layouts  10 us (8%)
  between operations  3.08 us (2%)
    all_to_all x1, waiting for transfers between devices, shards(): lax.all_to_all(leaving.reshape(ccds, cap, 8, COLS), 'ccd', split_axis=0,...  18.3 us
    all_to_all x1, waiting for transfers between devices, shards(): lax.all_to_all(outgoing, BOTH, split_axis=0, concat_axis=0, tiled=True)  14.7 us
    all_to_all x1, starting transfers between devices, shards(): lax.all_to_all(outgoing, BOTH, split_axis=0, concat_axis=0, tiled=True)  11.5 us
    pallas_call x1, Pallas kernels, tables(): pl.pallas_call(tables_body, out_shape=(shape((BASIS, 3, 128, 128), BF16),...  11.2 us
    all_to_all x1, starting transfers between devices, shards(): lax.all_to_all(leaving.reshape(ccds, cap, 8, COLS), 'ccd', split_axis=0,...  9.01 us
    pallas_call x1, Pallas kernels, difference_all(): pl.pallas_call(difference_body, out_shape=(shape((1, 128), F32), shape((R...  8.84 us
    unnamed x45, local copies, waits for them, and re-layouts  8.6 us
    pallas_call x1, Pallas kernels, across_all(): pl.pallas_call(across_body, out_shape=shape((BASIS, FRAMED, COLS), BF16),...  7.29 us
  transfers between devices with their start and end apart: 5, of which 4 were waited for; matrix products, arithmetic and copies ran while one was open for 2% of the time, Pallas kernels for 21%

profile of v5, /device:TPU:1, one launch (start us, length us, event | category | flops | bytes accessed | tf_op | source)
XLA Modules:
  0.0 124.8 jit_solution(16187492191184885796)
XLA Ops:
  0.6 3.5 %pack.1 = bf16[128,9,8,128]{3,2,1,0:T(8,128)(2,1)} custom-call(s32[128]{0:T(128)} %dest_in.1, s32[128]{0:T(128)} %row_in.1, bf16[128,8,512]{2,1,0:T(8,128)(2,1)} %pieces_in.1), custom_call_target="tpu_custom_call" | custom-call | tf_op jit(solution)/shard_map/pack/pallas_call | solution.py:114
  4.1 0.0 copy-start.18
  4.1 0.0 copy-start.19
  4.1 0.0 copy-start.20
  4.2 0.0 copy-start.21
  4.2 0.0 copy-start.15
  4.2 0.0 copy-start.16
  4.2 0.0 copy-start.17
  4.2 11.5 %all-to-all-start = ((bf16[128,9,8,128]{3,2,1,0:T(8,128)(2,1)}), bf16[128,9,8,128]{3,2,1,0:T(8,128)(2,1)S(1)}, u32[]{:S(2)}, u32[]{:S(2)}) async-start(bf16[128,9,8,128]{3,2,1,0:T(8,128)(2,1)} %pack.1), calls=%async_computation | async-start | bytes 4718592 | tf_op jit(solution)/shard_map/all_to_all | solution.py:703
  15.7 0.0 copy-done.18
  15.7 0.1 copy.17
  15.8 0.1 broadcast_in_dim.3
  15.9 0.1 reshape.23
  16.1 0.0 copy-done.19
  16.1 0.0 copy-done.20
  16.1 0.0 copy-done.21
  16.1 0.0 copy-done.15
  16.1 0.0 copy-done.16
  16.2 0.0 copy-done.17
  16.2 0.0 copy-start
  16.2 1.6 %copy-done = f32[1024,512]{1,0:T(8,128)S(1)} copy-done((f32[1024,512]{1,0:T(8,128)S(1)}, f32[1024,512]{1,0:T(8,128)}, u32[]{:S(2)}) %copy-start) | copy-done | bytes 2097176
  17.8 11.2 %tables.1 = (bf16[12,3,128,128]{3,2,1,0:T(8,128)(2,1)S(1)}, bf16[12,224,256]{2,1,0:T(8,128)(2,1)S(1)}, bf16[3,128,128]{2,1,0:T(8,128)(2,1)S(1)}, bf16[2,128,128]...) custom-call(f32[12,21]{1,0:T(8,128)S(1)} %convert_element_type.14.kr, ...), custom_call_target="tpu_custom_call" | custom-call | flops 2000000000 | bytes 4000000 | tf_op jit(solution)/shard_map/tables/pallas_call | solution.py:234
  28.9 0.0 copy-start.1
  28.9 1.1 copy-done.1
  30.0 0.0 copy-start.2
  30.0 1.0 copy-done.2
  31.0 0.0 copy-start.5
  31.0 0.7 copy-done.5
  31.7 0.0 copy-start.7
  31.7 0.7 copy-done.7
  32.4 0.0 copy-start.9
  32.4 0.6 copy-done.9
  33.1 0.6 copy-done.11
  33.7 0.6 copy-done.13
  34.3 14.7 %all-to-all-done.arrived = bf16[128,9,8,128]{3,2,1,0:T(8,128)(2,1)S(1)} async-done(((bf16[128,9,8,128]{3,2,1,0:T(8,128)(2,1)}), bf16[128,9,8,128]{3,2,1,0:T(8,128)(2,1)S(1)}, u32[]{:S(2)}, u32[]{:S(2)}) %all-to-all-start) | async-done | bytes 2359328 | tf_op jit(solution)/shard_map/all_to_all | solution.py:703
  49.0 2.6 %coadd.1 = (bf16[1024,512]{1,0:T(8,128)(2,1)S(1)}, bf16[16,512]{1,0:T(8,128)(2,1)S(1)}) custom-call(bf16[128,9,8,128]{3,2,1,0:T(8,128)(2,1)S(1)} %all-to-all-done.arrived, f32[8,128]{1,0:T(8,128)S(1)} %get-tuple-element.20.ready), custom_call_target="tpu_custom_call" | custom-call | tf_op jit(solution)/shard_map/coadd/pallas_call | solution.py:290
  51.6 0.0 copy-start.3
  51.6 1.1 collective-permute-start
  53.4 0.2 collective-permute-done.near
  53.5 0.0 copy-done.6
  53.5 0.0 copy-done.10
  53.6 0.0 copy-done.12
  53.6 4.9 %stamp_sums.1 = f32[128,2,128]{2,1,0:T(2,128)} custom-call(bf16[1024,512]{1,0:T(8,128)(2,1)S(1)} %get-tuple-element.21.image, bf16[16,512]{1,0:T(8,128)(2,1)S(1)} %collective-permute-done.near, f32[1]{0:T(128)S(6)} %copy.21.sigma.sigma_in, s32[16]{0:T(128)S(1)} %copy-done.15, s32[16]{0:T(128)S(1)} %copy-done.16, bf16[128,384]{1,0:T(8,128)(2,1)S(1)} %copy-done.10, ...), custom_call_target="tpu_custom_call" | custom-call | tf_op jit(solution)/shard_map/stamp_sums/pallas_call | solution.py:375
  58.4 3.8 %all-to-all-start.1 = ((f32[128,2,128]{2,1,0:T(2,128)}), f32[128,2,128]{2,1,0:T(2,128)S(1)}, u32[]{:S(2)}, u32[]{:S(2)}) async-start(f32[128,2,128]{2,1,0:T(2,128)} %stamp_sums.1), calls=%async_computation.1 | async-start | bytes 262144 | tf_op jit(solution)/shard_map/all_to_all | solution.py:712
  62.2 0.0 copy-done.3
  62.2 0.0 copy-start.8
  62.2 0.9 copy-done.8
  63.1 7.3 %across.1.across_in = bf16[12,1056,512]{2,1,0:T(8,128)(2,1)} custom-call(bf16[1024,512]{1,0:T(8,128)(2,1)S(1)} %get-tuple-element.21.image, bf16[16,512]{1,0:T(8,128)(2,1)S(1)} %collective-permute-done.near, bf16[12,3,128,128]{3,2,1,0:T(8,128)(2,1)S(1)} %copy-done.3, bf16[256,384]{1,0:T(8,128)(2,1)S(1)} %copy-done.8), custom_call_target="tpu_custom_call" | custom-call | flops 3321888768 | bytes 16000000 | tf_op jit(solution)/shard_map/across/pallas_call | solution.py:449
  70.4 1.8 %all-to-all-done.1.sums_in = f32[128,2,128]{2,1,0:T(2,128)S(1)} async-done(((f32[128,2,128]{2,1,0:T(2,128)}), f32[128,2,128]{2,1,0:T(2,128)S(1)}, u32[]{:S(2)}, u32[]{:S(2)}) %all-to-all-start.1) | async-done | bytes 131104 | tf_op jit(solution)/shard_map/all_to_all | solution.py:712
  72.3 8.8 %difference.1 = (f32[1,128]{1,0:T(1,128)S(1)}, bf16[128,8,512]{2,1,0:T(8,128)(2,1)}, bf16[256,8,512]{2,1,0:T(8,128)(2,1)}) custom-call(bf16[12,1056,512]{2,1,0:T(8,128)(2,1)} %across.1.across_in, f32[128,2,128]{2,1,0:T(2,128)S(1)} %all-to-all-done.1.sums_in, f32[1]{0:T(128)S(6)} %copy.21.sigma.sigma_in, s32[128]{0:T(128)S(1)} %get-tuple-element.28.slot_in, ...), custom_call_target="tpu_custom_call" | custom-call | tf_op jit(solution)/shard_map/difference/pallas_call | solution.py:560
  81.1 0.0 copy-start.4
  81.2 9.0 %all-to-all-start.2 = ((bf16[64,4,8,512]{3,2,1,0:T(8,128)(2,1)}), bf16[64,4,8,512]{3,2,1,0:T(8,128)(2,1)S(1)}, u32[]{:S(2)}, u32[]{:S(2)}) async-start(bf16[64,4,8,512]{3,2,1,0:T(8,128)(2,1)} %bitcast.19), calls=%async_computation.2 | async-start | bytes 4194304 | tf_op jit(solution)/shard_map/all_to_all | solution.py:717
  90.2 0.6 fusion
  92.1 0.0 copy-done.4
  92.1 0.0 copy-start.14
  92.1 6.1 %cut_stamps.1 = bf16[16,8,128]{2,1,0:T(8,128)(2,1)S(1)} custom-call(bf16[128,8,512]{2,1,0:T(8,128)(2,1)S(1)} %copy-done.4, s32[16]{0:T(128)S(1)} %copy-done.15, s32[16]{0:T(128)S(1)} %copy-done.16), custom_call_target="tpu_custom_call" | custom-call | flops 100000000 | bytes 3000000 | tf_op jit(solution)/shard_map/cut_stamps/pallas_call | solution.py:605
  98.2 0.6 copy.20
  98.8 0.5 slice_bitcast_fusion
  99.3 18.3 %all-to-all-done.2 = bf16[64,4,8,512]{3,2,1,0:T(8,128)(2,1)S(1)} async-done(((bf16[64,4,8,512]{3,2,1,0:T(8,128)(2,1)}), bf16[64,4,8,512]{3,2,1,0:T(8,128)(2,1)S(1)}, u32[]{:S(2)}, u32[]{:S(2)}) %all-to-all-start.2) | async-done | bytes 2097184 | tf_op jit(solution)/shard_map/all_to_all | solution.py:717
  117.6 3.1 %collective-permute-start.1 = (bf16[8,512]{1,0:T(8,128)(2,1)S(1)}, bf16[8,512]{1,0:T(8,128)(2,1)S(1)}, u32[]{:S(2)}, u32[]{:S(2)}) collective-permute-start(bf16[8,512]{1,0:T(8,128)(2,1)S(1)} %dynamic-slice_bitcast_fusion), channel_id=1, source_target_pairs={{0,1},{1,0},{2,3},{3,2},{4,5},{5,4},{6,7},{7,6},{8,9},{9,8},{10,11... | collective-permute-start | bytes 24584 | tf_op jit(solution)/shard_map/ppermute | solution.py:722
  120.7 2.1 %smooth.1.smoothed = bf16[1024,512]{1,0:T(8,128)(2,1)S(1)} custom-call(bf16[256,8,512]{2,1,0:T(8,128)(2,1)S(1)} %bitcast.16, s32[128]{0:T(128)S(1)} %get-tuple-element.33.pick, bf16[3,128,128]{2,1,0:T(8,128)(2,1)S(1)} %get-tuple-element.34.blocks.cblocks), custom_call_target="tpu_custom_call" | custom-call | flops 536870912 | bytes 3000000 | tf_op jit(solution)/shard_map/smooth/pallas_call | solution.py:635
  122.8 0.0 collective-permute-done.1.near
  122.8 0.0 copy-done.14
  122.8 1.8 %filter_rows.1 = f32[1024,512]{1,0:T(8,128)} custom-call(bf16[1024,512]{1,0:T(8,128)(2,1)S(1)} %smooth.1.smoothed, bf16[8,512]{1,0:T(8,128)(2,1)S(1)} %collective-permute-done.1.near, bf16[3,128,128]{2,1,0:T(8,128)(2,1)S(1)} %get-tuple-element.34.blocks.cblocks, bf16[2,128,128]{2,1,0:T(8,128)(2,1)S(1)} %copy-done.14), custom_call_target="tpu_custom_call" | custom-call | tf_op jit(solution)/shard_map/filter_rows/pallas_call | solution.py:676
  (11 shorter events, 0.0 us)
Async XLA Ops:
  4.1 11.6 %copy-start.18 = (bf16[12,21]{1,0:T(8,128)(2,1)S(1)}, bf16[12,21]{1,0:T(8,128)(2,1)}, u32[]{:S(2)}) copy-start(bf16[12,21]{1,0:T(8,128)(2,1)} %param.16) | copy-start | bytes 1516
  4.1 11.9 %copy-start.19 = (bf16[12,21]{1,0:T(8,128)(2,1)S(1)}, bf16[12,21]{1,0:T(8,128)(2,1)}, u32[]{:S(2)}) copy-start(bf16[12,21]{1,0:T(8,128)(2,1)} %param.15) | copy-start | bytes 1516
  4.1 11.9 %copy-start.20 = (bf16[15]{0:T(256)(128)(2,1)S(1)}, bf16[15]{0:T(256)(128)(2,1)}, u32[]{:S(2)}) copy-start(bf16[15]{0:T(256)(128)(2,1)} %param.22) | copy-start | bytes 94
  4.2 11.9 %copy-start.21 = (bf16[15]{0:T(256)(128)(2,1)S(1)}, bf16[15]{0:T(256)(128)(2,1)}, u32[]{:S(2)}) copy-start(bf16[15]{0:T(256)(128)(2,1)} %param.23) | copy-start | bytes 94
  4.2 12.0 %copy-start.15 = (s32[16]{0:T(128)S(1)}, s32[16]{0:T(128)}, u32[]{:S(2)}) copy-start(s32[16]{0:T(128)} %srow.5) | copy-start | bytes 196
  4.2 12.0 %copy-start.16 = (s32[16]{0:T(128)S(1)}, s32[16]{0:T(128)}, u32[]{:S(2)}) copy-start(s32[16]{0:T(128)} %scol.5) | copy-start | bytes 196
  4.2 12.0 %copy-start.17 = (s32[128]{0:T(128)S(1)}, s32[128]{0:T(128)}, u32[]{:S(2)}) copy-start(s32[128]{0:T(128)} %shift.1) | copy-start | bytes 1540
  4.2 44.8 %all-to-all-start = ((bf16[128,9,8,128]{3,2,1,0:T(8,128)(2,1)}), bf16[128,9,8,128]{3,2,1,0:T(8,128)(2,1)S(1)}, u32[]{:S(2)}, u32[]{:S(2)}) async-start(bf16[128,9,8,128]{3,2,1,0:T(8,128)(2,1)} %pack.1), calls=%async_computation | async-start | bytes 4718592 | tf_op jit(solution)/shard_map/all_to_all | solution.py:703
  16.2 1.6 %copy-start = (f32[1024,512]{1,0:T(8,128)S(1)}, f32[1024,512]{1,0:T(8,128)}, u32[]{:S(2)}) copy-start(f32[1024,512]{1,0:T(8,128)} %science_in.1) | copy-start | bytes 6291460
  28.9 1.1 copy-start.1
  30.0 1.0 copy-start.2
  31.0 0.7 copy-start.5
  31.7 0.7 copy-start.7
  32.4 0.6 copy-start.9
  33.0 0.6 copy-start.11
  33.7 0.6 copy-start.13
  49.0 4.6 %copy-start.6 = (f32[16,32,128]{2,1,0:T(8,128)S(1)}, f32[16,32,128]{2,1,0:T(8,128)}, u32[]{:S(2)}) copy-start(f32[16,32,128]{2,1,0:T(8,128)} %copy-done.5) | copy-start | bytes 786436
  49.0 4.6 %copy-start.10 = (bf16[128,384]{1,0:T(8,128)(2,1)S(1)}, bf16[128,384]{1,0:T(8,128)(2,1)}, u32[]{:S(2)}) copy-start(bf16[128,384]{1,0:T(8,128)(2,1)} %copy-done.9) | copy-start | bytes 294916
  49.0 4.6 %copy-start.12 = (bf16[3,128,64]{2,1,0:T(8,128)(2,1)S(1)}, bf16[3,128,64]{2,1,0:T(8,128)(2,1)}, u32[]{:S(2)}) copy-start(bf16[3,128,64]{2,1,0:T(8,128)(2,1)} %copy-done.11) | copy-start | bytes 147460
  51.6 10.6 %copy-start.3 = (bf16[12,3,128,128]{3,2,1,0:T(8,128)(2,1)S(1)}, bf16[12,3,128,128]{3,2,1,0:T(8,128)(2,1)}, u32[]{:S(2)}) copy-start(bf16[12,3,128,128]{3,2,1,0:T(8,128)(2,1)} %copy-done.2) | copy-start | bytes 3538948
  51.6 2.0 %collective-permute-start = (bf16[16,512]{1,0:T(8,128)(2,1)S(1)}, bf16[16,512]{1,0:T(8,128)(2,1)S(1)}, u32[]{:S(2)}, u32[]{:S(2)}) collective-permute-start(bf16[16,512]{1,0:T(8,128)(2,1)S(1)} %get-tuple-element.22), channel_id=1, source_target_pairs={{0,1},{1,0},{2,3},{3,2},{4,5},{5,4},{6,7},{7,6},{8,9},{9,8},{10,11... | collective-permute-start | bytes 49160 | tf_op jit(solution)/shard_map/ppermute | solution.py:708
  58.4 13.9 %all-to-all-start.1 = ((f32[128,2,128]{2,1,0:T(2,128)}), f32[128,2,128]{2,1,0:T(2,128)S(1)}, u32[]{:S(2)}, u32[]{:S(2)}) async-start(f32[128,2,128]{2,1,0:T(2,128)} %stamp_sums.1), calls=%async_computation.1 | async-start | bytes 262144 | tf_op jit(solution)/shard_map/all_to_all | solution.py:712
  62.2 0.9 copy-start.8
  81.1 10.9 %copy-start.4 = (bf16[128,8,512]{2,1,0:T(8,128)(2,1)S(1)}, bf16[128,8,512]{2,1,0:T(8,128)(2,1)}, u32[]{:S(2)}) copy-start(bf16[128,8,512]{2,1,0:T(8,128)(2,1)} %get-tuple-element.30.diff) | copy-start | bytes 3145732
  81.2 36.5 %all-to-all-start.2 = ((bf16[64,4,8,512]{3,2,1,0:T(8,128)(2,1)}), bf16[64,4,8,512]{3,2,1,0:T(8,128)(2,1)S(1)}, u32[]{:S(2)}, u32[]{:S(2)}) async-start(bf16[64,4,8,512]{3,2,1,0:T(8,128)(2,1)} %bitcast.19), calls=%async_computation.2 | async-start | bytes 4194304 | tf_op jit(solution)/shard_map/all_to_all | solution.py:717
  92.1 30.8 %copy-start.14 = (bf16[2,128,128]{2,1,0:T(8,128)(2,1)S(1)}, bf16[2,128,128]{2,1,0:T(8,128)(2,1)}, u32[]{:S(2)}) copy-start(bf16[2,128,128]{2,1,0:T(8,128)(2,1)} %copy-done.13) | copy-start | bytes 196612
  117.6 5.2 %collective-permute-start.1 = (bf16[8,512]{1,0:T(8,128)(2,1)S(1)}, bf16[8,512]{1,0:T(8,128)(2,1)S(1)}, u32[]{:S(2)}, u32[]{:S(2)}) collective-permute-start(bf16[8,512]{1,0:T(8,128)(2,1)S(1)} %dynamic-slice_bitcast_fusion), channel_id=1, source_target_pairs={{0,1},{1,0},{2,3},{3,2},{4,5},{5,4},{6,7},{7,6},{8,9},{9,8},{10,11... | collective-permute-start | bytes 24584 | tf_op jit(solution)/shard_map/ppermute | solution.py:722

commit v6 on v5

--- a/solution.py
+++ b/solution.py
@@ -150,7 +150,7 @@
 
 def tables_body(
     kr, kc, pr, pc, kcl, shift, srow, scol, science,
-    cols_out, rows_out, pcols_out, prows_out, stamp_out, ready_out, down_out, seam_out,
+    cols_out, rows_out, pcols_out, prows_out, stamp_out, ready_out, down_out,
     slot_out, pick_out, sky_out, count,
 ):
     for b in range(BASIS):
@@ -187,7 +187,7 @@
             for t in range(KTAPS):
                 table = jnp.where(lag == t, kr[4 * q + g, t], table)
             down_out[q, 32 * g : 32 * g + 32] = table.astype(BF16)
-    seam_out[...] = jnp.zeros(seam_out.shape, BF16)
+    nothing = jnp.zeros((112, 128), F32)
     place = ((iota((32, 128), 1) + 16) & 31) - 16
     source = iota((32, 128), 0) - 16
     crosses = (place >= -10) & (place < 10) & ((place < 0) != (source < 0))
@@ -197,7 +197,8 @@
         table = jnp.zeros((32, 128), F32)
         for t in range(KTAPS):
             table = jnp.where(lag == t, taps[t : t + 1, :], table)
-        seam_out[112:144, 128 * v : 128 * v + 128] = table.astype(BF16)
+        cols_out[BASIS, v] = jnp.concatenate([nothing, table[:16]], axis=0).astype(BF16)
+        cols_out[BASIS + 1, v] = jnp.concatenate([table[16:], nothing], axis=0).astype(BF16)
 
     own, ccds = lax.axis_index("ccd"), lax.axis_size("ccd")
     cap = slot_out.shape[0] * 2 // ccds
@@ -234,20 +235,19 @@
     return pl.pallas_call(
         tables_body,
         out_shape=(
-            shape((BASIS, 3, 128, 128), BF16),
+            shape((BASIS + 2, 3, 128, 128), BF16),
             shape((BASIS, STEP, SPAN), BF16),
             shape((3, 128, 128), BF16),
             shape((2, 128, 128), BF16),
             shape((128, LANES), BF16),
             shape((8, 128), F32),
             shape((3, 128, WIN), BF16),
-            shape((256, LANES), BF16),
             shape(band_shift.shape, I32),
             shape(band_shift.shape, I32),
             shape((STAMPS, 32, 128), F32),
         ),
         in_specs=[smem()] * 4 + [vmem()] + [smem()] * 3 + [vmem()],
-        out_specs=(vmem(),) * 8 + (smem(),) * 2 + (vmem(),),
+        out_specs=(vmem(),) * 7 + (smem(),) * 2 + (vmem(),),
         scratch_shapes=[pltpu.SMEM((64,), I32)],
         compiler_params=params(16),
         cost_estimate=cost(2 * 10**9, 4 * 10**6),
@@ -397,13 +397,13 @@
                 wide[128 * i : 128 * i + 128, 128 * o : 128 * o + 128] = jnp.zeros((128, 128), BF16)
 
 
-def across_body(image, near, blocks, seam, out, framed, wide, border, held, sems):
+def across_body(image, near, blocks, out, framed, wide, border, held, sems):
     frame(framed, image, near)
     for m in range(0, FRAMED, 352):
         for v in range(3):
             border[v, m : m + 352] = jnp.dot(
                 framed[m : m + 352, 128:384],
-                seam[:, 128 * v : 128 * v + 128],
+                jnp.concatenate([blocks[BASIS, v], blocks[BASIS + 1, v]], axis=0),
                 preferred_element_type=F32,
             )
     lane = iota((352, 128), 1)
@@ -445,11 +445,11 @@
         save(BASIS - 4 + g, g).wait()
 
 
-def across_all(image, near, blocks, seam):
+def across_all(image, near, blocks):
     return pl.pallas_call(
         across_body,
         out_shape=shape((BASIS, FRAMED, COLS), BF16),
-        in_specs=[vmem()] * 4,
+        in_specs=[vmem()] * 3,
         out_specs=hbm(),
         scratch_shapes=[
             pltpu.VMEM((FRAMED, COLS), BF16),
@@ -461,7 +461,7 @@
         compiler_params=params(50),
         cost_estimate=cost(BASIS * FRAMED * COLS * COLS, 16 * 10**6),
         name="across",
-    )(image, near, blocks, seam)
+    )(image, near, blocks)
 
 
 def solve(sums):
@@ -701,7 +701,7 @@
     cap = 2 * bands // ccds
     outgoing = pack(route_dest, route_row, template, devices)
     arrived = lax.all_to_all(outgoing, BOTH, split_axis=0, concat_axis=0, tiled=True)
-    cols, rows, pcols, prows, stamp_table, ready, down, seam, slot, pick, sky = tables(
+    cols, rows, pcols, prows, stamp_table, ready, down, slot, pick, sky = tables(
         kern_row, kern_col, psf_row, psf_col, band_shift, stamp_row, stamp_col, science
     )
     image, edge = coadd(arrived, ready)
@@ -710,7 +710,7 @@
         image, near, noise_sigma, stamp_row, stamp_col, stamp_table, down, sky, devices
     )
     sums = lax.all_to_all(sums, BOTH, split_axis=0, concat_axis=0, tiled=True)
-    across = across_all(image, near, cols, seam)
+    across = across_all(image, near, cols)
     coef, diff, leaving = difference_all(
         sums, across, rows, science, noise_sigma, slot, ccds * cap
     )

time: 125 us -> 124 us (level)
  waiting for transfers between devices: 35 us -> 36.6 us
  local copies, waits for them, and re-layouts: 10 us -> 8.44 us
    unnamed x45 -> x41, local copies, waits for them, and re-layouts: 8.6 us -> 7.04 us
where the time goes in v6:
time: 124 us
  Pallas kernels  48.2 us (39%)
  waiting for transfers between devices  36.6 us (30%)
  starting transfers between devices  27.6 us (22%)
  local copies, waits for them, and re-layouts  8.44 us (7%)
  between operations  3.07 us (2%)
    all_to_all x1, waiting for transfers between devices, shards(): lax.all_to_all(leaving.reshape(ccds, cap, 8, COLS), 'ccd', split_axis=0,...  18.3 us
    all_to_all x1, waiting for transfers between devices, shards(): lax.all_to_all(outgoing, BOTH, split_axis=0, concat_axis=0, tiled=True)  15.3 us
    all_to_all x1, starting transfers between devices, shards(): lax.all_to_all(outgoing, BOTH, split_axis=0, concat_axis=0, tiled=True)  11.5 us
    pallas_call x1, Pallas kernels, tables(): pl.pallas_call(tables_body, out_shape=(shape((BASIS + 2, 3, 128, 128), BF...  11.2 us
    pallas_call x1, Pallas kernels, difference_all(): pl.pallas_call(difference_body, out_shape=(shape((1, 128), F32), shape((R...  8.84 us
    all_to_all x1, starting transfers between devices, shards(): lax.all_to_all(leaving.reshape(ccds, cap, 8, COLS), 'ccd', split_axis=0,...  8.07 us
    pallas_call x1, Pallas kernels, across_all(): pl.pallas_call(across_body, out_shape=shape((BASIS, FRAMED, COLS), BF16),...  7.28 us
    unnamed x41, local copies, waits for them, and re-layouts  7.04 us
  transfers between devices with their start and end apart: 5, of which 4 were waited for; matrix products, arithmetic and copies ran while one was open for 2% of the time, Pallas kernels for 21%

profile of v6, /device:TPU:1, one launch (start us, length us, event | category | flops | bytes accessed | tf_op | source)
XLA Modules:
  0.0 123.9 jit_solution(5519619112748215256)
XLA Ops:
  0.6 3.5 %pack.1 = bf16[128,9,8,128]{3,2,1,0:T(8,128)(2,1)} custom-call(s32[128]{0:T(128)} %dest_in.1, s32[128]{0:T(128)} %row_in.1, bf16[128,8,512]{2,1,0:T(8,128)(2,1)} %pieces_in.1), custom_call_target="tpu_custom_call" | custom-call | tf_op jit(solution)/shard_map/pack/pallas_call | solution.py:114
  4.1 0.0 copy-start.16
  4.1 0.0 copy-start.17
  4.1 0.0 copy-start.18
  4.2 0.0 copy-start.19
  4.2 0.0 copy-start.13
  4.2 0.0 copy-start.14
  4.2 0.0 copy-start.15
  4.2 11.5 %all-to-all-start = ((bf16[128,9,8,128]{3,2,1,0:T(8,128)(2,1)}), bf16[128,9,8,128]{3,2,1,0:T(8,128)(2,1)S(1)}, u32[]{:S(2)}, u32[]{:S(2)}) async-start(bf16[128,9,8,128]{3,2,1,0:T(8,128)(2,1)} %pack.1), calls=%async_computation | async-start | bytes 4718592 | tf_op jit(solution)/shard_map/all_to_all | solution.py:703
  15.7 0.0 copy-done.16
  15.7 0.1 copy.17
  15.8 0.1 broadcast_in_dim.3
  15.9 0.1 reshape.23
  16.0 0.0 copy-done.17
  16.1 0.0 copy-done.18
  16.1 0.0 copy-done.19
  16.1 0.0 copy-done.13
  16.1 0.0 copy-done.14
  16.1 0.0 copy-done.15
  16.2 0.0 copy-start
  16.2 1.6 %copy-done = f32[1024,512]{1,0:T(8,128)S(1)} copy-done((f32[1024,512]{1,0:T(8,128)S(1)}, f32[1024,512]{1,0:T(8,128)}, u32[]{:S(2)}) %copy-start) | copy-done | bytes 2097176
  17.8 11.2 %tables.1 = (bf16[14,3,128,128]{3,2,1,0:T(8,128)(2,1)S(1)}, bf16[12,224,256]{2,1,0:T(8,128)(2,1)S(1)}, bf16[3,128,128]{2,1,0:T(8,128)(2,1)S(1)}, bf16[2,128,128]...) custom-call(f32[12,21]{1,0:T(8,128)S(1)} %convert_element_type.14.kr, ...), custom_call_target="tpu_custom_call" | custom-call | flops 2000000000 | bytes 4000000 | tf_op jit(solution)/shard_map/tables/pallas_call | solution.py:235
  28.9 0.0 copy-start.1
  28.9 1.1 copy-done.1
  30.0 0.0 copy-start.2
  30.0 1.1 copy-done.2
  31.1 0.0 copy-start.5
  31.1 0.7 copy-done.5
  31.8 0.0 copy-start.7
  31.8 0.6 copy-done.7
  32.4 0.0 copy-start.9
  32.4 0.6 copy-done.9
  33.0 0.0 copy-start.11
  33.0 0.6 copy-done.11
  33.7 15.3 %all-to-all-done.arrived = bf16[128,9,8,128]{3,2,1,0:T(8,128)(2,1)S(1)} async-done(((bf16[128,9,8,128]{3,2,1,0:T(8,128)(2,1)}), bf16[128,9,8,128]{3,2,1,0:T(8,128)(2,1)S(1)}, u32[]{:S(2)}, u32[]{:S(2)}) %all-to-all-start) | async-done | bytes 2359328 | tf_op jit(solution)/shard_map/all_to_all | solution.py:703
  49.0 0.0 copy-start.6
  49.0 0.0 copy-start.8
  49.0 2.6 %coadd.1 = (bf16[1024,512]{1,0:T(8,128)(2,1)S(1)}, bf16[16,512]{1,0:T(8,128)(2,1)S(1)}) custom-call(bf16[128,9,8,128]{3,2,1,0:T(8,128)(2,1)S(1)} %all-to-all-done.arrived, f32[8,128]{1,0:T(8,128)S(1)} %get-tuple-element.19.ready), custom_call_target="tpu_custom_call" | custom-call | tf_op jit(solution)/shard_map/coadd/pallas_call | solution.py:290
  51.6 0.0 copy-start.3
  51.6 1.1 collective-permute-start
  53.4 0.2 collective-permute-done.near
  53.5 0.0 copy-done.6
  53.5 0.0 copy-done.8
  53.5 0.0 copy-done.10
  53.5 4.9 %stamp_sums.1 = f32[128,2,128]{2,1,0:T(2,128)} custom-call(bf16[1024,512]{1,0:T(8,128)(2,1)S(1)} %get-tuple-element.20.image, bf16[16,512]{1,0:T(8,128)(2,1)S(1)} %collective-permute-done.near, f32[1]{0:T(128)S(6)} %copy.21.sigma.sigma_in, s32[16]{0:T(128)S(1)} %copy-done.13, s32[16]{0:T(128)S(1)} %copy-done.14, bf16[128,384]{1,0:T(8,128)(2,1)S(1)} %copy-done.8, ...), custom_call_target="tpu_custom_call" | custom-call | tf_op jit(solution)/shard_map/stamp_sums/pallas_call | solution.py:375
  58.4 3.8 %all-to-all-start.1 = ((f32[128,2,128]{2,1,0:T(2,128)}), f32[128,2,128]{2,1,0:T(2,128)S(1)}, u32[]{:S(2)}, u32[]{:S(2)}) async-start(f32[128,2,128]{2,1,0:T(2,128)} %stamp_sums.1), calls=%async_computation.1 | async-start | bytes 262144 | tf_op jit(solution)/shard_map/all_to_all | solution.py:712
  62.2 0.0 copy-done.3
  62.2 7.3 %across.1.across_in = bf16[12,1056,512]{2,1,0:T(8,128)(2,1)} custom-call(bf16[1024,512]{1,0:T(8,128)(2,1)S(1)} %get-tuple-element.20.image, bf16[16,512]{1,0:T(8,128)(2,1)S(1)} %collective-permute-done.near, bf16[14,3,128,128]{3,2,1,0:T(8,128)(2,1)S(1)} %copy-done.3), custom_call_target="tpu_custom_call" | custom-call | flops 3321888768 | bytes 16000000 | tf_op jit(solution)/shard_map/across/pallas_call | solution.py:449
  69.5 2.8 %all-to-all-done.1.sums_in = f32[128,2,128]{2,1,0:T(2,128)S(1)} async-done(((f32[128,2,128]{2,1,0:T(2,128)}), f32[128,2,128]{2,1,0:T(2,128)S(1)}, u32[]{:S(2)}, u32[]{:S(2)}) %all-to-all-start.1) | async-done | bytes 131104 | tf_op jit(solution)/shard_map/all_to_all | solution.py:712
  72.3 8.8 %difference.1 = (f32[1,128]{1,0:T(1,128)S(1)}, bf16[128,8,512]{2,1,0:T(8,128)(2,1)}, bf16[256,8,512]{2,1,0:T(8,128)(2,1)}) custom-call(bf16[12,1056,512]{2,1,0:T(8,128)(2,1)} %across.1.across_in, f32[128,2,128]{2,1,0:T(2,128)S(1)} %all-to-all-done.1.sums_in, f32[1]{0:T(128)S(6)} %copy.21.sigma.sigma_in, s32[128]{0:T(128)S(1)} %get-tuple-element.26.slot_in, ...), custom_call_target="tpu_custom_call" | custom-call | tf_op jit(solution)/shard_map/difference/pallas_call | solution.py:560
  81.1 0.0 copy-start.4
  81.1 8.1 %all-to-all-start.2 = ((bf16[64,4,8,512]{3,2,1,0:T(8,128)(2,1)}), bf16[64,4,8,512]{3,2,1,0:T(8,128)(2,1)S(1)}, u32[]{:S(2)}, u32[]{:S(2)}) async-start(bf16[64,4,8,512]{3,2,1,0:T(8,128)(2,1)} %bitcast.19), calls=%async_computation.2 | async-start | bytes 4194304 | tf_op jit(solution)/shard_map/all_to_all | solution.py:717
  89.2 0.6 fusion
  91.1 0.0 copy-done.4
  91.1 0.0 copy-start.12
  91.1 6.1 %cut_stamps.1 = bf16[16,8,128]{2,1,0:T(8,128)(2,1)S(1)} custom-call(bf16[128,8,512]{2,1,0:T(8,128)(2,1)S(1)} %copy-done.4, s32[16]{0:T(128)S(1)} %copy-done.13, s32[16]{0:T(128)S(1)} %copy-done.14), custom_call_target="tpu_custom_call" | custom-call | flops 100000000 | bytes 3000000 | tf_op jit(solution)/shard_map/cut_stamps/pallas_call | solution.py:605
  97.2 0.6 copy.20
  97.9 0.5 slice_bitcast_fusion
  98.4 18.3 %all-to-all-done.2 = bf16[64,4,8,512]{3,2,1,0:T(8,128)(2,1)S(1)} async-done(((bf16[64,4,8,512]{3,2,1,0:T(8,128)(2,1)}), bf16[64,4,8,512]{3,2,1,0:T(8,128)(2,1)S(1)}, u32[]{:S(2)}, u32[]{:S(2)}) %all-to-all-start.2) | async-done | bytes 2097184 | tf_op jit(solution)/shard_map/all_to_all | solution.py:717
  116.7 3.1 %collective-permute-start.1 = (bf16[8,512]{1,0:T(8,128)(2,1)S(1)}, bf16[8,512]{1,0:T(8,128)(2,1)S(1)}, u32[]{:S(2)}, u32[]{:S(2)}) collective-permute-start(bf16[8,512]{1,0:T(8,128)(2,1)S(1)} %dynamic-slice_bitcast_fusion), channel_id=1, source_target_pairs={{0,1},{1,0},{2,3},{3,2},{4,5},{5,4},{6,7},{7,6},{8,9},{9,8},{10,11... | collective-permute-start | bytes 24584 | tf_op jit(solution)/shard_map/ppermute | solution.py:722
  119.8 2.1 %smooth.1.smoothed = bf16[1024,512]{1,0:T(8,128)(2,1)S(1)} custom-call(bf16[256,8,512]{2,1,0:T(8,128)(2,1)S(1)} %bitcast.16, s32[128]{0:T(128)S(1)} %get-tuple-element.31.pick, bf16[3,128,128]{2,1,0:T(8,128)(2,1)S(1)} %get-tuple-element.32.blocks.cblocks), custom_call_target="tpu_custom_call" | custom-call | flops 536870912 | bytes 3000000 | tf_op jit(solution)/shard_map/smooth/pallas_call | solution.py:635
  121.9 0.0 collective-permute-done.1.near
  121.9 0.0 copy-done.12
  121.9 1.8 %filter_rows.1 = f32[1024,512]{1,0:T(8,128)} custom-call(bf16[1024,512]{1,0:T(8,128)(2,1)S(1)} %smooth.1.smoothed, bf16[8,512]{1,0:T(8,128)(2,1)S(1)} %collective-permute-done.1.near, bf16[3,128,128]{2,1,0:T(8,128)(2,1)S(1)} %get-tuple-element.32.blocks.cblocks, bf16[2,128,128]{2,1,0:T(8,128)(2,1)S(1)} %copy-done.12), custom_call_target="tpu_custom_call" | custom-call | tf_op jit(solution)/shard_map/filter_rows/pallas_call | solution.py:676
  (7 shorter events, 0.0 us)
Async XLA Ops:
  4.1 11.6 %copy-start.16 = (bf16[12,21]{1,0:T(8,128)(2,1)S(1)}, bf16[12,21]{1,0:T(8,128)(2,1)}, u32[]{:S(2)}) copy-start(bf16[12,21]{1,0:T(8,128)(2,1)} %param.16) | copy-start | bytes 1516
  4.1 11.9 %copy-start.17 = (bf16[12,21]{1,0:T(8,128)(2,1)S(1)}, bf16[12,21]{1,0:T(8,128)(2,1)}, u32[]{:S(2)}) copy-start(bf16[12,21]{1,0:T(8,128)(2,1)} %param.15) | copy-start | bytes 1516
  4.1 11.9 %copy-start.18 = (bf16[15]{0:T(256)(128)(2,1)S(1)}, bf16[15]{0:T(256)(128)(2,1)}, u32[]{:S(2)}) copy-start(bf16[15]{0:T(256)(128)(2,1)} %param.22) | copy-start | bytes 94
  4.2 11.9 %copy-start.19 = (bf16[15]{0:T(256)(128)(2,1)S(1)}, bf16[15]{0:T(256)(128)(2,1)}, u32[]{:S(2)}) copy-start(bf16[15]{0:T(256)(128)(2,1)} %param.23) | copy-start | bytes 94
  4.2 12.0 %copy-start.13 = (s32[16]{0:T(128)S(1)}, s32[16]{0:T(128)}, u32[]{:S(2)}) copy-start(s32[16]{0:T(128)} %srow.5) | copy-start | bytes 196
  4.2 12.0 %copy-start.14 = (s32[16]{0:T(128)S(1)}, s32[16]{0:T(128)}, u32[]{:S(2)}) copy-start(s32[16]{0:T(128)} %scol.5) | copy-start | bytes 196
  4.2 12.0 %copy-start.15 = (s32[128]{0:T(128)S(1)}, s32[128]{0:T(128)}, u32[]{:S(2)}) copy-start(s32[128]{0:T(128)} %shift.1) | copy-start | bytes 1540
  4.2 44.8 %all-to-all-start = ((bf16[128,9,8,128]{3,2,1,0:T(8,128)(2,1)}), bf16[128,9,8,128]{3,2,1,0:T(8,128)(2,1)S(1)}, u32[]{:S(2)}, u32[]{:S(2)}) async-start(bf16[128,9,8,128]{3,2,1,0:T(8,128)(2,1)} %pack.1), calls=%async_computation | async-start | bytes 4718592 | tf_op jit(solution)/shard_map/all_to_all | solution.py:703
  16.2 1.6 %copy-start = (f32[1024,512]{1,0:T(8,128)S(1)}, f32[1024,512]{1,0:T(8,128)}, u32[]{:S(2)}) copy-start(f32[1024,512]{1,0:T(8,128)} %science_in.1) | copy-start | bytes 6291460
  28.9 1.1 copy-start.1
  30.0 1.1 copy-start.2
  31.1 0.7 copy-start.5
  31.8 0.6 copy-start.7
  32.4 0.6 copy-start.9
  33.0 0.6 copy-start.11
  49.0 4.6 %copy-start.6 = (f32[16,32,128]{2,1,0:T(8,128)S(1)}, f32[16,32,128]{2,1,0:T(8,128)}, u32[]{:S(2)}) copy-start(f32[16,32,128]{2,1,0:T(8,128)} %copy-done.5) | copy-start | bytes 786436
  49.0 4.6 %copy-start.8 = (bf16[128,384]{1,0:T(8,128)(2,1)S(1)}, bf16[128,384]{1,0:T(8,128)(2,1)}, u32[]{:S(2)}) copy-start(bf16[128,384]{1,0:T(8,128)(2,1)} %copy-done.7) | copy-start | bytes 294916
  49.0 4.6 %copy-start.10 = (bf16[3,128,64]{2,1,0:T(8,128)(2,1)S(1)}, bf16[3,128,64]{2,1,0:T(8,128)(2,1)}, u32[]{:S(2)}) copy-start(bf16[3,128,64]{2,1,0:T(8,128)(2,1)} %copy-done.9) | copy-start | bytes 147460
  51.6 10.6 %copy-start.3 = (bf16[14,3,128,128]{3,2,1,0:T(8,128)(2,1)S(1)}, bf16[14,3,128,128]{3,2,1,0:T(8,128)(2,1)}, u32[]{:S(2)}) copy-start(bf16[14,3,128,128]{3,2,1,0:T(8,128)(2,1)} %copy-done.2) | copy-start | bytes 4128772
  51.6 2.0 %collective-permute-start = (bf16[16,512]{1,0:T(8,128)(2,1)S(1)}, bf16[16,512]{1,0:T(8,128)(2,1)S(1)}, u32[]{:S(2)}, u32[]{:S(2)}) collective-permute-start(bf16[16,512]{1,0:T(8,128)(2,1)S(1)} %get-tuple-element.21), channel_id=1, source_target_pairs={{0,1},{1,0},{2,3},{3,2},{4,5},{5,4},{6,7},{7,6},{8,9},{9,8},{10,11... | collective-permute-start | bytes 49160 | tf_op jit(solution)/shard_map/ppermute | solution.py:708
  58.4 13.9 %all-to-all-start.1 = ((f32[128,2,128]{2,1,0:T(2,128)}), f32[128,2,128]{2,1,0:T(2,128)S(1)}, u32[]{:S(2)}, u32[]{:S(2)}) async-start(f32[128,2,128]{2,1,0:T(2,128)} %stamp_sums.1), calls=%async_computation.1 | async-start | bytes 262144 | tf_op jit(solution)/shard_map/all_to_all | solution.py:712
  81.1 10.0 %copy-start.4 = (bf16[128,8,512]{2,1,0:T(8,128)(2,1)S(1)}, bf16[128,8,512]{2,1,0:T(8,128)(2,1)}, u32[]{:S(2)}) copy-start(bf16[128,8,512]{2,1,0:T(8,128)(2,1)} %get-tuple-element.28.diff) | copy-start | bytes 3145732
  81.1 35.5 %all-to-all-start.2 = ((bf16[64,4,8,512]{3,2,1,0:T(8,128)(2,1)}), bf16[64,4,8,512]{3,2,1,0:T(8,128)(2,1)S(1)}, u32[]{:S(2)}, u32[]{:S(2)}) async-start(bf16[64,4,8,512]{3,2,1,0:T(8,128)(2,1)} %bitcast.19), calls=%async_computation.2 | async-start | bytes 4194304 | tf_op jit(solution)/shard_map/all_to_all | solution.py:717
  91.1 30.8 %copy-start.12 = (bf16[2,128,128]{2,1,0:T(8,128)(2,1)S(1)}, bf16[2,128,128]{2,1,0:T(8,128)(2,1)}, u32[]{:S(2)}) copy-start(bf16[2,128,128]{2,1,0:T(8,128)(2,1)} %copy-done.11) | copy-start | bytes 196612
  116.7 5.2 %collective-permute-start.1 = (bf16[8,512]{1,0:T(8,128)(2,1)S(1)}, bf16[8,512]{1,0:T(8,128)(2,1)S(1)}, u32[]{:S(2)}, u32[]{:S(2)}) collective-permute-start(bf16[8,512]{1,0:T(8,128)(2,1)S(1)} %dynamic-slice_bitcast_fusion), channel_id=1, source_target_pairs={{0,1},{1,0},{2,3},{3,2},{4,5},{5,4},{6,7},{7,6},{8,9},{9,8},{10,11... | collective-permute-start | bytes 24584 | tf_op jit(solution)/shard_map/ppermute | solution.py:722
